TPU v7x, 128 devices: a whole 4x4x4 slice. The times are simulated.
128 devices in a mesh: row: 16 (over x_lo, z, core), col: 8 (over x_hi, y).
Axes of the slice: x: 4 (x_hi: 2, x_lo: 2; x = x_hi * 2 + x_lo), y: 4, z: 4, core: 2. Of those that a mesh axis runs over, the one named last changes fastest.
Arguments:
- u_start: float32 [128, 262144], P('col', 'row'), may hold values from -24 to 24
- v_start: float32 [128, 131072], P('row', 'col'), may hold values from -24 to 24
- keep_u: float32 [128, 40], replicated, may hold values from -1 to 1, as said below
- keep_v: float32 [128, 40], replicated, may hold values from -1 to 1, as said below
- v_next: float32 [131072], P(('col', 'row')), may hold values from -96 to 96
- tile_blocks: bfloat16 [8192, 256, 256], P(('row', 'col')), may hold values from -0.375 to 0.375
- tile_rows: int32 [8192], P(('row', 'col')), may hold values from 0 to 63
- tile_cols: int32 [8192], P(('row', 'col')), may hold values from 0 to 63
- tile_count: int32 [128], P(('row', 'col')), may hold values from 32 to 64
Outputs:
- u_basis: float32 [42, 262144], P(None, ('row', 'col'))
- v_basis: float32 [43, 131072], P(None, ('col', 'row'))
- bidiagonal: float32 [2, 2], replicated
Inputs may be any that keep to these rules, and one draw needn't show every extreme that they name: `tile_rows`: tile row within the device's row group. `tile_cols`: tile column within the device's column group. `tile_count`: slots at this index and beyond hold no tile. `keep_u`: the columns are orthonormal. `keep_v`: the columns are orthonormal.
All inputs are finite; a program needn't handle non-finite values.
Results may differ from a plain program's by a relative error of at most 0.00155.
Values may be sent and summed in bfloat16 or wider, within the bound.
No kernel may reach another device: no remote copies, remote signals or barrier semaphores. Data moves between devices by JAX's collectives and lax.ppermute only.
A program may use at most 64 MiB of HBM per device.

v0:
```python
import functools

import jax
import jax.numpy as jnp
from jax import lax
from jax.sharding import Mesh
from jax.sharding import PartitionSpec as P

STEPS = 2
ROW_COL = ("row_0", "row_1", "row_2", "col_0", "col_1")
ROW = ("row_0", "row_1", "row_2")
COL = ("col_0", "col_1")
COL_ROW = ("col_0", "col_1", "row_0", "row_1", "row_2")


HIGH = lax.Precision.HIGHEST


def one_axis_at_a_time(x, axes):
    return functools.reduce(lax.psum, axes, x)


def in_blocks(x, dim, devices):
    lengths = x.shape
    tiles = x.reshape(*lengths[:dim], devices, lengths[dim] // devices, *lengths[dim + 1 :])
    return jnp.moveaxis(tiles, dim, 0)


def sum_at_owner(x, axis, dim):
    devices = lax.axis_size(axis)
    tiles = lax.all_to_all(in_blocks(x, dim, devices), axis, 0, 0, tiled=True)
    return jnp.sum(tiles, axis=0)


def laid_out(tiles, dim):
    lengths = list(tiles.shape[1:])
    lengths[dim] *= tiles.shape[0]
    return jnp.moveaxis(tiles, 0, dim).reshape(lengths)


def from_everyone(x, axis):
    devices = lax.axis_size(axis)
    return lax.all_to_all(jnp.broadcast_to(x[None], (devices, *x.shape)), axis, 0, 0, tiled=True)


def gathered_copies(x, axis, dim):
    return laid_out(from_everyone(x, axis), dim)


def orthonormal(basis_rows, vector, length, gram_matrix):
    first_coef = one_axis_at_a_time(jnp.dot(basis_rows, vector, precision=HIGH), ROW_COL) / length
    once_clean = vector - jnp.dot(first_coef, basis_rows, precision=HIGH)
    second_coef = (
        one_axis_at_a_time(jnp.dot(basis_rows, once_clean, precision=HIGH), ROW_COL) / length
    )
    twice_clean = once_clean - jnp.dot(second_coef, basis_rows, precision=HIGH)
    mean_square = one_axis_at_a_time(jnp.sum(twice_clean * twice_clean), ROW_COL) / length
    scale_now = jnp.sqrt(mean_square + 1e-06)
    return (twice_clean / scale_now, scale_now, gram_matrix)


def per_device(
    u_start, v_start, keep_u, keep_v, v_next, tile_blocks, tile_rows, tile_cols, tile_count
):
    row_total = lax.axis_size(ROW)
    col_total = lax.axis_size(COL)
    u_here = u_start.shape[0]
    u_part = lax.dynamic_slice_in_dim(keep_u, lax.axis_index(COL) * u_here, u_here, 0)
    u_kept = sum_at_owner(jnp.dot(u_part.T, u_start, precision=HIGH), COL, 1)
    v_here = v_start.shape[0]
    v_part = lax.dynamic_slice_in_dim(keep_v, lax.axis_index(ROW) * v_here, v_here, 0)
    v_kept = sum_at_owner(jnp.dot(v_part.T, v_start, precision=HIGH), ROW, 1)
    u_length = u_kept.shape[1] * row_total * col_total
    v_length = v_kept.shape[1] * row_total * col_total
    gram_left = None
    gram_right = None
    tile_size = tile_blocks.shape[1]
    slot_total = tile_blocks.shape[0]
    row_blocks = u_kept.shape[1] * col_total // tile_size
    col_blocks = v_kept.shape[1] * row_total // tile_size
    active = (jnp.arange(slot_total, dtype=jnp.int32) < tile_count[0]).astype(jnp.float32)
    row_hot = (tile_rows[None, :] == jnp.arange(row_blocks, dtype=jnp.int32)[:, None]).astype(
        jnp.float32
    ) * active[None, :]
    col_hot = (tile_cols[None, :] == jnp.arange(col_blocks, dtype=jnp.int32)[:, None]).astype(
        jnp.float32
    ) * active[None, :]
    first_right, beta_start, gram_right = orthonormal(v_kept, v_next, v_length, gram_right)
    left_rows = u_kept
    right_rows = jnp.concatenate([v_kept, first_right[None, :]], axis=0)
    current = first_right
    alpha_list = []
    beta_list = []
    for iteration in range(STEPS):
        forward_gathered = gathered_copies(current.astype(jnp.bfloat16), ROW, 0)
        forward_picked = forward_gathered.reshape(col_blocks, tile_size)[tile_cols]
        forward_products = jnp.einsum(
            "tij,tj->ti", tile_blocks, forward_picked, preferred_element_type=jnp.float32
        )
        forward_partial_value = jnp.dot(row_hot, forward_products, precision=HIGH).reshape(-1)
        image = sum_at_owner(forward_partial_value, COL, 0)
        left_new, alpha, gram_left = orthonormal(left_rows, image, u_length, gram_left)
        left_rows = jnp.concatenate([left_rows, left_new[None, :]], axis=0)
        gathered = gathered_copies(left_new.astype(jnp.bfloat16), COL, 0)
        picked = gathered.reshape(row_blocks, tile_size)[tile_rows]
        products = jnp.einsum("tij,ti->tj", tile_blocks, picked, preferred_element_type=jnp.float32)
        partial_value = jnp.dot(col_hot, products, precision=HIGH).reshape(-1)
        back_image = sum_at_owner(partial_value, ROW, 0)
        current, beta, gram_right = orthonormal(right_rows, back_image, v_length, gram_right)
        right_rows = jnp.concatenate([right_rows, current[None, :]], axis=0)
        alpha_list.append(alpha)
        beta_list.append(beta)
    bidiagonal = jnp.stack([jnp.stack(alpha_list), jnp.stack(beta_list)])
    return (left_rows, right_rows, bidiagonal)


def solution(mesh):
    finer = Mesh(mesh.devices.reshape(2, 4, 2, 2, 4), ("row_0", "row_1", "row_2", "col_0", "col_1"))
    return jax.shard_map(
        per_device,
        mesh=finer,
        in_specs=(
            P(COL, ROW),
            P(ROW, COL),
            P(),
            P(),
            P(COL_ROW),
            P(ROW_COL, None, None),
            P(ROW_COL),
            P(ROW_COL),
            P(ROW_COL),
        ),
        out_specs=(P(None, ROW_COL), P(None, COL_ROW), P()),
        check_vma=False,
    )
```

profile of v0, /device:TPU:1, one launch (start us, length us, event | category | flops | bytes accessed | tf_op | source)
XLA Modules:
  0.0 695.4 jit_solution(2143629357093605114)
XLA Ops:
  5.8 7.8 %all-to-all-start.1 = ((f32[16,40,1024]{2,1,0:T(8,128)}), f32[16,40,1024]{2,1,0:T(8,128)}, u32[]{:S(2)}, u32[]{:S(2)}) async-start(f32[16,40,1024]{2,1,0:T(8,128)} %bitcast.140), calls=%async_computation.1 | async-start | bytes 5242880 | tf_op jit(solution)/shard_map/all_to_all | solution.py:31
  13.6 33.7 %all-to-all-done.1 = f32[16,40,1024]{2,1,0:T(8,128)} async-done(((f32[16,40,1024]{2,1,0:T(8,128)}), f32[16,40,1024]{2,1,0:T(8,128)}, u32[]{:S(2)}, u32[]{:S(2)}) %all-to-all-start.1) | async-done | bytes 2621472 | tf_op jit(solution)/shard_map/all_to_all | solution.py:31
  53.2 12.7 %psum.526 = f32[40]{0:T(128)S(1)} all-reduce(f32[40]{0:T(128)S(1)} %psum.525), channel_id=1, replica_groups=mesh['row_0'=2,'row_1'=4,'row_2'=2,'col_0'=2,'col_1'=4] {'row_1'}, use_global_device_ids=true, to_apply=%region_3.0 | all-reduce | flops 40 | bytes 320 | tf_op jit(solution)/shard_map/psum | solution.py:20
  76.7 8.7 %psum.529 = f32[40]{0:T(128)S(1)} all-reduce(f32[40]{0:T(128)S(1)} %psum.528), channel_id=1, replica_groups=mesh['row_0'=2,'row_1'=4,'row_2'=2,'col_0'=2,'col_1'=4] {'col_1'}, use_global_device_ids=true, to_apply=%region_6.0 | all-reduce | flops 40 | bytes 320 | tf_op jit(solution)/shard_map/psum | solution.py:20
  95.6 8.5 %psum.532 = f32[40]{0:T(128)S(1)} all-reduce(f32[40]{0:T(128)S(1)} %psum.531), channel_id=1, replica_groups=mesh['row_0'=2,'row_1'=4,'row_2'=2,'col_0'=2,'col_1'=4] {'row_2'}, use_global_device_ids=true, to_apply=%region_9.0 | all-reduce | flops 40 | bytes 320 | tf_op jit(solution)/shard_map/psum | solution.py:20
  120.5 8.3 %psum.536 = f32[]{:T(128)} all-reduce(f32[]{:T(128)} %psum.535), channel_id=1, replica_groups=mesh['row_0'=2,'row_1'=4,'row_2'=2,'col_0'=2,'col_1'=4] {'row_1'}, use_global_device_ids=true, to_apply=%region_14.0 | all-reduce | flops 1 | bytes 8 | tf_op jit(solution)/shard_map/psum | solution.py:20
  128.9 9.1 %psum.537 = f32[]{:T(128)} all-reduce(f32[]{:T(128)} %psum.536), channel_id=1, replica_groups=mesh['row_0'=2,'row_1'=4,'row_2'=2,'col_0'=2,'col_1'=4] {'row_2'}, use_global_device_ids=true, to_apply=%region_15.0 | all-reduce | flops 1 | bytes 8 | tf_op jit(solution)/shard_map/psum | solution.py:20
  143.9 8.3 %psum.539 = f32[]{:T(128)} all-reduce(f32[]{:T(128)} %psum.538), channel_id=1, replica_groups=mesh['row_0'=2,'row_1'=4,'row_2'=2,'col_0'=2,'col_1'=4] {'col_1'}, use_global_device_ids=true, to_apply=%region_17.0 | all-reduce | flops 1 | bytes 8 | tf_op jit(solution)/shard_map/psum | solution.py:20
  155.0 6.8 all-to-all-start.2
  180.2 23.6 %all-to-all-done = f32[8,40,2048]{2,1,0:T(8,128)} async-done(((f32[8,40,2048]{2,1,0:T(8,128)}), f32[8,40,2048]{2,1,0:T(8,128)}, u32[]{:S(2)}, u32[]{:S(2)}) %all-to-all-start) | async-done | bytes 2621472 | tf_op jit(solution)/shard_map/all_to_all | solution.py:31
  219.9 6.9 psum.541
  226.8 7.2 %psum.542 = f32[40]{0:T(128)S(1)} all-reduce(f32[40]{0:T(128)S(1)} %psum.541), channel_id=1, replica_groups=mesh['row_0'=2,'row_1'=4,'row_2'=2,'col_0'=2,'col_1'=4] {'row_2'}, use_global_device_ids=true, to_apply=%region_21.0 | all-reduce | flops 40 | bytes 320 | tf_op jit(solution)/shard_map/psum | solution.py:20
  239.2 6.8 psum.544
  250.5 6.5 psum.546
  257.0 8.8 %psum.547 = f32[40]{0:T(128)S(1)} all-reduce(f32[40]{0:T(128)S(1)} %psum.546), channel_id=1, replica_groups=mesh['row_0'=2,'row_1'=4,'row_2'=2,'col_0'=2,'col_1'=4] {'row_2'}, use_global_device_ids=true, to_apply=%region_26.0 | all-reduce | flops 40 | bytes 320 | tf_op jit(solution)/shard_map/psum | solution.py:20
  271.1 6.5 psum.549
  282.9 7.5 %psum.551 = f32[]{:T(128)} all-reduce(f32[]{:T(128)} %psum.550), channel_id=1, replica_groups=mesh['row_0'=2,'row_1'=4,'row_2'=2,'col_0'=2,'col_1'=4] {'row_1'}, use_global_device_ids=true, to_apply=%region_31.0 | all-reduce | flops 1 | bytes 8 | tf_op jit(solution)/shard_map/psum | solution.py:20
  290.4 9.4 %psum.552 = f32[]{:T(128)} all-reduce(f32[]{:T(128)} %psum.551), channel_id=1, replica_groups=mesh['row_0'=2,'row_1'=4,'row_2'=2,'col_0'=2,'col_1'=4] {'row_2'}, use_global_device_ids=true, to_apply=%region_32.0 | all-reduce | flops 1 | bytes 8 | tf_op jit(solution)/shard_map/psum | solution.py:20
  305.7 7.7 %psum.554 = f32[]{:T(128)} all-reduce(f32[]{:T(128)} %psum.553), channel_id=1, replica_groups=mesh['row_0'=2,'row_1'=4,'row_2'=2,'col_0'=2,'col_1'=4] {'col_1'}, use_global_device_ids=true, to_apply=%region_34.0 | all-reduce | flops 1 | bytes 8 | tf_op jit(solution)/shard_map/psum | solution.py:20
  319.0 6.5 all-to-all-done.4
  331.3 13.4 %all_to_all.74 = f32[16,1,1024]{2,1,0:T(1,128)S(1)} all-to-all(f32[16,1,1024]{2,1,0:T(1,128)S(1)} %all_to_all.61), channel_id=1, replica_groups=mesh['row_0'=2,'row_1'=4,'row_2'=2,'col_0'=2,'col_1'=4] {'row_0','row_1'..., dimensions={0} | all-to-all | bytes 131072 | tf_op jit(solution)/shard_map/all_to_all | solution.py:31
  348.8 7.3 %psum.556 = f32[41]{0:T(128)S(1)} all-reduce(f32[41]{0:T(128)S(1)} %psum.555), channel_id=1, replica_groups=mesh['row_0'=2,'row_1'=4,'row_2'=2,'col_0'=2,'col_1'=4] {'row_1'}, use_global_device_ids=true, to_apply=%region_37.0 | all-reduce | flops 41 | bytes 328 | tf_op jit(solution)/shard_map/psum | solution.py:20
  366.7 6.8 psum.559
  384.3 8.8 %psum.562 = f32[41]{0:T(128)S(1)} all-reduce(f32[41]{0:T(128)S(1)} %psum.561), channel_id=1, replica_groups=mesh['row_0'=2,'row_1'=4,'row_2'=2,'col_0'=2,'col_1'=4] {'row_2'}, use_global_device_ids=true, to_apply=%region_43.0 | all-reduce | flops 41 | bytes 328 | tf_op jit(solution)/shard_map/psum | solution.py:20
  398.4 6.5 psum.564
  410.1 7.6 %psum.566 = f32[]{:T(128)} all-reduce(f32[]{:T(128)} %psum.565), channel_id=1, replica_groups=mesh['row_0'=2,'row_1'=4,'row_2'=2,'col_0'=2,'col_1'=4] {'row_1'}, use_global_device_ids=true, to_apply=%region_48.0 | all-reduce | flops 1 | bytes 8 | tf_op jit(solution)/shard_map/psum | solution.py:20
  417.7 9.4 %psum.567 = f32[]{:T(128)} all-reduce(f32[]{:T(128)} %psum.566), channel_id=1, replica_groups=mesh['row_0'=2,'row_1'=4,'row_2'=2,'col_0'=2,'col_1'=4] {'row_2'}, use_global_device_ids=true, to_apply=%region_49.0 | all-reduce | flops 1 | bytes 8 | tf_op jit(solution)/shard_map/psum | solution.py:20
  433.0 7.5 %psum.569 = f32[]{:T(128)} all-reduce(f32[]{:T(128)} %psum.568), channel_id=1, replica_groups=mesh['row_0'=2,'row_1'=4,'row_2'=2,'col_0'=2,'col_1'=4] {'col_1'}, use_global_device_ids=true, to_apply=%region_51.0 | all-reduce | flops 1 | bytes 8 | tf_op jit(solution)/shard_map/psum | solution.py:20
  442.1 11.8 %all_to_all.75 = bf16[16,2,512]{2,1,0:T(2,128)(2,1)S(1)} all-to-all(bf16[16,2,512]{2,1,0:T(2,128)(2,1)S(1)} %reshape.153), channel_id=1, replica_groups=mesh['row_0'=2,'row_1'=4,'row_2'=2,'col_0'=2,'col_1'=4] {'row_0','row_1'..., dimensions={0} | all-to-all | bytes 65536 | tf_op jit(solution)/shard_map/all_to_all | solution.py:43
  460.7 9.1 %all_to_all.76 = f32[8,1,2048]{2,1,0:T(1,128)S(1)} all-to-all(f32[8,1,2048]{2,1,0:T(1,128)S(1)} %all_to_all.62), channel_id=1, replica_groups=mesh['row_0'=2,'row_1'=4,'row_2'=2,'col_0'=2,'col_1'=4] {'col_0','col_1'}, dimensions={0} | all-to-all | bytes 131072 | tf_op jit(solution)/shard_map/all_to_all | solution.py:31
  474.1 6.9 psum.571
  481.0 7.1 %psum.572 = f32[41]{0:T(128)S(1)} all-reduce(f32[41]{0:T(128)S(1)} %psum.571), channel_id=1, replica_groups=mesh['row_0'=2,'row_1'=4,'row_2'=2,'col_0'=2,'col_1'=4] {'row_2'}, use_global_device_ids=true, to_apply=%region_55.0 | all-reduce | flops 41 | bytes 328 | tf_op jit(solution)/shard_map/psum | solution.py:20
  493.3 6.8 psum.574
  504.7 6.5 psum.576
  511.2 8.8 %psum.577 = f32[41]{0:T(128)S(1)} all-reduce(f32[41]{0:T(128)S(1)} %psum.576), channel_id=1, replica_groups=mesh['row_0'=2,'row_1'=4,'row_2'=2,'col_0'=2,'col_1'=4] {'row_2'}, use_global_device_ids=true, to_apply=%region_60.0 | all-reduce | flops 41 | bytes 328 | tf_op jit(solution)/shard_map/psum | solution.py:20
  525.2 6.5 psum.579
  537.1 7.5 %psum.581 = f32[]{:T(128)} all-reduce(f32[]{:T(128)} %psum.580), channel_id=1, replica_groups=mesh['row_0'=2,'row_1'=4,'row_2'=2,'col_0'=2,'col_1'=4] {'row_1'}, use_global_device_ids=true, to_apply=%region_65.0 | all-reduce | flops 1 | bytes 8 | tf_op jit(solution)/shard_map/psum | solution.py:20
  544.6 9.4 %psum.582 = f32[]{:T(128)} all-reduce(f32[]{:T(128)} %psum.581), channel_id=1, replica_groups=mesh['row_0'=2,'row_1'=4,'row_2'=2,'col_0'=2,'col_1'=4] {'row_2'}, use_global_device_ids=true, to_apply=%region_66.0 | all-reduce | flops 1 | bytes 8 | tf_op jit(solution)/shard_map/psum | solution.py:20
  559.9 7.5 %psum.584 = f32[]{:T(128)} all-reduce(f32[]{:T(128)} %psum.583), channel_id=1, replica_groups=mesh['row_0'=2,'row_1'=4,'row_2'=2,'col_0'=2,'col_1'=4] {'col_1'}, use_global_device_ids=true, to_apply=%region_68.0 | all-reduce | flops 1 | bytes 8 | tf_op jit(solution)/shard_map/psum | solution.py:20
  569.0 9.0 %all_to_all.77 = bf16[8,2,1024]{2,1,0:T(2,128)(2,1)S(1)} all-to-all(bf16[8,2,1024]{2,1,0:T(2,128)(2,1)S(1)} %reshape.155), channel_id=1, replica_groups=mesh['row_0'=2,'row_1'=4,'row_2'=2,'col_0'=2,'col_1'=4] {'col_0','col_1'}, dimensions={0} | all-to-all | bytes 65536 | tf_op jit(solution)/shard_map/all_to_all | solution.py:43
  583.8 13.0 %all_to_all.78 = f32[16,1,1024]{2,1,0:T(1,128)S(1)} all-to-all(f32[16,1,1024]{2,1,0:T(1,128)S(1)} %all_to_all.63), channel_id=1, replica_groups=mesh['row_0'=2,'row_1'=4,'row_2'=2,'col_0'=2,'col_1'=4] {'row_0','row_1'..., dimensions={0} | all-to-all | bytes 131072 | tf_op jit(solution)/shard_map/all_to_all | solution.py:31
  600.9 7.0 %psum.586 = f32[42]{0:T(128)S(1)} all-reduce(f32[42]{0:T(128)S(1)} %psum.585), channel_id=1, replica_groups=mesh['row_0'=2,'row_1'=4,'row_2'=2,'col_0'=2,'col_1'=4] {'row_1'}, use_global_device_ids=true, to_apply=%region_71.0 | all-reduce | flops 42 | bytes 336 | tf_op jit(solution)/shard_map/psum | solution.py:20
  618.8 6.8 psum.589
  636.4 8.8 %psum.592 = f32[42]{0:T(128)S(1)} all-reduce(f32[42]{0:T(128)S(1)} %psum.591), channel_id=1, replica_groups=mesh['row_0'=2,'row_1'=4,'row_2'=2,'col_0'=2,'col_1'=4] {'row_2'}, use_global_device_ids=true, to_apply=%region_77.0 | all-reduce | flops 42 | bytes 336 | tf_op jit(solution)/shard_map/psum | solution.py:20
  650.4 6.5 psum.594
  662.2 7.6 %psum.596 = f32[]{:T(128)} all-reduce(f32[]{:T(128)} %psum.595), channel_id=1, replica_groups=mesh['row_0'=2,'row_1'=4,'row_2'=2,'col_0'=2,'col_1'=4] {'row_1'}, use_global_device_ids=true, to_apply=%region_82.0 | all-reduce | flops 1 | bytes 8 | tf_op jit(solution)/shard_map/psum | solution.py:20
  669.8 9.4 %psum.597 = f32[]{:T(128)} all-reduce(f32[]{:T(128)} %psum.596), channel_id=1, replica_groups=mesh['row_0'=2,'row_1'=4,'row_2'=2,'col_0'=2,'col_1'=4] {'row_2'}, use_global_device_ids=true, to_apply=%region_83.0 | all-reduce | flops 1 | bytes 8 | tf_op jit(solution)/shard_map/psum | solution.py:20
  685.9 7.5 %psum.599 = f32[]{:T(128)} all-reduce(f32[]{:T(128)} %psum.598), channel_id=1, replica_groups=mesh['row_0'=2,'row_1'=4,'row_2'=2,'col_0'=2,'col_1'=4] {'col_1'}, use_global_device_ids=true, to_apply=%region_85.0 | all-reduce | flops 1 | bytes 8 | tf_op jit(solution)/shard_map/psum | solution.py:20
  (147 shorter events, 258.0 us)
Async XLA Ops:
  0.6 161.1 %copy-start = (f32[16,16384]{1,0:T(8,128)S(1)}, f32[16,16384]{1,0:T(8,128)}, u32[]{:S(2)}) copy-start(f32[16,16384]{1,0:T(8,128)} %param.9) | copy-start | bytes 3145732
  0.6 48.5 %copy-start.2 = (f32[1024]{0:T(1024)S(1)}, f32[1024]{0:T(1024)}, u32[]{:S(2)}) copy-start(f32[1024]{0:T(1024)} %param.13) | copy-start | bytes 12292
  0.7 161.1 %copy-start.1 = (f32[128,40]{0,1:T(8,128)S(1)}, f32[128,40]{0,1:T(8,128)}, u32[]{:S(2)}) copy-start(f32[128,40]{0,1:T(8,128)} %param.11) | copy-start | bytes 61444
  5.8 41.5 %all-to-all-start.1 = ((f32[16,40,1024]{2,1,0:T(8,128)}), f32[16,40,1024]{2,1,0:T(8,128)}, u32[]{:S(2)}, u32[]{:S(2)}) async-start(f32[16,40,1024]{2,1,0:T(8,128)} %bitcast.140), calls=%async_computation.1 | async-start | bytes 5242880 | tf_op jit(solution)/shard_map/all_to_all | solution.py:31
  13.5 159.1 %copy-start.4 = (s32[64]{0:T(128)S(1)}, s32[64]{0:T(128)}, u32[]{:S(2)}) copy-start(s32[64]{0:T(128)} %param.16) | copy-start | bytes 772
  155.0 12.7 %all-to-all-start.2 = ((bf16[16,2,512]{2,1,0:T(2,128)(2,1)}), bf16[16,2,512]{2,1,0:T(2,128)(2,1)S(1)}, u32[]{:S(2)}, u32[]{:S(2)}) async-start(bf16[16,2,512]{2,1,0:T(2,128)(2,1)} %reshape.149), calls=%async_computation.2 | async-start | bytes 65536 | tf_op jit(solution)/shard_map/all_to_all | solution.py:43
  165.8 13.5 %copy-start.3 = (s32[64]{0:T(128)S(1)}, s32[64]{0:T(128)}, u32[]{:S(2)}) copy-start(s32[64]{0:T(128)} %param.15) | copy-start | bytes 772
  167.6 36.2 %all-to-all-start = ((f32[8,40,2048]{2,1,0:T(8,128)}), f32[8,40,2048]{2,1,0:T(8,128)}, u32[]{:S(2)}, u32[]{:S(2)}) async-start(f32[8,40,2048]{2,1,0:T(8,128)} %bitcast.139), calls=%async_computation | async-start | bytes 5242880 | tf_op jit(solution)/shard_map/all_to_all | solution.py:31
  203.8 11.8 %all-to-all-start.3 = ((f32[8,1,2048]{2,1,0:T(1,128)}), f32[8,1,2048]{2,1,0:T(1,128)S(1)}, u32[]{:S(2)}, u32[]{:S(2)}) async-start(f32[8,1,2048]{2,1,0:T(1,128)} %all_to_all.60), calls=%async_computation.3 | async-start | bytes 131072 | tf_op jit(solution)/shard_map/all_to_all | solution.py:31
  315.6 9.9 %all-to-all-start.4 = ((bf16[8,2,1024]{2,1,0:T(2,128)(2,1)}), bf16[8,2,1024]{2,1,0:T(2,128)(2,1)S(1)}, u32[]{:S(2)}, u32[]{:S(2)}) async-start(bf16[8,2,1024]{2,1,0:T(2,128)(2,1)} %reshape.151), calls=%async_computation.4 | async-start | bytes 65536 | tf_op jit(solution)/shard_map/all_to_all | solution.py:43
where the time goes:
time: 700 us; the launch traced here: 695 us
  blocking collectives  538 us (77%)
  waiting for transfers between devices  70.5 us (10%)
  matrix products  32.1 us (5%)
  starting transfers between devices  27.4 us (4%)
  other arithmetic  13.3 us (2%)
  local copies, waits for them, and re-layouts  9.33 us (1%)
    psum x75, blocking collectives, one_axis_at_a_time(): return functools.reduce(lax.psum, axes, x)  481 us
    all_to_all x3, waiting for transfers between devices, sum_at_owner(): tiles = lax.all_to_all(in_blocks(x, dim, devices), axis, 0, 0, tiled=True)  62.1 us
    all_to_all x3, blocking collectives, sum_at_owner(): tiles = lax.all_to_all(in_blocks(x, dim, devices), axis, 0, 0, tiled=True)  35.4 us
    all_to_all x2, blocking collectives, from_everyone(): lax.all_to_all(jnp.broadcast_to(x[None], (devices, *x.shape)), axis, 0, 0...  20.8 us
    all_to_all x3, starting transfers between devices, sum_at_owner(): tiles = lax.all_to_all(in_blocks(x, dim, devices), axis, 0, 0, tiled=True)  17.3 us
  transfers between devices with their start and end apart: 5, of which 5 were waited for; matrix products, arithmetic and copies ran while one was open for 2% of the time, Pallas kernels for 0%

commit v1 on v0

v1 whole, which is shorter than its diff:
```python
import jax
import jax.numpy as jnp
from jax import lax
from jax.sharding import Mesh
from jax.sharding import PartitionSpec as P

STEPS = 2
ROW = ("row_0", "row_1", "row_2")
COL = ("col_0", "col_1")
ROW_COL = ROW + COL
COL_ROW = COL + ROW

HIGH = lax.Precision.HIGHEST


def swapped(blocks, axis):
    return lax.all_to_all(blocks, axis, 0, 0, tiled=True)


def in_blocks(x, devices):
    rows, length = x.shape
    return jnp.moveaxis(x.reshape(rows, devices, length // devices), 1, 0)


def from_everyone(x, axis):
    return swapped(jnp.broadcast_to(x[None], (lax.axis_size(axis), *x.shape)), axis)


def summed_everywhere(x):
    return jnp.sum(from_everyone(x, ROW_COL), axis=0)


def kept(start, keep, axis):
    here = swapped(in_blocks(start, lax.axis_size(axis)), axis)
    return jnp.dot(keep.T, here.reshape(-1, here.shape[-1]), precision=HIGH)


def orthonormal(basis, vector, gram, dots, square):
    coef = 2.0 * dots - jnp.dot(gram, dots, precision=HIGH)
    clean = vector - jnp.dot(coef, basis, precision=HIGH)
    across = dots - jnp.dot(gram, coef, precision=HIGH)
    mean_square = square - jnp.dot(coef, dots, precision=HIGH) - jnp.dot(coef, across, precision=HIGH)
    scale = jnp.sqrt(jnp.maximum(mean_square, 0.0) + 1e-06)
    new = clean / scale
    across = across / scale
    own = mean_square / (scale * scale)
    grown = jnp.concatenate(
        [
            jnp.concatenate([gram, across[:, None]], axis=1),
            jnp.concatenate([across, own[None]])[None, :],
        ],
        axis=0,
    )
    return new, scale, grown


def per_device(
    u_start, v_start, keep_u, keep_v, v_next, tile_blocks, tile_rows, tile_cols, tile_count
):
    total = lax.axis_size(ROW_COL)
    v_kept = kept(v_start, keep_v, ROW)
    u_kept = kept(u_start, keep_u, COL)
    u_length = u_kept.shape[1] * total
    v_length = v_kept.shape[1] * total
    slots, size = tile_blocks.shape[:2]
    row_blocks = u_kept.shape[1] * lax.axis_size(COL) // size
    col_blocks = v_kept.shape[1] * lax.axis_size(ROW) // size
    active = jnp.arange(slots, dtype=jnp.int32) < tile_count[0]
    row_hot = (
        (tile_rows[None, :] == jnp.arange(row_blocks, dtype=jnp.int32)[:, None]) & active[None, :]
    ).astype(jnp.float32)
    col_hot = (
        (tile_cols[None, :] == jnp.arange(col_blocks, dtype=jnp.int32)[:, None]) & active[None, :]
    ).astype(jnp.float32)

    keep_count = v_kept.shape[0]
    stacked = jnp.concatenate([v_kept, v_next[None, :]], axis=0)
    first = summed_everywhere(
        jnp.dot(stacked, stacked.T, precision=HIGH).reshape(-1)
    ).reshape(keep_count + 1, keep_count + 1) / v_length
    current, _, gram_v = orthonormal(
        v_kept, v_next, first[:keep_count, :keep_count], first[keep_count, :keep_count], first[keep_count, keep_count]
    )
    right = jnp.concatenate([v_kept, current[None, :]], axis=0)
    left = u_kept
    gram_u = None
    alphas = []
    betas = []
    for step in range(STEPS):
        wide = from_everyone(current.astype(jnp.bfloat16), ROW).reshape(col_blocks, size)
        products = jnp.einsum(
            "tij,tj->ti", tile_blocks, wide[tile_cols], preferred_element_type=jnp.float32
        )
        partial = jnp.dot(row_hot, products, precision=HIGH)
        image = jnp.sum(swapped(partial.reshape(lax.axis_size(COL), -1), COL), axis=0)
        if gram_u is None:
            stacked = jnp.concatenate([left, image[None, :]], axis=0)
            first = summed_everywhere(
                jnp.dot(stacked, stacked.T, precision=HIGH).reshape(-1)
            ).reshape(keep_count + 1, keep_count + 1) / u_length
            gram_u, dots, square = first[:keep_count, :keep_count], first[keep_count, :keep_count], first[keep_count, keep_count]
        else:
            stacked = jnp.concatenate([left, image[None, :]], axis=0)
            first = summed_everywhere(jnp.dot(stacked, image, precision=HIGH)) / u_length
            dots, square = first[:-1], first[-1]
        new, alpha, gram_u = orthonormal(left, image, gram_u, dots, square)
        left = jnp.concatenate([left, new[None, :]], axis=0)
        wide = from_everyone(new.astype(jnp.bfloat16), COL).reshape(row_blocks, size)
        products = jnp.einsum(
            "tij,ti->tj", tile_blocks, wide[tile_rows], preferred_element_type=jnp.float32
        )
        partial = jnp.dot(col_hot, products, precision=HIGH)
        image = jnp.sum(swapped(partial.reshape(lax.axis_size(ROW), -1), ROW), axis=0)
        stacked = jnp.concatenate([right, image[None, :]], axis=0)
        first = summed_everywhere(jnp.dot(stacked, image, precision=HIGH)) / v_length
        current, beta, gram_v = orthonormal(right, image, gram_v, first[:-1], first[-1])
        right = jnp.concatenate([right, current[None, :]], axis=0)
        alphas.append(alpha)
        betas.append(beta)
    return left, right, jnp.stack([jnp.stack(alphas), jnp.stack(betas)])


def solution(mesh):
    finer = Mesh(mesh.devices.reshape(2, 4, 2, 2, 4), ROW_COL)
    return jax.shard_map(
        per_device,
        mesh=finer,
        in_specs=(
            P(COL, ROW),
            P(ROW, COL),
            P(),
            P(),
            P(COL_ROW),
            P(ROW_COL, None, None),
            P(ROW_COL),
            P(ROW_COL),
            P(ROW_COL),
        ),
        out_specs=(P(None, ROW_COL), P(None, COL_ROW), P()),
        check_vma=False,
    )
```

time: 700 us -> 272 us (0.39)
  blocking collectives: 538 us -> 41.3 us
  starting transfers between devices: 27.4 us -> 60.1 us
  waiting for transfers between devices: 70.5 us -> 94.3 us
  local copies, waits for them, and re-layouts: 9.33 us -> 20.2 us
    psum x75 -> x0, blocking collectives: 481 us -> none  [one_axis_at_a_time(): return functools.reduce(lax.psum, axes, x)]
    all_to_all x5 -> x13, starting transfers between devices: 27.4 us -> 60.1 us  [swapped(): return lax.all_to_all(blocks, axis, 0, 0, tiled=True)]
    all_to_all x5 -> x13, waiting for transfers between devices: 70.5 us -> 94.3 us  [swapped(): return lax.all_to_all(blocks, axis, 0, 0, tiled=True)]
    all_to_all x5 -> x2, blocking collectives: 56.2 us -> 41.3 us  [swapped(): return lax.all_to_all(blocks, axis, 0, 0, tiled=True)]
  transfers between devices with their start and end apart: 5 -> 13, of which waited for: 5 -> 13; matrix products, arithmetic and copies ran while one was open for 2% -> 5% of each run, Pallas kernels for 0% -> 0%
where the time goes in v1:
time: 272 us; the launch traced here: 270 us
  waiting for transfers between devices  94.3 us (35%)
  starting transfers between devices  60.1 us (22%)
  blocking collectives  41.3 us (15%)
  matrix products  32.9 us (12%)
  local copies, waits for them, and re-layouts  20.2 us (7%)
  between operations  11.7 us (4%)
  other arithmetic  9.7 us (4%)
    all_to_all x13, waiting for transfers between devices, swapped(): return lax.all_to_all(blocks, axis, 0, 0, tiled=True)  94.3 us
    all_to_all x13, starting transfers between devices, swapped(): return lax.all_to_all(blocks, axis, 0, 0, tiled=True)  60.1 us
    all_to_all x2, blocking collectives, swapped(): return lax.all_to_all(blocks, axis, 0, 0, tiled=True)  41.3 us
    dot_general x2, matrix products, per_device(): jnp.einsum('tij,tj->ti', tile_blocks, wide[tile_cols], preferred_element_...  11.3 us
    dot_general x2, matrix products, per_device(): jnp.einsum('tij,ti->tj', tile_blocks, wide[tile_rows], preferred_element_...  9.15 us
  transfers between devices with their start and end apart: 13, of which 13 were waited for; matrix products, arithmetic and copies ran while one was open for 5% of the time, Pallas kernels for 0%

profile of v1, /device:TPU:1, one launch (start us, length us, event | category | flops | bytes accessed | tf_op | source)
XLA Modules:
  0.0 270.1 jit_solution(7920764123609703309)
XLA Ops:
  0.6 17.6 %all_to_all.104 = f32[16,8,1024]{2,1,0:T(8,128)S(1)} all-to-all(f32[16,8,1024]{2,1,0:T(8,128)} %bitcast.217), channel_id=1, replica_groups=mesh['row_0'=2,'row_1'=4,'row_2'=2,'col_0'=2,'col_1'=4] {'row_0','row_1'..., dimensions={0} | all-to-all | bytes 1048576 | tf_op jit(solution)/shard_map/all_to_all | solution.py:17
  18.2 1.1 fusion.14
  19.3 1.1 fusion.22
  21.0 23.8 %all_to_all.105 = f32[128,1,1681]{2,1,0:T(1,128)S(1)} all-to-all(f32[128,1,1681]{2,1,0:T(1,128)S(1)} %broadcast_in_dim.129), channel_id=1, replica_groups=mesh['row_0'=2,'row_1'=4,'row_2'=2,'col_0'=2,'col_1'=4] {'row_0','row_1'..., dimensions={0} | all-to-all | bytes 1721344 | tf_op jit(solution)/shard_map/all_to_all | solution.py:17
  50.4 0.8 reduce.33
  51.9 5.3 %all-to-all-start.3 = ((bf16[16,2,512]{2,1,0:T(2,128)(2,1)}), bf16[16,2,512]{2,1,0:T(2,128)(2,1)S(1)}, u32[]{:S(2)}, u32[]{:S(2)}) async-start(bf16[16,2,512]{2,1,0:T(2,128)(2,1)} %reshape.242), calls=%async_computation.3 | async-start | bytes 65536 | tf_op jit(solution)/shard_map/all_to_all | solution.py:17
  58.5 1.8 copy.105
  60.3 1.6 copy.59
  61.9 1.1 all-to-all-done.3
  63.0 3.8 %all-to-all-start = ((f32[8,16,2048]{2,1,0:T(8,128)}), f32[8,16,2048]{2,1,0:T(8,128)S(1)}, u32[]{:S(2)}, u32[]{:S(2)}) async-start(f32[8,16,2048]{2,1,0:T(8,128)} %copy.59), calls=%async_computation | async-start | bytes 2097152 | tf_op jit(solution)/shard_map/all_to_all | solution.py:17
  67.7 5.6 %fusion.51 = f32[64,1,256]{2,1,0:T(1,128)S(1)} fusion(bf16[64,256,256]{2,1,0:T(8,128)(2,1)} %param.14, bf16[64,256,1]{1,0,2:T(8,128)(2,1)S(1)} %bitcast.219), kind=kOutput, calls=%fused_computation.77 | convolution fusion | flops 8388608 | bytes 8486912 | tf_op jit(solution)/shard_map/tij,tj->ti/dot_general | solution.py:91
  74.3 7.0 %all-to-all-done = f32[8,16,2048]{2,1,0:T(8,128)S(1)} async-done(((f32[8,16,2048]{2,1,0:T(8,128)}), f32[8,16,2048]{2,1,0:T(8,128)S(1)}, u32[]{:S(2)}, u32[]{:S(2)}) %all-to-all-start) | async-done | bytes 1048608 | tf_op jit(solution)/shard_map/all_to_all | solution.py:17
  81.3 5.6 %all-to-all-start.4 = ((f32[8,1,2048]{2,1,0:T(1,128)}), f32[8,1,2048]{2,1,0:T(1,128)S(1)}, u32[]{:S(2)}, u32[]{:S(2)}) async-start(f32[8,1,2048]{2,1,0:T(1,128)} %all_to_all.85), calls=%async_computation.4 | async-start | bytes 131072 | tf_op jit(solution)/shard_map/all_to_all | solution.py:17
  87.6 6.0 %all-to-all-done.4 = f32[8,1,2048]{2,1,0:T(1,128)S(1)} async-done(((f32[8,1,2048]{2,1,0:T(1,128)}), f32[8,1,2048]{2,1,0:T(1,128)S(1)}, u32[]{:S(2)}, u32[]{:S(2)}) %all-to-all-start.4) | async-done | bytes 65568 | tf_op jit(solution)/shard_map/all_to_all | solution.py:17
  94.2 1.4 broadcast_in_dim.134
  95.6 6.1 %all-to-all-start.5 = ((f32[128,1,1681]{2,1,0:T(1,128)}), f32[128,1,1681]{2,1,0:T(1,128)S(1)}, u32[]{:S(2)}, u32[]{:S(2)}) async-start(f32[128,1,1681]{2,1,0:T(1,128)} %broadcast_in_dim.134), calls=%async_computation.5 | async-start | bytes 1835008 | tf_op jit(solution)/shard_map/all_to_all | solution.py:17
  101.7 16.1 %all-to-all-done.5 = f32[128,1,1681]{2,1,0:T(1,128)S(1)} async-done(((f32[128,1,1681]{2,1,0:T(1,128)}), f32[128,1,1681]{2,1,0:T(1,128)S(1)}, u32[]{:S(2)}, u32[]{:S(2)}) %all-to-all-start.5) | async-done | bytes 860704 | tf_op jit(solution)/shard_map/all_to_all | solution.py:17
  119.3 0.8 multiply_reduce_fusion.4
  122.5 0.8 reduce.34
  124.0 4.9 %all-to-all-start.6 = ((bf16[8,2,1024]{2,1,0:T(2,128)(2,1)}), bf16[8,2,1024]{2,1,0:T(2,128)(2,1)S(1)}, u32[]{:S(2)}, u32[]{:S(2)}) async-start(bf16[8,2,1024]{2,1,0:T(2,128)(2,1)} %reshape.244), calls=%async_computation.6 | async-start | bytes 65536 | tf_op jit(solution)/shard_map/all_to_all | solution.py:17
  129.0 6.5 %all-to-all-done.6 = bf16[8,2,1024]{2,1,0:T(2,128)(2,1)S(1)} async-done(((bf16[8,2,1024]{2,1,0:T(2,128)(2,1)}), bf16[8,2,1024]{2,1,0:T(2,128)(2,1)S(1)}, u32[]{:S(2)}, u32[]{:S(2)}) %all-to-all-start.6) | async-done | bytes 32800 | tf_op jit(solution)/shard_map/all_to_all | solution.py:17
  136.4 4.6 %fusion.48 = f32[64,1,256]{2,1,0:T(1,128)S(1)} fusion(bf16[64,256,256]{2,1,0:T(8,128)(2,1)} %param.14, bf16[64,256,1]{1,0,2:T(8,128)(2,1)S(1)} %bitcast.216), kind=kOutput, calls=%fused_computation.74 | convolution fusion | flops 8388608 | bytes 8486912 | tf_op jit(solution)/shard_map/tij,ti->tj/dot_general | solution.py:109
  141.9 5.2 %all-to-all-start.7 = ((f32[16,1,1024]{2,1,0:T(1,128)}), f32[16,1,1024]{2,1,0:T(1,128)S(1)}, u32[]{:S(2)}, u32[]{:S(2)}) async-start(f32[16,1,1024]{2,1,0:T(1,128)} %all_to_all.86), calls=%async_computation.7 | async-start | bytes 131072 | tf_op jit(solution)/shard_map/all_to_all | solution.py:17
  147.2 5.8 %all-to-all-done.7 = f32[16,1,1024]{2,1,0:T(1,128)S(1)} async-done(((f32[16,1,1024]{2,1,0:T(1,128)}), f32[16,1,1024]{2,1,0:T(1,128)S(1)}, u32[]{:S(2)}, u32[]{:S(2)}) %all-to-all-start.7) | async-done | bytes 65568 | tf_op jit(solution)/shard_map/all_to_all | solution.py:17
  153.9 3.8 %all-to-all-start.8 = ((f32[128,1,42]{2,1,0:T(1,128)}), f32[128,1,42]{2,1,0:T(1,128)S(1)}, u32[]{:S(2)}, u32[]{:S(2)}) async-start(f32[128,1,42]{2,1,0:T(1,128)} %broadcast_in_dim.140), calls=%async_computation.8 | async-start | bytes 131072 | tf_op jit(solution)/shard_map/all_to_all | solution.py:17
  157.8 9.4 %all-to-all-done.8 = f32[128,1,42]{2,1,0:T(1,128)S(1)} async-done(((f32[128,1,42]{2,1,0:T(1,128)}), f32[128,1,42]{2,1,0:T(1,128)S(1)}, u32[]{:S(2)}, u32[]{:S(2)}) %all-to-all-start.8) | async-done | bytes 21536 | tf_op jit(solution)/shard_map/all_to_all | solution.py:17
  168.1 0.9 multiply_reduce_fusion.2
  171.2 0.8 reduce.35
  172.6 4.3 %all-to-all-start.9 = ((bf16[16,2,512]{2,1,0:T(2,128)(2,1)}), bf16[16,2,512]{2,1,0:T(2,128)(2,1)S(1)}, u32[]{:S(2)}, u32[]{:S(2)}) async-start(bf16[16,2,512]{2,1,0:T(2,128)(2,1)} %reshape.246), calls=%async_computation.9 | async-start | bytes 65536 | tf_op jit(solution)/shard_map/all_to_all | solution.py:17
  177.1 5.7 %all-to-all-done.9 = bf16[16,2,512]{2,1,0:T(2,128)(2,1)S(1)} async-done(((bf16[16,2,512]{2,1,0:T(2,128)(2,1)}), bf16[16,2,512]{2,1,0:T(2,128)(2,1)S(1)}, u32[]{:S(2)}, u32[]{:S(2)}) %all-to-all-start.9) | async-done | bytes 32800 | tf_op jit(solution)/shard_map/all_to_all | solution.py:17
  183.8 5.6 %fusion.45 = f32[64,1,256]{2,1,0:T(1,128)S(1)} fusion(bf16[64,256,256]{2,1,0:T(8,128)(2,1)} %param.14, bf16[64,256,1]{1,0,2:T(8,128)(2,1)S(1)} %bitcast.218), kind=kOutput, calls=%fused_computation.71 | convolution fusion | flops 8388608 | bytes 8486912 | tf_op jit(solution)/shard_map/tij,tj->ti/dot_general | solution.py:91
  190.3 3.4 %all-to-all-start.10 = ((f32[8,1,2048]{2,1,0:T(1,128)}), f32[8,1,2048]{2,1,0:T(1,128)S(1)}, u32[]{:S(2)}, u32[]{:S(2)}) async-start(f32[8,1,2048]{2,1,0:T(1,128)} %all_to_all.87), calls=%async_computation.10 | async-start | bytes 131072 | tf_op jit(solution)/shard_map/all_to_all | solution.py:17
  193.7 6.6 %all-to-all-done.10 = f32[8,1,2048]{2,1,0:T(1,128)S(1)} async-done(((f32[8,1,2048]{2,1,0:T(1,128)}), f32[8,1,2048]{2,1,0:T(1,128)S(1)}, u32[]{:S(2)}, u32[]{:S(2)}) %all-to-all-start.10) | async-done | bytes 65568 | tf_op jit(solution)/shard_map/all_to_all | solution.py:17
  201.5 5.1 %all-to-all-start.11 = ((f32[128,1,42]{2,1,0:T(1,128)}), f32[128,1,42]{2,1,0:T(1,128)S(1)}, u32[]{:S(2)}, u32[]{:S(2)}) async-start(f32[128,1,42]{2,1,0:T(1,128)} %broadcast_in_dim.146), calls=%async_computation.11 | async-start | bytes 131072 | tf_op jit(solution)/shard_map/all_to_all | solution.py:17
  206.6 9.4 %all-to-all-done.11 = f32[128,1,42]{2,1,0:T(1,128)S(1)} async-done(((f32[128,1,42]{2,1,0:T(1,128)}), f32[128,1,42]{2,1,0:T(1,128)S(1)}, u32[]{:S(2)}, u32[]{:S(2)}) %all-to-all-start.11) | async-done | bytes 21536 | tf_op jit(solution)/shard_map/all_to_all | solution.py:17
  216.1 0.8 multiply_reduce_fusion.1
  217.2 0.9 fusion.13
  220.7 0.8 reduce.36
  222.2 3.3 %all-to-all-start.12 = ((bf16[8,2,1024]{2,1,0:T(2,128)(2,1)}), bf16[8,2,1024]{2,1,0:T(2,128)(2,1)S(1)}, u32[]{:S(2)}, u32[]{:S(2)}) async-start(bf16[8,2,1024]{2,1,0:T(2,128)(2,1)} %reshape.248), calls=%async_computation.12 | async-start | bytes 65536 | tf_op jit(solution)/shard_map/all_to_all | solution.py:17
  225.7 6.4 %all-to-all-done.12 = bf16[8,2,1024]{2,1,0:T(2,128)(2,1)S(1)} async-done(((bf16[8,2,1024]{2,1,0:T(2,128)(2,1)}), bf16[8,2,1024]{2,1,0:T(2,128)(2,1)S(1)}, u32[]{:S(2)}, u32[]{:S(2)}) %all-to-all-start.12) | async-done | bytes 32800 | tf_op jit(solution)/shard_map/all_to_all | solution.py:17
  233.1 4.6 %fusion.42 = f32[64,1,256]{2,1,0:T(1,128)S(1)} fusion(bf16[64,256,256]{2,1,0:T(8,128)(2,1)} %param.14, bf16[64,256,1]{1,0,2:T(8,128)(2,1)S(1)} %bitcast.215), kind=kOutput, calls=%fused_computation.68 | convolution fusion | flops 8388608 | bytes 8486912 | tf_op jit(solution)/shard_map/tij,ti->tj/dot_general | solution.py:109
  238.5 5.5 %all-to-all-start.13 = ((f32[16,1,1024]{2,1,0:T(1,128)}), f32[16,1,1024]{2,1,0:T(1,128)S(1)}, u32[]{:S(2)}, u32[]{:S(2)}) async-start(f32[16,1,1024]{2,1,0:T(1,128)} %all_to_all.88), calls=%async_computation.13 | async-start | bytes 131072 | tf_op jit(solution)/shard_map/all_to_all | solution.py:17
  244.1 5.8 %all-to-all-done.13 = f32[16,1,1024]{2,1,0:T(1,128)S(1)} async-done(((f32[16,1,1024]{2,1,0:T(1,128)}), f32[16,1,1024]{2,1,0:T(1,128)S(1)}, u32[]{:S(2)}, u32[]{:S(2)}) %all-to-all-start.13) | async-done | bytes 65568 | tf_op jit(solution)/shard_map/all_to_all | solution.py:17
  250.9 3.8 %all-to-all-start.14 = ((f32[128,1,43]{2,1,0:T(1,128)}), f32[128,1,43]{2,1,0:T(1,128)S(1)}, u32[]{:S(2)}, u32[]{:S(2)}) async-start(f32[128,1,43]{2,1,0:T(1,128)} %broadcast_in_dim.154), calls=%async_computation.14 | async-start | bytes 131072 | tf_op jit(solution)/shard_map/all_to_all | solution.py:17
  254.7 0.8 pad_maximum_fusion.4
  255.5 8.6 %all-to-all-done.14 = f32[128,1,43]{2,1,0:T(1,128)S(1)} async-done(((f32[128,1,43]{2,1,0:T(1,128)}), f32[128,1,43]{2,1,0:T(1,128)S(1)}, u32[]{:S(2)}, u32[]{:S(2)}) %all-to-all-start.14) | async-done | bytes 22048 | tf_op jit(solution)/shard_map/all_to_all | solution.py:17
  264.8 0.8 multiply_reduce_fusion
  265.7 0.9 fusion.12
  (107 shorter events, 26.1 us)
Async XLA Ops:
  0.6 86.2 %copy-start = (f32[128,40]{0,1:T(8,128)S(1)}, f32[128,40]{0,1:T(8,128)}, u32[]{:S(2)}) copy-start(f32[128,40]{0,1:T(8,128)} %param.11) | copy-start | bytes 61444
  44.8 28.6 %copy-start.1 = (s32[64]{0:T(128)S(1)}, s32[64]{0:T(128)}, u32[]{:S(2)}) copy-start(s32[64]{0:T(128)} %param.15) | copy-start | bytes 772
  51.9 11.1 %all-to-all-start.3 = ((bf16[16,2,512]{2,1,0:T(2,128)(2,1)}), bf16[16,2,512]{2,1,0:T(2,128)(2,1)S(1)}, u32[]{:S(2)}, u32[]{:S(2)}) async-start(bf16[16,2,512]{2,1,0:T(2,128)(2,1)} %reshape.242), calls=%async_computation.3 | async-start | bytes 65536 | tf_op jit(solution)/shard_map/all_to_all | solution.py:17
  63.0 18.3 %all-to-all-start = ((f32[8,16,2048]{2,1,0:T(8,128)}), f32[8,16,2048]{2,1,0:T(8,128)S(1)}, u32[]{:S(2)}, u32[]{:S(2)}) async-start(f32[8,16,2048]{2,1,0:T(8,128)} %copy.59), calls=%async_computation | async-start | bytes 2097152 | tf_op jit(solution)/shard_map/all_to_all | solution.py:17
  81.3 12.3 %all-to-all-start.4 = ((f32[8,1,2048]{2,1,0:T(1,128)}), f32[8,1,2048]{2,1,0:T(1,128)S(1)}, u32[]{:S(2)}, u32[]{:S(2)}) async-start(f32[8,1,2048]{2,1,0:T(1,128)} %all_to_all.85), calls=%async_computation.4 | async-start | bytes 131072 | tf_op jit(solution)/shard_map/all_to_all | solution.py:17
  95.6 22.2 %all-to-all-start.5 = ((f32[128,1,1681]{2,1,0:T(1,128)}), f32[128,1,1681]{2,1,0:T(1,128)S(1)}, u32[]{:S(2)}, u32[]{:S(2)}) async-start(f32[128,1,1681]{2,1,0:T(1,128)} %broadcast_in_dim.134), calls=%async_computation.5 | async-start | bytes 1835008 | tf_op jit(solution)/shard_map/all_to_all | solution.py:17
  124.0 11.5 %all-to-all-start.6 = ((bf16[8,2,1024]{2,1,0:T(2,128)(2,1)}), bf16[8,2,1024]{2,1,0:T(2,128)(2,1)S(1)}, u32[]{:S(2)}, u32[]{:S(2)}) async-start(bf16[8,2,1024]{2,1,0:T(2,128)(2,1)} %reshape.244), calls=%async_computation.6 | async-start | bytes 65536 | tf_op jit(solution)/shard_map/all_to_all | solution.py:17
  129.0 12.0 %copy-start.2 = (s32[64]{0:T(128)S(1)}, s32[64]{0:T(128)}, u32[]{:S(2)}) copy-start(s32[64]{0:T(128)} %param.16) | copy-start | bytes 772
  141.9 11.1 %all-to-all-start.7 = ((f32[16,1,1024]{2,1,0:T(1,128)}), f32[16,1,1024]{2,1,0:T(1,128)S(1)}, u32[]{:S(2)}, u32[]{:S(2)}) async-start(f32[16,1,1024]{2,1,0:T(1,128)} %all_to_all.86), calls=%async_computation.7 | async-start | bytes 131072 | tf_op jit(solution)/shard_map/all_to_all | solution.py:17
  153.9 13.2 %all-to-all-start.8 = ((f32[128,1,42]{2,1,0:T(1,128)}), f32[128,1,42]{2,1,0:T(1,128)S(1)}, u32[]{:S(2)}, u32[]{:S(2)}) async-start(f32[128,1,42]{2,1,0:T(1,128)} %broadcast_in_dim.140), calls=%async_computation.8 | async-start | bytes 131072 | tf_op jit(solution)/shard_map/all_to_all | solution.py:17
  172.6 10.2 %all-to-all-start.9 = ((bf16[16,2,512]{2,1,0:T(2,128)(2,1)}), bf16[16,2,512]{2,1,0:T(2,128)(2,1)S(1)}, u32[]{:S(2)}, u32[]{:S(2)}) async-start(bf16[16,2,512]{2,1,0:T(2,128)(2,1)} %reshape.246), calls=%async_computation.9 | async-start | bytes 65536 | tf_op jit(solution)/shard_map/all_to_all | solution.py:17
  190.3 10.0 %all-to-all-start.10 = ((f32[8,1,2048]{2,1,0:T(1,128)}), f32[8,1,2048]{2,1,0:T(1,128)S(1)}, u32[]{:S(2)}, u32[]{:S(2)}) async-start(f32[8,1,2048]{2,1,0:T(1,128)} %all_to_all.87), calls=%async_computation.10 | async-start | bytes 131072 | tf_op jit(solution)/shard_map/all_to_all | solution.py:17
  201.5 14.5 %all-to-all-start.11 = ((f32[128,1,42]{2,1,0:T(1,128)}), f32[128,1,42]{2,1,0:T(1,128)S(1)}, u32[]{:S(2)}, u32[]{:S(2)}) async-start(f32[128,1,42]{2,1,0:T(1,128)} %broadcast_in_dim.146), calls=%async_computation.11 | async-start | bytes 131072 | tf_op jit(solution)/shard_map/all_to_all | solution.py:17
  222.2 9.9 %all-to-all-start.12 = ((bf16[8,2,1024]{2,1,0:T(2,128)(2,1)}), bf16[8,2,1024]{2,1,0:T(2,128)(2,1)S(1)}, u32[]{:S(2)}, u32[]{:S(2)}) async-start(bf16[8,2,1024]{2,1,0:T(2,128)(2,1)} %reshape.248), calls=%async_computation.12 | async-start | bytes 65536 | tf_op jit(solution)/shard_map/all_to_all | solution.py:17
  238.5 11.4 %all-to-all-start.13 = ((f32[16,1,1024]{2,1,0:T(1,128)}), f32[16,1,1024]{2,1,0:T(1,128)S(1)}, u32[]{:S(2)}, u32[]{:S(2)}) async-start(f32[16,1,1024]{2,1,0:T(1,128)} %all_to_all.88), calls=%async_computation.13 | async-start | bytes 131072 | tf_op jit(solution)/shard_map/all_to_all | solution.py:17
  250.9 13.2 %all-to-all-start.14 = ((f32[128,1,43]{2,1,0:T(1,128)}), f32[128,1,43]{2,1,0:T(1,128)S(1)}, u32[]{:S(2)}, u32[]{:S(2)}) async-start(f32[128,1,43]{2,1,0:T(1,128)} %broadcast_in_dim.154), calls=%async_computation.14 | async-start | bytes 131072 | tf_op jit(solution)/shard_map/all_to_all | solution.py:17

commit v2 on v1

v2 whole, which is shorter than its diff:
```python
import functools

import jax
import jax.numpy as jnp
from jax import lax
from jax.experimental import pallas as pl
from jax.experimental.pallas import tpu as pltpu
from jax.sharding import Mesh
from jax.sharding import PartitionSpec as P

ROW = ("row_0", "row_1", "row_2")
COL = ("col_0", "col_1")
ROW_COL = ROW + COL
COL_ROW = COL + ROW

HIGH = lax.Precision.HIGHEST
F32 = jnp.float32
BF16 = jnp.bfloat16
LANES = 128
PAD = 48
EPS = 1e-06
VMEM_LIMIT = 30 << 20


def swapped(blocks, axis):
    return lax.all_to_all(blocks, axis, 0, 0, tiled=True)


def iota(shape, dim):
    return lax.broadcasted_iota(jnp.int32, shape, dim)


def as_row(col):
    spot = iota((PAD, LANES), 0) == iota((PAD, LANES), 1)
    return jnp.sum(jnp.where(spot, col, 0.0), axis=0, keepdims=True)


def as_col(row):
    spot = iota((PAD, LANES), 0) == iota((PAD, LANES), 1)
    return jnp.sum(jnp.where(spot, row, 0.0), axis=1, keepdims=True)


def total(x):
    return jnp.sum(jnp.sum(x, axis=1, keepdims=True), axis=0, keepdims=True)


def packed(gram, n):
    width = n // 2 + 1
    twice = gram + pltpu.roll(gram, n, 1)
    turned, sub = twice, iota((PAD, LANES), 0)
    for bit in (1, 2, 4, 8, 16, 32):
        turned = jnp.where(sub & bit != 0, pltpu.roll(turned, LANES - bit, 1), turned)
    turned = jnp.where(iota((PAD, LANES), 1) < width, turned, 0.0)
    out = turned[0:8]
    for g in range(1, PAD // 8):
        out = out + pltpu.roll(turned[8 * g : 8 * g + 8], width * g, 1)
    return out


def unpacked(pack, n):
    width = n // 2 + 1
    groups = [pack] + [
        pltpu.roll(pack, LANES - width * g, 1) for g in range(1, PAD // 8)
    ]
    turned = jnp.concatenate(groups, axis=0)
    turned = jnp.where(iota((PAD, LANES), 1) < width, turned, 0.0)
    wide = pltpu.roll(turned, 0, 1, stride=1, stride_axis=0)
    half = wide + pltpu.roll(wide, LANES - n, 1)
    lane, sub = iota((PAD, LANES), 1), iota((PAD, LANES), 0)
    half = jnp.where((lane < n) & (sub < n), half, 0.0)
    square = jnp.concatenate([half, jnp.zeros((LANES - PAD, LANES), F32)], axis=0)
    return half + jnp.where(lane == sub, 0.0, square.T[:PAD])


def solve(gram, dots_col, square, m):
    coef_col = 2.0 * dots_col - jnp.sum(gram * as_row(dots_col), axis=1, keepdims=True)
    across = dots_col - jnp.sum(gram * as_row(coef_col), axis=1, keepdims=True)
    mean_square = square - total(coef_col * (dots_col + across))
    mean_square = jnp.maximum(mean_square, 0.0)
    scale = jnp.sqrt(mean_square + EPS)
    inverse = 1.0 / scale
    across = across * inverse
    lane, sub = iota((PAD, LANES), 1), iota((PAD, LANES), 0)
    grown = jnp.where(sub == m, as_row(across), gram)
    grown = jnp.where(lane == m, across, grown)
    grown = jnp.where((lane == m) & (sub == m), mean_square * inverse * inverse, grown)
    return coef_col, scale, inverse, grown


def at(value, index):
    return jnp.where(iota((PAD, 1), 0) == index, value, 0.0)


def padded(col):
    return jnp.concatenate([col, jnp.zeros((PAD - col.shape[0], 1), F32)], axis=0)


def regroup_kernel(start_ref, out_ref):
    out_ref[...] = start_ref[...][None]


def kept_kernel(start_ref, keep_ref, out_ref, gram_ref):
    basis = lax.dot_general(
        keep_ref[...], start_ref[...], (((0,), (0,)), ((), ())), precision=HIGH, preferred_element_type=F32
    )
    out_ref[...] = basis
    rows = basis.shape[0]
    wide = jnp.concatenate([basis, jnp.zeros((PAD - rows, basis.shape[1]), F32)], axis=0)
    full = jnp.concatenate([wide, jnp.zeros((LANES - PAD, basis.shape[1]), F32)], axis=0)
    gram = lax.dot_general(
        wide, full, (((1,), (1,)), ((), ())), precision=HIGH, preferred_element_type=F32
    )
    gram_ref[...] = packed(gram, rows + 1)


def kept_with_kernel(start_ref, keep_ref, next_ref, out_ref, message_ref, wide_ref):
    basis = lax.dot_general(
        keep_ref[...], start_ref[...], (((0,), (0,)), ((), ())), precision=HIGH, preferred_element_type=F32
    )
    out_ref[...] = basis
    rows = basis.shape[0]
    wide_ref[...] = jnp.zeros_like(wide_ref)
    wide_ref[:rows] = basis
    for j in range(next_ref.shape[0]):
        wide_ref[rows : rows + 1, j * LANES : (j + 1) * LANES] = next_ref[j : j + 1]
    full = wide_ref[...]
    gram = lax.dot_general(
        full[:PAD], full, (((1,), (1,)), ((), ())), precision=HIGH, preferred_element_type=F32
    )
    message_ref[...] = jnp.broadcast_to(packed(gram, rows + 1)[None], message_ref.shape)


def projected_slice(vector_ref, basis_ref, coef_col):
    count = basis_ref.shape[0]
    rows = []
    for j in range(vector_ref.shape[0]):
        part = basis_ref[:, j * LANES : (j + 1) * LANES] * coef_col[:count]
        rows.append(jnp.sum(part, axis=0, keepdims=True))
    return vector_ref[...] - jnp.concatenate(rows, axis=0)


def first_kernel(length, got_ref, basis_ref, next_ref, vector_ref, gram_ref, message_ref):
    count = basis_ref.shape[0]
    gram = unpacked(jnp.sum(got_ref[...], axis=0), count + 1) * (1.0 / length)
    lane, sub = iota((PAD, LANES), 1), iota((PAD, LANES), 0)
    dots = jnp.sum(jnp.where((lane == count) & (sub < count), gram, 0.0), axis=1, keepdims=True)
    square = total(jnp.where((lane == count) & (sub == count), gram, 0.0))
    gram = jnp.where((lane < count) & (sub < count), gram, 0.0)
    coef, scale, inverse, grown = solve(gram, dots, square, count)
    new = projected_slice(next_ref, basis_ref, coef) * inverse
    vector_ref[...] = new
    gram_ref[...] = grown
    message_ref[...] = jnp.broadcast_to(new[None], message_ref.shape)


def multiplied(forward, entries, tiles_ref, pick_ref, place_ref, count_ref, picked_ref, product_ref):
    slots, size = tiles_ref.shape[:2]
    blocks = size // LANES
    rows = entries.shape[0]
    values = entries.astype(BF16)
    lane = iota((slots, rows), 1)
    for b in range(blocks):
        hot = (lane == blocks * pick_ref[...] + b).astype(BF16)
        picked_ref[:, b * LANES : (b + 1) * LANES] = jnp.dot(hot, values, preferred_element_type=F32)
    for t in range(slots):
        product_ref[t : t + 1] = lax.dot_general(
            picked_ref[t : t + 1].astype(BF16),
            tiles_ref[t],
            (((1,), (1 if forward else 0,)), ((), ())),
            preferred_element_type=F32,
        )
    sub, slot = iota((rows, slots), 0), iota((rows, slots), 1)
    out = None
    for b in range(blocks):
        hot = ((sub == blocks * place_ref[...] + b) & (slot < count_ref[0])).astype(F32)
        part = jnp.dot(
            hot, product_ref[:, b * LANES : (b + 1) * LANES], precision=HIGH, preferred_element_type=F32
        )
        out = part if out is None else out + part
    return out


def forward_kernel(
    extra, got_ref, tiles_ref, pick_ref, place_ref, count_ref, *refs
):
    if extra:
        gram_ref, message_ref, picked_ref, product_ref = refs
    else:
        message_ref, picked_ref, product_ref = refs
    entries = got_ref[...].reshape(-1, LANES)
    sums = multiplied(True, entries, tiles_ref, pick_ref, place_ref, count_ref, picked_ref, product_ref)
    rows = sums.shape[0]
    for k in range(message_ref.shape[0]):
        message_ref[k, :rows] = sums
        if extra:
            message_ref[k, rows:] = gram_ref[...]


def left_dots_kernel(length, got_ref, wide_ref, *refs):
    refs = list(refs)
    first = got_ref.shape[1] > LANES
    others = [] if first else [refs.pop(0)]
    image_ref, message_ref = refs
    image = jnp.sum(got_ref[:, :LANES], axis=0)
    image_ref[...] = image
    parts, count, width = wide_ref.shape
    across = width // LANES
    acc = jnp.zeros((count, LANES), F32)
    for k in range(parts):
        for j in range(across):
            r = k * across + j
            acc = acc + wide_ref[k, :, j * LANES : (j + 1) * LANES] * image_ref[r : r + 1]
    dots = padded(jnp.sum(acc, axis=1, keepdims=True))
    for n, other in enumerate(others):
        dots = dots + at(total(other[...] * image), count + n)
    dots = dots + at(total(image * image), PAD - 1)
    row = as_row(dots) * (1.0 / length)
    if first:
        gram = jnp.sum(got_ref[:, LANES:], axis=0) * (1.0 / length)
        message_ref[:, :8] = jnp.broadcast_to(gram[None], (message_ref.shape[0], 8, LANES))
        message_ref[:, 8:] = jnp.broadcast_to(row[None], (message_ref.shape[0], 8, LANES))
    else:
        message_ref[...] = jnp.broadcast_to(row, message_ref.shape)


def split_dots(row):
    col = as_col(row)
    last = iota((PAD, 1), 0) == PAD - 1
    return jnp.where(last, 0.0, col), total(jnp.where(last, col, 0.0))


def left_kernel(
    m, got_ref, image_ref, wide_ref, tiles_ref, pick_ref, place_ref, count_ref, own_ref, *refs
):
    refs = list(refs)
    first = len(got_ref.shape) == 3
    gram_in = None if first else refs.pop(0)
    others = [] if first else [refs.pop(0)]
    new_ref, own_out_ref, gram_ref, scale_ref, message_ref, picked_ref, product_ref = refs
    parts, count, width = wide_ref.shape
    if first:
        got = jnp.sum(got_ref[...], axis=0)
        gram = unpacked(got[:8], count + 1)
        row = got[8:9]
    else:
        gram = gram_in[...]
        row = jnp.sum(got_ref[...], axis=0, keepdims=True)
    dots, square = split_dots(row)
    coef, scale, inverse, grown = solve(gram, dots, square, m)
    gram_ref[...] = grown
    scale_ref[...] = jnp.broadcast_to(scale, scale_ref.shape)
    across = width // LANES
    by_lane = jnp.broadcast_to(coef[:count], (count, LANES))
    for k in range(parts):
        for j in range(across):
            r = k * across + j
            part = wide_ref[k, :, j * LANES : (j + 1) * LANES] * by_lane
            new_ref[r : r + 1] = image_ref[r : r + 1] - jnp.sum(part, axis=0, keepdims=True)
    new = new_ref[...]
    for n, other in enumerate(others):
        new = new - coef[count + n : count + n + 1] * other[...]
    new = new * inverse
    new_ref[...] = new
    own_out_ref[...] = new_ref[pl.ds(pl.multiple_of(own_ref[0] * across, across), across)]
    sums = multiplied(False, new, tiles_ref, pick_ref, place_ref, count_ref, picked_ref, product_ref)
    message_ref[...] = sums.reshape(message_ref.shape)


def right_dots_kernel(length, got_ref, basis_ref, *refs):
    refs = list(refs)
    image_ref, message_ref = refs[-2:]
    others = refs[:-2]
    image = jnp.sum(got_ref[...], axis=0)
    image_ref[...] = image
    count = basis_ref.shape[0]
    acc = jnp.zeros((count, LANES), F32)
    for j in range(image.shape[0]):
        acc = acc + basis_ref[:, j * LANES : (j + 1) * LANES] * image_ref[j : j + 1]
    dots = padded(jnp.sum(acc, axis=1, keepdims=True))
    for n, other in enumerate(others):
        dots = dots + at(total(other[...] * image), count + n)
    dots = dots + at(total(image * image), PAD - 1)
    message_ref[...] = jnp.broadcast_to(as_row(dots) * (1.0 / length), message_ref.shape)


def new_right(m, got_ref, image_ref, basis_ref, gram_ref, others):
    count = basis_ref.shape[0]
    dots, square = split_dots(jnp.sum(got_ref[...], axis=0, keepdims=True))
    coef, scale, inverse, grown = solve(gram_ref[...], dots, square, m)
    new = projected_slice(image_ref, basis_ref, coef)
    for n, other in enumerate(others):
        new = new - coef[count + n : count + n + 1] * other[...]
    return new * inverse, scale, grown


def right_kernel(m, got_ref, image_ref, basis_ref, gram_in_ref, *refs):
    refs = list(refs)
    vector_ref, gram_ref, scale_ref, message_ref = refs[-4:]
    new, scale, grown = new_right(m, got_ref, image_ref, basis_ref, gram_in_ref, refs[:-4])
    vector_ref[...] = new
    gram_ref[...] = grown
    scale_ref[...] = jnp.broadcast_to(scale, scale_ref.shape)
    message_ref[...] = jnp.broadcast_to(new[None], message_ref.shape)


def put_rows(out_ref, row, vector):
    for j in range(vector.shape[0]):
        out_ref[row : row + 1, j * LANES : (j + 1) * LANES] = vector[j : j + 1]


def last_kernel(
    m, got_ref, image_ref, basis_ref, gram_ref, old_0_ref, old_1_ref,
    alpha_0_ref, alpha_1_ref, beta_0_ref, out_ref, scales_ref,
):
    new, scale, _ = new_right(m, got_ref, image_ref, basis_ref, gram_ref, [old_0_ref, old_1_ref])
    count = basis_ref.shape[0]
    out_ref[:count] = basis_ref[...]
    put_rows(out_ref, count, old_0_ref[...])
    put_rows(out_ref, count + 1, old_1_ref[...])
    put_rows(out_ref, count + 2, new)
    lane = iota((1, LANES), 1)
    alphas = jnp.where(lane == 0, alpha_0_ref[...], alpha_1_ref[...])
    betas = jnp.where(lane == 0, beta_0_ref[...], jnp.broadcast_to(scale, (1, LANES)))
    scales_ref[...] = jnp.concatenate([alphas, betas], axis=0)[:, :2]


def left_out_kernel(basis_ref, new_0_ref, new_1_ref, out_ref):
    count = basis_ref.shape[0]
    out_ref[:count] = basis_ref[...]
    put_rows(out_ref, count, new_0_ref[...])
    put_rows(out_ref, count + 1, new_1_ref[...])


WHOLE = pl.BlockSpec(memory_space=pltpu.VMEM)
SCALAR = pl.BlockSpec(memory_space=pltpu.SMEM)


def call(kernel, name, outs, args, scalars=(), scratch=()):
    shapes = tuple(jax.ShapeDtypeStruct(s, F32) for s in outs)
    result = pl.pallas_call(
        kernel,
        name=name,
        out_shape=shapes,
        in_specs=[SCALAR if i in scalars else WHOLE for i in range(len(args))],
        out_specs=tuple(WHOLE for _ in shapes),
        scratch_shapes=list(scratch),
        compiler_params=pltpu.CompilerParams(vmem_limit_bytes=VMEM_LIMIT),
    )(*args)
    return result


def per_device(
    u_start, v_start, keep_u, keep_v, v_next, tile_blocks, tile_rows, tile_cols, tile_count
):
    rows_n, cols_n = lax.axis_size(ROW), lax.axis_size(COL)
    devices = rows_n * cols_n
    keep = keep_u.shape[1]
    slots, size = tile_blocks.shape[:2]
    u_here, u_range = u_start.shape
    v_here, v_range = v_start.shape
    u_own, v_own = u_range // cols_n, v_range // rows_n
    u_length, v_length = u_range * rows_n, v_range * cols_n
    u_rows, v_rows = u_own // LANES, v_own // LANES
    full = u_range // LANES
    row_lane, row_sub = tile_rows.reshape(1, slots), tile_rows.reshape(slots, 1)
    col_lane, col_sub = tile_cols.reshape(1, slots), tile_cols.reshape(slots, 1)
    own = lax.axis_index(COL).reshape(1)
    products = [pltpu.VMEM((slots, size), F32), pltpu.VMEM((slots, size), F32)]

    u_blocks = pl.pallas_call(
        regroup_kernel,
        name="regroup",
        grid=(cols_n,),
        in_specs=[pl.BlockSpec((u_here, u_own), lambda k: (0, k))],
        out_specs=pl.BlockSpec((1, u_here, u_own), lambda k: (k, 0, 0)),
        out_shape=jax.ShapeDtypeStruct((cols_n, u_here, u_own), F32),
    )(u_start)
    u_got = swapped(u_blocks, COL).reshape(-1, u_own)
    u_kept, u_gram = call(kept_kernel, "left_kept", [(keep, u_own), (8, LANES)], [u_got, keep_u])
    u_wide = lax.all_gather(u_kept, COL, axis=0)

    v_blocks = jnp.moveaxis(v_start.reshape(v_here, rows_n, v_own), 1, 0)
    v_got = swapped(v_blocks, ROW).reshape(-1, v_own)
    next_rows = v_next.reshape(v_rows, LANES)
    v_kept, message = call(
        kept_with_kernel,
        "right_kept",
        [(keep, v_own), (devices, 8, LANES)],
        [v_got, keep_v, next_rows],
        scratch=[pltpu.VMEM((LANES, v_own), F32)],
    )
    got = swapped(message, ROW_COL)
    v_0, gram_v, message = call(
        functools.partial(first_kernel, v_length),
        "first_right",
        [(v_rows, LANES), (PAD, LANES), (rows_n, v_rows, LANES)],
        [got, v_kept, next_rows],
    )

    def forward(message, extra):
        got = swapped(message, ROW)
        (message,) = call(
            functools.partial(forward_kernel, bool(extra)),
            "forward",
            [(cols_n, full + 8 * len(extra), LANES)],
            [got, tile_blocks, col_sub, row_lane, tile_count, *extra],
            scalars=(4,),
            scratch=products,
        )
        return swapped(message, COL)

    def left(got, m, gram, others):
        first = gram is None
        image, message = call(
            functools.partial(left_dots_kernel, u_length),
            "left_dots",
            [(full, LANES), (rows_n, 16, LANES) if first else (rows_n, LANES)],
            [got, u_wide, *others],
        )
        got = swapped(message, ROW)
        known = [] if first else [gram]
        new, own_new, gram, scale, message = call(
            functools.partial(left_kernel, m),
            "left",
            [(full, LANES), (u_rows, LANES), (PAD, LANES), (1, LANES), (rows_n, v_rows, LANES)],
            [got, image, u_wide, tile_blocks, row_sub, col_lane, tile_count, own, *known, *others],
            scalars=(6, 7),
            scratch=products,
        )
        return new, own_new, gram, scale, swapped(message, ROW)

    def right_dots(got, others):
        image, message = call(
            functools.partial(right_dots_kernel, v_length),
            "right_dots",
            [(v_rows, LANES), (devices, LANES)],
            [got, v_kept, *others],
        )
        return image, swapped(message, ROW_COL)

    got = forward(message, [u_gram])
    u_0_wide, u_0, gram_u, alpha_0, got = left(got, keep, None, [])
    image, got = right_dots(got, [v_0])
    v_1, gram_v, beta_0, message = call(
        functools.partial(right_kernel, keep + 1),
        "right",
        [(v_rows, LANES), (PAD, LANES), (1, LANES), (rows_n, v_rows, LANES)],
        [got, image, v_kept, gram_v, v_0],
    )
    got = forward(message, [])
    _, u_1, gram_u, alpha_1, got = left(got, keep + 1, gram_u, [u_0_wide])
    (u_basis,) = call(left_out_kernel, "left_out", [(keep + 2, u_own)], [u_kept, u_0, u_1])
    image, got = right_dots(got, [v_0, v_1])
    v_basis, scales = call(
        functools.partial(last_kernel, keep + 2),
        "last_right",
        [(keep + 3, v_own), (2, 2)],
        [got, image, v_kept, gram_v, v_0, v_1, alpha_0, alpha_1, beta_0],
    )
    return u_basis, v_basis, scales


def solution(mesh):
    finer = Mesh(mesh.devices.reshape(2, 4, 2, 2, 4), ROW_COL)
    return jax.shard_map(
        per_device,
        mesh=finer,
        in_specs=(
            P(COL, ROW),
            P(ROW, COL),
            P(),
            P(),
            P(COL_ROW),
            P(ROW_COL, None, None),
            P(ROW_COL),
            P(ROW_COL),
            P(ROW_COL),
        ),
        out_specs=(P(None, ROW_COL), P(None, COL_ROW), P()),
        check_vma=False,
    )
```

time: 272 us -> 224 us (0.82)
  blocking collectives: 41.3 us -> 95.9 us
  waiting for transfers between devices: 94.3 us -> 43.1 us
  matrix products: 32.9 us -> 0 us
  starting transfers between devices: 60.1 us -> 29.9 us
  Pallas kernels: 0 us -> 25.9 us
  other arithmetic: 9.7 us -> 0 us
  local copies, waits for them, and re-layouts: 20.2 us -> 12.8 us
  between operations: 11.7 us -> 14.8 us
    all_to_all x2 -> x8, blocking collectives: 41.3 us -> 95.9 us  [swapped(): return lax.all_to_all(blocks, axis, 0, 0, tiled=True)]
    all_to_all x13 -> x5, waiting for transfers between devices: 94.3 us -> 43.1 us  [swapped(): return lax.all_to_all(blocks, axis, 0, 0, tiled=True)]
    dot_general x30 -> x0, matrix products: 32.9 us -> none  [the longest x2 11.3 us: per_device(): jnp.einsum('tij,tj->ti', tile_blocks, wide[tile_cols], preferred_element_...]
    all_to_all x13 -> x5, starting transfers between devices: 60.1 us -> 29.9 us  [swapped(): return lax.all_to_all(blocks, axis, 0, 0, tiled=True)]
    pallas_call x0 -> x15, Pallas kernels: none -> 25.9 us  [the longest x14 20.7 us: call(): pl.pallas_call(kernel, name=name, out_shape=shapes, in_specs=[SCALAR if i...]
    unnamed x15 -> x20, local copies, waits for them, and re-layouts: 4.5 us -> 12.6 us
    broadcast_in_dim x15 -> x0, local copies, waits for them, and re-layouts: 5.19 us -> none  [the longest x12 4.9 us: from_everyone(): jnp.broadcast_to(x[None], (lax.axis_size(axis), *x.shape))]
    broadcast_in_dim x10 -> x0, other arithmetic: 3.54 us -> none  [the longest x4 3.3 us: from_everyone(): jnp.broadcast_to(x[None], (lax.axis_size(axis), *x.shape))]
  transfers between devices with their start and end apart: 13 -> 6, of which waited for: 13 -> 5; matrix products, arithmetic and copies ran while one was open for 5% -> 1% of each run, Pallas kernels for 0% -> 3%
where the time goes in v2:
time: 224 us; the launch traced here: 222 us
  blocking collectives  95.9 us (43%)
  waiting for transfers between devices  43.1 us (19%)
  starting transfers between devices  29.9 us (13%)
  Pallas kernels  25.9 us (12%)
  between operations  14.8 us (7%)
  local copies, waits for them, and re-layouts  12.8 us (6%)
    all_to_all x8, blocking collectives, swapped(): return lax.all_to_all(blocks, axis, 0, 0, tiled=True)  95.9 us
    all_to_all x5, waiting for transfers between devices, swapped(): return lax.all_to_all(blocks, axis, 0, 0, tiled=True)  43.1 us
    all_to_all x5, starting transfers between devices, swapped(): return lax.all_to_all(blocks, axis, 0, 0, tiled=True)  29.9 us
    pallas_call x14, Pallas kernels, call(): pl.pallas_call(kernel, name=name, out_shape=shapes, in_specs=[SCALAR if i...  20.7 us
    unnamed x20, local copies, waits for them, and re-layouts  12.6 us
    pallas_call x1, Pallas kernels, per_device(): pl.pallas_call(regroup_kernel, name='regroup', grid=(cols_n,), in_specs=[...  5.19 us
  transfers between devices with their start and end apart: 6, of which 5 were waited for; matrix products, arithmetic and copies ran while one was open for 1% of the time, Pallas kernels for 3%

profile of v2, /device:TPU:1, one launch (start us, length us, event | category | flops | bytes accessed | tf_op | source)
XLA Modules:
  0.0 222.4 jit_solution(10033800002327255175)
XLA Ops:
  7.2 0.0 copy-start.8
  7.2 0.0 copy-start.7
  7.2 5.2 %regroup.1 = f32[8,16,2048]{2,1,0:T(8,128)} custom-call(f32[16,16384]{1,0:T(8,128)} %start_ref.1), custom_call_target="tpu_custom_call" | custom-call | tf_op jit(solution)/shard_map/regroup/pallas_call | solution.py:370
  12.4 7.5 %all-to-all-start = ((f32[8,16,2048]{2,1,0:T(8,128)}), f32[8,16,2048]{2,1,0:T(8,128)S(1)}, u32[]{:S(2)}, u32[]{:S(2)}) async-start(f32[8,16,2048]{2,1,0:T(8,128)} %regroup.1), calls=%async_computation | async-start | bytes 2097152 | tf_op jit(solution)/shard_map/all_to_all | solution.py:26
  19.9 0.0 all-gather.3.cloned.1.call-start
  19.9 0.8 copy.18.keep_ref
  20.7 13.3 %all-to-all-done = f32[8,16,2048]{2,1,0:T(8,128)S(1)} async-done(((f32[8,16,2048]{2,1,0:T(8,128)}), f32[8,16,2048]{2,1,0:T(8,128)S(1)}, u32[]{:S(2)}, u32[]{:S(2)}) %all-to-all-start) | async-done | bytes 1048608 | tf_op jit(solution)/shard_map/all_to_all | solution.py:26
  34.0 1.6 left_kept.1
  35.7 0.0 all-gather.3.cloned.1.call-update
  35.7 8.0 %all-to-all-start.1 = ((f32[16,8,1024]{2,1,0:T(8,128)}), f32[16,8,1024]{2,1,0:T(8,128)S(1)}, u32[]{:S(2)}, u32[]{:S(2)}) async-start(f32[16,8,1024]{2,1,0:T(8,128)} %bitcast.43), calls=%async_computation.1 | async-start | bytes 1048576 | tf_op jit(solution)/shard_map/all_to_all | solution.py:26
  43.7 0.8 copy.19.keep_ref
  44.5 10.4 %all-to-all-done.1 = f32[16,8,1024]{2,1,0:T(8,128)S(1)} async-done(((f32[16,8,1024]{2,1,0:T(8,128)}), f32[16,8,1024]{2,1,0:T(8,128)S(1)}, u32[]{:S(2)}, u32[]{:S(2)}) %all-to-all-start.1) | async-done | bytes 524320 | tf_op jit(solution)/shard_map/all_to_all | solution.py:26
  54.9 0.7 copy-done.6
  55.6 1.5 right_kept.1
  57.1 17.7 %all_to_all.83.got_ref = f32[128,8,128]{2,1,0:T(8,128)S(1)} all-to-all(f32[128,8,128]{2,1,0:T(8,128)S(1)} %get-tuple-element.33), channel_id=1, replica_groups=mesh['row_0'=2,'row_1'=4,'row_2'=2,'col_0'=2,'col_1'=4] {'row_0','row_1'..., dimensions={0} | all-to-all | bytes 1048576 | tf_op jit(solution)/shard_map/all_to_all | solution.py:26
  74.8 1.3 first_right.1
  76.2 4.9 %all-to-all-start.3 = ((f32[16,8,128]{2,1,0:T(8,128)}), f32[16,8,128]{2,1,0:T(8,128)S(1)}, u32[]{:S(2)}, u32[]{:S(2)}) async-start(f32[16,8,128]{2,1,0:T(8,128)} %get-tuple-element.35), calls=%async_computation.3 | async-start | bytes 131072 | tf_op jit(solution)/shard_map/all_to_all | solution.py:26
  81.7 0.0 copy-done.8
  81.7 0.1 copy.20.pick_ref
  81.8 5.6 %all-to-all-done.3.got_ref = f32[16,8,128]{2,1,0:T(8,128)S(1)} async-done(((f32[16,8,128]{2,1,0:T(8,128)}), f32[16,8,128]{2,1,0:T(8,128)S(1)}, u32[]{:S(2)}, u32[]{:S(2)}) %all-to-all-start.3) | async-done | bytes 65568 | tf_op jit(solution)/shard_map/all_to_all | solution.py:26
  87.5 0.0 copy-done.7
  87.5 3.4 %copy-done = bf16[64,256,256]{2,1,0:T(8,128)(2,1)S(1)} copy-done((bf16[64,256,256]{2,1,0:T(8,128)(2,1)S(1)}, bf16[64,256,256]{2,1,0:T(8,128)(2,1)}, u32[]{:S(2)}) %copy-start) | copy-done | bytes 8388632
  90.9 2.8 %forward.2 = f32[8,136,128]{2,1,0:T(8,128)S(1)} custom-call(f32[16,8,128]{2,1,0:T(8,128)S(1)} %all-to-all-done.3.got_ref, bf16[64,256,256]{2,1,0:T(8,128)(2,1)S(1)} %copy-done, s32[64,1]{1,0:T(8,128)S(1)} %copy.20.pick_ref, s32[1,64]{1,0:T(1,128)S(1)} %bitcast.37, s32[1]{0:T(128)S(6)} %copy.27.count_ref, f32[8,128]{1,0:T(8,128)S(1)} %get-tuple-element.36.refs_0_), custom_call_target="tpu_custom_call" | custom-call | tf_op jit(solution)/shard_map/forward/pallas_call | solution.py:340
  93.7 14.1 %all_to_all.84.got_ref = f32[8,136,128]{2,1,0:T(8,128)S(1)} all-to-all(f32[8,136,128]{2,1,0:T(8,128)S(1)} %forward.2), channel_id=1, replica_groups=mesh['row_0'=2,'row_1'=4,'row_2'=2,'col_0'=2,'col_1'=4] {'col_0','col_1'}, dimensions={0} | all-to-all | bytes 1114112 | tf_op jit(solution)/shard_map/all_to_all | solution.py:26
  107.8 1.7 copy-done.3
  109.5 1.1 left_dots.2
  110.6 5.7 %all-to-all-start.5 = ((f32[16,16,128]{2,1,0:T(8,128)}), f32[16,16,128]{2,1,0:T(8,128)S(1)}, u32[]{:S(2)}, u32[]{:S(2)}) async-start(f32[16,16,128]{2,1,0:T(8,128)} %get-tuple-element.37), calls=%async_computation.5 | async-start | bytes 262144 | tf_op jit(solution)/shard_map/all_to_all | solution.py:26
  116.3 0.1 copy.21.pick_ref
  116.4 6.1 %all-to-all-done.5.got_ref = f32[16,16,128]{2,1,0:T(8,128)S(1)} async-done(((f32[16,16,128]{2,1,0:T(8,128)}), f32[16,16,128]{2,1,0:T(8,128)S(1)}, u32[]{:S(2)}, u32[]{:S(2)}) %all-to-all-start.5) | async-done | bytes 131104 | tf_op jit(solution)/shard_map/all_to_all | solution.py:26
  122.5 3.4 %copy-done.1 = bf16[64,256,256]{2,1,0:T(8,128)(2,1)S(1)} copy-done((bf16[64,256,256]{2,1,0:T(8,128)(2,1)S(1)}, bf16[64,256,256]{2,1,0:T(8,128)(2,1)}, u32[]{:S(2)}) %copy-start.1) | copy-done | bytes 8388632
  125.9 1.7 copy-done.4
  127.7 2.5 %left.2 = (f32[128,128]{1,0:T(8,128)S(1)}, f32[16,128]{1,0:T(8,128)S(1)}, f32[48,128]{1,0:T(8,128)S(1)}, f32[1,128]{1,0:T(1,128)S(1)}, f32[16,8,128]{2,1,0:T(8,128)S(1)}) custom-call(f32[16,16,128]{2,1,0:T(8,128)S(1)} %all-to-all-done.5.got_ref, f32[128,128]{1,0:T(8,128)S(1)} %get-tuple-element.38.image_ref, f32[8,40,2048]{2,1,0:T(8,128)S(1)} %bitcast.25, ...), custom_call_target="tpu_custom_call" | custom-call | tf_op jit(solution)/shard_map/left/pallas_call | solution.py:340
  130.1 9.1 %all_to_all.85.got_ref = f32[16,8,128]{2,1,0:T(8,128)S(1)} all-to-all(f32[16,8,128]{2,1,0:T(8,128)S(1)} %get-tuple-element.40), channel_id=1, replica_groups=mesh['row_0'=2,'row_1'=4,'row_2'=2,'col_0'=2,'col_1'=4] {'row_0','row_1'..., dimensions={0} | all-to-all | bytes 131072 | tf_op jit(solution)/shard_map/all_to_all | solution.py:26
  139.2 0.2 right_dots.2
  139.4 12.7 %all_to_all.86 = f32[128,1,128]{2,1,0:T(1,128)S(1)} all-to-all(f32[128,1,128]{2,1,0:T(1,128)S(1)} %bitcast.32), channel_id=1, replica_groups=mesh['row_0'=2,'row_1'=4,'row_2'=2,'col_0'=2,'col_1'=4] {'row_0','row_1'..., dimensions={0} | all-to-all | bytes 131072 | tf_op jit(solution)/shard_map/all_to_all | solution.py:26
  152.1 0.3 right.1
  152.4 9.4 %all_to_all.87.got_ref = f32[16,8,128]{2,1,0:T(8,128)S(1)} all-to-all(f32[16,8,128]{2,1,0:T(8,128)S(1)} %get-tuple-element.45), channel_id=1, replica_groups=mesh['row_0'=2,'row_1'=4,'row_2'=2,'col_0'=2,'col_1'=4] {'row_0','row_1'..., dimensions={0} | all-to-all | bytes 131072 | tf_op jit(solution)/shard_map/all_to_all | solution.py:26
  161.8 2.8 %forward.3 = f32[8,128,128]{2,1,0:T(8,128)S(1)} custom-call(f32[16,8,128]{2,1,0:T(8,128)S(1)} %all_to_all.87.got_ref, bf16[64,256,256]{2,1,0:T(8,128)(2,1)S(1)} %copy-done.2, s32[64,1]{1,0:T(8,128)S(1)} %copy.20.pick_ref, s32[1,64]{1,0:T(1,128)S(1)} %bitcast.39, s32[1]{0:T(128)S(6)} %copy.27.count_ref), custom_call_target="tpu_custom_call" | custom-call | tf_op jit(solution)/shard_map/forward/pallas_call | solution.py:340
  164.7 13.7 %all_to_all.88.got_ref = f32[8,128,128]{2,1,0:T(8,128)S(1)} all-to-all(f32[8,128,128]{2,1,0:T(8,128)S(1)} %forward.3), channel_id=1, replica_groups=mesh['row_0'=2,'row_1'=4,'row_2'=2,'col_0'=2,'col_1'=4] {'col_0','col_1'}, dimensions={0} | all-to-all | bytes 1048576 | tf_op jit(solution)/shard_map/all_to_all | solution.py:26
  178.3 0.4 left_dots.3
  178.8 10.4 %all_to_all.89 = f32[16,1,128]{2,1,0:T(1,128)S(1)} all-to-all(f32[16,1,128]{2,1,0:T(1,128)S(1)} %bitcast.36), channel_id=1, replica_groups=mesh['row_0'=2,'row_1'=4,'row_2'=2,'col_0'=2,'col_1'=4] {'row_0','row_1'..., dimensions={0} | all-to-all | bytes 16384 | tf_op jit(solution)/shard_map/all_to_all | solution.py:26
  189.1 2.4 %left.3 = (f32[128,128]{1,0:T(8,128)}, f32[16,128]{1,0:T(8,128)S(1)}, f32[48,128]{1,0:T(8,128)}, f32[1,128]{1,0:T(1,128)S(1)}, f32[16,8,128]{2,1,0:T(8,128)S(1)}) custom-call(f32[16,128]{1,0:T(8,128)S(1)} %bitcast.33, f32[128,128]{1,0:T(8,128)S(1)} %get-tuple-element.48.image_ref, f32[8,40,2048]{2,1,0:T(8,128)S(1)} %bitcast.27, ...), custom_call_target="tpu_custom_call" | custom-call | tf_op jit(solution)/shard_map/left/pallas_call | solution.py:340
  191.6 8.9 %all_to_all.90.got_ref = f32[16,8,128]{2,1,0:T(8,128)S(1)} all-to-all(f32[16,8,128]{2,1,0:T(8,128)S(1)} %get-tuple-element.51), channel_id=1, replica_groups=mesh['row_0'=2,'row_1'=4,'row_2'=2,'col_0'=2,'col_1'=4] {'row_0','row_1'..., dimensions={0} | all-to-all | bytes 131072 | tf_op jit(solution)/shard_map/all_to_all | solution.py:26
  200.5 0.9 right_dots.3
  201.4 3.8 %all-to-all-start.12 = ((f32[128,1,128]{2,1,0:T(1,128)}), f32[128,1,128]{2,1,0:T(1,128)S(1)}, u32[]{:S(2)}, u32[]{:S(2)}) async-start(f32[128,1,128]{2,1,0:T(1,128)} %bitcast.18), calls=%async_computation.12 | async-start | bytes 131072 | tf_op jit(solution)/shard_map/all_to_all | solution.py:26
  205.2 1.7 left_out.1
  207.0 7.6 %all-to-all-done.12 = f32[128,1,128]{2,1,0:T(1,128)S(1)} async-done(((f32[128,1,128]{2,1,0:T(1,128)}), f32[128,1,128]{2,1,0:T(1,128)S(1)}, u32[]{:S(2)}, u32[]{:S(2)}) %all-to-all-start.12) | async-done | bytes 65568 | tf_op jit(solution)/shard_map/all_to_all | solution.py:26
  214.6 1.0 last_right.1
  (10 shorter events, 0.0 us)
Async XLA Ops:
  7.2 74.6 %copy-start.8 = (s32[64]{0:T(128)S(1)}, s32[64]{0:T(128)}, u32[]{:S(2)}) copy-start(s32[64]{0:T(128)} %param.16) | copy-start | bytes 772
  7.2 80.3 %copy-start.7 = (s32[64]{0:T(128)S(1)}, s32[64]{0:T(128)}, u32[]{:S(2)}) copy-start(s32[64]{0:T(128)} %param.15) | copy-start | bytes 772
  12.4 21.7 %all-to-all-start = ((f32[8,16,2048]{2,1,0:T(8,128)}), f32[8,16,2048]{2,1,0:T(8,128)S(1)}, u32[]{:S(2)}, u32[]{:S(2)}) async-start(f32[8,16,2048]{2,1,0:T(8,128)} %regroup.1), calls=%async_computation | async-start | bytes 2097152 | tf_op jit(solution)/shard_map/all_to_all | solution.py:26
  19.9 87.9 %all-gather.3.cloned.1.call-start = ((), (), s32[]{:S(2)}) async-start(), calls=%async_computation.13 | async-start | bytes 2949120 | tf_op jit(solution)/shard_map/all_gather | solution.py:380
  35.7 19.2 %all-to-all-start.1 = ((f32[16,8,1024]{2,1,0:T(8,128)}), f32[16,8,1024]{2,1,0:T(8,128)S(1)}, u32[]{:S(2)}, u32[]{:S(2)}) async-start(f32[16,8,1024]{2,1,0:T(8,128)} %bitcast.43), calls=%async_computation.1 | async-start | bytes 1048576 | tf_op jit(solution)/shard_map/all_to_all | solution.py:26
  54.9 0.7 copy-start.6
  76.2 11.3 %all-to-all-start.3 = ((f32[16,8,128]{2,1,0:T(8,128)}), f32[16,8,128]{2,1,0:T(8,128)S(1)}, u32[]{:S(2)}, u32[]{:S(2)}) async-start(f32[16,8,128]{2,1,0:T(8,128)} %get-tuple-element.35), calls=%async_computation.3 | async-start | bytes 131072 | tf_op jit(solution)/shard_map/all_to_all | solution.py:26
  87.5 3.4 %copy-start = (bf16[64,256,256]{2,1,0:T(8,128)(2,1)S(1)}, bf16[64,256,256]{2,1,0:T(8,128)(2,1)}, u32[]{:S(2)}) copy-start(bf16[64,256,256]{2,1,0:T(8,128)(2,1)} %tiles_ref.7) | copy-start | bytes 25165828
  107.8 1.7 copy-start.3
  110.6 11.9 %all-to-all-start.5 = ((f32[16,16,128]{2,1,0:T(8,128)}), f32[16,16,128]{2,1,0:T(8,128)S(1)}, u32[]{:S(2)}, u32[]{:S(2)}) async-start(f32[16,16,128]{2,1,0:T(8,128)} %get-tuple-element.37), calls=%async_computation.5 | async-start | bytes 262144 | tf_op jit(solution)/shard_map/all_to_all | solution.py:26
  122.5 3.4 %copy-start.1 = (bf16[64,256,256]{2,1,0:T(8,128)(2,1)S(1)}, bf16[64,256,256]{2,1,0:T(8,128)(2,1)}, u32[]{:S(2)}) copy-start(bf16[64,256,256]{2,1,0:T(8,128)(2,1)} %tiles_ref.7) | copy-start | bytes 25165828
  125.9 1.7 copy-start.4
  127.7 34.2 %copy-start.2 = (bf16[64,256,256]{2,1,0:T(8,128)(2,1)S(1)}, bf16[64,256,256]{2,1,0:T(8,128)(2,1)}, u32[]{:S(2)}) copy-start(bf16[64,256,256]{2,1,0:T(8,128)(2,1)} %tiles_ref.7) | copy-start | bytes 25165828
  127.7 50.7 %copy-start.5 = (f32[320,2048]{1,0:T(8,128)S(1)}, f32[320,2048]{1,0:T(8,128)}, u32[]{:S(2)}) copy-start(f32[320,2048]{1,0:T(8,128)} %all-gather.3.cloned.1.call-done) | copy-start | bytes 7864324
  201.4 13.2 %all-to-all-start.12 = ((f32[128,1,128]{2,1,0:T(1,128)}), f32[128,1,128]{2,1,0:T(1,128)S(1)}, u32[]{:S(2)}, u32[]{:S(2)}) async-start(f32[128,1,128]{2,1,0:T(1,128)} %bitcast.18), calls=%async_computation.12 | async-start | bytes 131072 | tf_op jit(solution)/shard_map/all_to_all | solution.py:26
Sparse Core Ops, SparseCore 0:
  35.8 60.9 all-gather.2

commit v3 on v2

--- a/solution.py
+++ b/solution.py
@@ -19,7 +19,8 @@
 LANES = 128
 PAD = 48
 EPS = 1e-06
-VMEM_LIMIT = 30 << 20
+VMEM_LIMIT = 24 << 20
+CHUNKS = 8
 
 
 def swapped(blocks, axis):
@@ -95,14 +96,34 @@
     return jnp.concatenate([col, jnp.zeros((PAD - col.shape[0], 1), F32)], axis=0)
 
 
-def regroup_kernel(start_ref, out_ref):
-    out_ref[...] = start_ref[...][None]
+def prepare_kernel(
+    count_ref, own_u_ref, own_v_ref, start_ref, rows_ref, cols_ref, keep_u_ref, keep_v_ref, next_ref,
+    out_ref, keep_u_out, keep_v_out, next_out, row_lane_ref, col_lane_ref, row_sub_ref, col_sub_ref,
+    index_ref, sems,
+):
+    blocks, _, width = out_ref.shape
+    pairs = [(start_ref.at[:, k * width : (k + 1) * width], out_ref.at[k]) for k in range(blocks)]
+    pairs += [(keep_u_ref, keep_u_out), (keep_v_ref, keep_v_out), (next_ref, next_out)]
+    pairs += [(rows_ref, index_ref.at[0]), (cols_ref, index_ref.at[1])]
+    copies = [pltpu.make_async_copy(a, b, sems.at[n]) for n, (a, b) in enumerate(pairs)]
+    for copy in copies:
+        copy.start()
+    for copy in copies[::-1]:
+        copy.wait()
+    slots = rows_ref.shape[1]
+    double = 2 * slots
+    pair = iota((double, slots), 0) // 2 == iota((double, slots), 1)
+    spot = iota((double, double), 0) == iota((double, double), 1)
+    used = iota((1, double), 1) // 2 < count_ref[0]
+    for n, (lane_ref, sub_ref) in enumerate(((row_lane_ref, row_sub_ref), (col_lane_ref, col_sub_ref))):
+        sub = jnp.sum(jnp.where(pair, index_ref[n].astype(F32), 0.0), axis=1, keepdims=True)
+        sub_ref[...] = sub
+        lane = jnp.sum(jnp.where(spot, sub, 0.0), axis=0, keepdims=True)
+        lane_ref[...] = jnp.where(used, lane, -1.0)
 
 
 def kept_kernel(start_ref, keep_ref, out_ref, gram_ref):
-    basis = lax.dot_general(
-        keep_ref[...], start_ref[...], (((0,), (0,)), ((), ())), precision=HIGH, preferred_element_type=F32
-    )
+    basis = jnp.dot(keep_ref[...], start_ref[...], precision=HIGH, preferred_element_type=F32)
     out_ref[...] = basis
     rows = basis.shape[0]
     wide = jnp.concatenate([basis, jnp.zeros((PAD - rows, basis.shape[1]), F32)], axis=0)
@@ -114,9 +135,7 @@
 
 
 def kept_with_kernel(start_ref, keep_ref, next_ref, out_ref, message_ref, wide_ref):
-    basis = lax.dot_general(
-        keep_ref[...], start_ref[...], (((0,), (0,)), ((), ())), precision=HIGH, preferred_element_type=F32
-    )
+    basis = jnp.dot(keep_ref[...], start_ref[...], precision=HIGH, preferred_element_type=F32)
     out_ref[...] = basis
     rows = basis.shape[0]
     wide_ref[...] = jnp.zeros_like(wide_ref)
@@ -153,26 +172,46 @@
     message_ref[...] = jnp.broadcast_to(new[None], message_ref.shape)
 
 
-def multiplied(forward, entries, tiles_ref, pick_ref, place_ref, count_ref, picked_ref, product_ref):
+def started(source, target, sems):
+    parts = sems.shape[0]
+    step = source.shape[0] // parts
+    copies = [
+        pltpu.make_async_copy(
+            source.at[n * step : (n + 1) * step], target.at[n * step : (n + 1) * step], sems.at[n]
+        )
+        for n in range(parts)
+    ]
+    for copy in copies:
+        copy.start()
+    return copies
+
+
+def multiplied(forward, both, entries, tiles_ref, tile_copies, pick_ref, put_ref, picked_ref, product_ref):
     slots, size = tiles_ref.shape[:2]
     blocks = size // LANES
     rows = entries.shape[0]
-    values = entries.astype(BF16)
-    lane = iota((slots, rows), 1)
+    high = entries.astype(BF16)
+    low = (entries - high.astype(F32)).astype(BF16)
+    lane, part = iota((2 * slots, rows), 1).astype(F32), iota((2 * slots, rows), 0) % 2
     for b in range(blocks):
-        hot = (lane == blocks * pick_ref[...] + b).astype(BF16)
-        picked_ref[:, b * LANES : (b + 1) * LANES] = jnp.dot(hot, values, preferred_element_type=F32)
+        spot = lane == blocks * pick_ref[...] + b
+        picked = jnp.dot((spot & (part == 0)).astype(BF16), high, preferred_element_type=F32)
+        if both:
+            picked = picked + jnp.dot((spot & (part == 1)).astype(BF16), low, preferred_element_type=F32)
+        picked_ref[:, b * LANES : (b + 1) * LANES] = picked
     for t in range(slots):
-        product_ref[t : t + 1] = lax.dot_general(
-            picked_ref[t : t + 1].astype(BF16),
+        if tile_copies and t % (slots // CHUNKS) == 0:
+            tile_copies[t // (slots // CHUNKS)].wait()
+        product_ref[2 * t : 2 * t + 2] = lax.dot_general(
+            picked_ref[2 * t : 2 * t + 2].astype(BF16),
             tiles_ref[t],
             (((1,), (1 if forward else 0,)), ((), ())),
             preferred_element_type=F32,
         )
-    sub, slot = iota((rows, slots), 0), iota((rows, slots), 1)
+    sub = iota((rows, 2 * slots), 0).astype(F32)
     out = None
     for b in range(blocks):
-        hot = ((sub == blocks * place_ref[...] + b) & (slot < count_ref[0])).astype(F32)
+        hot = (sub == blocks * put_ref[...] + b).astype(F32)
         part = jnp.dot(
             hot, product_ref[:, b * LANES : (b + 1) * LANES], precision=HIGH, preferred_element_type=F32
         )
@@ -180,43 +219,53 @@
     return out
 
 
-def forward_kernel(
-    extra, got_ref, tiles_ref, pick_ref, place_ref, count_ref, *refs
+def first_forward_kernel(
+    got_ref, tiles_hbm, pick_ref, put_ref, gram_ref, message_ref, picked_ref, product_ref, tile_sems, tiles_ref
 ):
-    if extra:
-        gram_ref, message_ref, picked_ref, product_ref = refs
-    else:
-        message_ref, picked_ref, product_ref = refs
+    copies = started(tiles_hbm, tiles_ref, tile_sems)
     entries = got_ref[...].reshape(-1, LANES)
-    sums = multiplied(True, entries, tiles_ref, pick_ref, place_ref, count_ref, picked_ref, product_ref)
+    sums = multiplied(True, False, entries, tiles_ref, copies, pick_ref, put_ref, picked_ref, product_ref).astype(BF16)
     rows = sums.shape[0]
+    gram = gram_ref[...]
+    high = gram.astype(BF16).astype(F32)
+    middle = (gram - high).astype(BF16).astype(F32)
+    low = gram - high - middle
+    first = jnp.concatenate([high, middle], axis=0).astype(BF16)
+    second = jnp.concatenate([low, jnp.zeros_like(low)], axis=0).astype(BF16)
     for k in range(message_ref.shape[0]):
         message_ref[k, :rows] = sums
-        if extra:
-            message_ref[k, rows:] = gram_ref[...]
-
-
-def left_dots_kernel(length, got_ref, wide_ref, *refs):
-    refs = list(refs)
+        message_ref[k, rows : rows + 16] = first
+        message_ref[k, rows + 16 : rows + 32] = second
+
+
+def dots_kernel(length, fetch, got_ref, wide_ref, *refs):
+    copies = []
+    if fetch:
+        *others, image_ref, message_ref, near_ref, wide_sems = refs
+        copies = started(wide_ref, near_ref, wide_sems)
+        wide_ref = near_ref
+    else:
+        *others, image_ref, message_ref = refs
     first = got_ref.shape[1] > LANES
-    others = [] if first else [refs.pop(0)]
-    image_ref, message_ref = refs
-    image = jnp.sum(got_ref[:, :LANES], axis=0)
+    image = jnp.sum(got_ref[:, :LANES].astype(F32), axis=0)
     image_ref[...] = image
     parts, count, width = wide_ref.shape
     across = width // LANES
     acc = jnp.zeros((count, LANES), F32)
     for k in range(parts):
+        if copies and k % (parts // CHUNKS) == 0:
+            copies[k // (parts // CHUNKS)].wait()
         for j in range(across):
             r = k * across + j
             acc = acc + wide_ref[k, :, j * LANES : (j + 1) * LANES] * image_ref[r : r + 1]
     dots = padded(jnp.sum(acc, axis=1, keepdims=True))
     for n, other in enumerate(others):
-        dots = dots + at(total(other[...] * image), count + n)
+        dots = dots + at(total(other[...].reshape(image.shape) * image), count + n)
     dots = dots + at(total(image * image), PAD - 1)
     row = as_row(dots) * (1.0 / length)
     if first:
-        gram = jnp.sum(got_ref[:, LANES:], axis=0) * (1.0 / length)
+        grams = jnp.sum(got_ref[:, LANES:].astype(F32), axis=0)
+        gram = (grams[:8] + grams[8:16] + grams[16:24]) * (1.0 / length)
         message_ref[:, :8] = jnp.broadcast_to(gram[None], (message_ref.shape[0], 8, LANES))
         message_ref[:, 8:] = jnp.broadcast_to(row[None], (message_ref.shape[0], 8, LANES))
     else:
@@ -229,22 +278,27 @@
     return jnp.where(last, 0.0, col), total(jnp.where(last, col, 0.0))
 
 
-def left_kernel(
-    m, got_ref, image_ref, wide_ref, tiles_ref, pick_ref, place_ref, count_ref, own_ref, *refs
+def vector_kernel(
+    m, forward, known, fetch, own_ref, got_ref, image_ref, wide_ref, tiles_ref, pick_ref, put_ref, *refs
 ):
-    refs = list(refs)
-    first = len(got_ref.shape) == 3
-    gram_in = None if first else refs.pop(0)
-    others = [] if first else [refs.pop(0)]
-    new_ref, own_out_ref, gram_ref, scale_ref, message_ref, picked_ref, product_ref = refs
+    copies = []
+    if fetch:
+        *refs, near_ref, picked_ref, product_ref, tile_sems = refs if fetch == "keep" else refs[:-4] + refs[-1:] + refs[-4:-1]
+        copies = started(tiles_ref, near_ref, tile_sems)
+        tiles_ref = near_ref
+    else:
+        *refs, picked_ref, product_ref = refs
+    *inputs, new_ref, own_out_ref, gram_ref, scale_ref, message_ref = refs
     parts, count, width = wide_ref.shape
-    if first:
+    if known:
+        gram = inputs[0][...]
+        row = jnp.sum(got_ref[...], axis=0, keepdims=True)
+        others = inputs[1:]
+    else:
         got = jnp.sum(got_ref[...], axis=0)
         gram = unpacked(got[:8], count + 1)
         row = got[8:9]
-    else:
-        gram = gram_in[...]
-        row = jnp.sum(got_ref[...], axis=0, keepdims=True)
+        others = inputs
     dots, square = split_dots(row)
     coef, scale, inverse, grown = solve(gram, dots, square, m)
     gram_ref[...] = grown
@@ -252,18 +306,23 @@
     across = width // LANES
     by_lane = jnp.broadcast_to(coef[:count], (count, LANES))
     for k in range(parts):
-        for j in range(across):
-            r = k * across + j
-            part = wide_ref[k, :, j * LANES : (j + 1) * LANES] * by_lane
-            new_ref[r : r + 1] = image_ref[r : r + 1] - jnp.sum(part, axis=0, keepdims=True)
+        sums = [
+            jnp.sum(wide_ref[k, :, j * LANES : (j + 1) * LANES] * by_lane, axis=0, keepdims=True)
+            for j in range(across)
+        ]
+        span = slice(k * across, (k + 1) * across)
+        new_ref[span] = image_ref[span] - jnp.concatenate(sums, axis=0)
     new = new_ref[...]
     for n, other in enumerate(others):
-        new = new - coef[count + n : count + n + 1] * other[...]
+        new = new - coef[count + n : count + n + 1] * other[...].reshape(new.shape)
     new = new * inverse
     new_ref[...] = new
     own_out_ref[...] = new_ref[pl.ds(pl.multiple_of(own_ref[0] * across, across), across)]
-    sums = multiplied(False, new, tiles_ref, pick_ref, place_ref, count_ref, picked_ref, product_ref)
-    message_ref[...] = sums.reshape(message_ref.shape)
+    sums = multiplied(forward, True, new, tiles_ref, copies, pick_ref, put_ref, picked_ref, product_ref)
+    if message_ref.shape[1] == sums.shape[0]:
+        message_ref[...] = jnp.broadcast_to(sums.astype(message_ref.dtype)[None], message_ref.shape)
+    else:
+        message_ref[...] = sums.reshape(message_ref.shape)
 
 
 def right_dots_kernel(length, got_ref, basis_ref, *refs):
@@ -293,16 +352,6 @@
     return new * inverse, scale, grown
 
 
-def right_kernel(m, got_ref, image_ref, basis_ref, gram_in_ref, *refs):
-    refs = list(refs)
-    vector_ref, gram_ref, scale_ref, message_ref = refs[-4:]
-    new, scale, grown = new_right(m, got_ref, image_ref, basis_ref, gram_in_ref, refs[:-4])
-    vector_ref[...] = new
-    gram_ref[...] = grown
-    scale_ref[...] = jnp.broadcast_to(scale, scale_ref.shape)
-    message_ref[...] = jnp.broadcast_to(new[None], message_ref.shape)
-
-
 def put_rows(out_ref, row, vector):
     for j in range(vector.shape[0]):
         out_ref[row : row + 1, j * LANES : (j + 1) * LANES] = vector[j : j + 1]
@@ -333,20 +382,33 @@
 
 WHOLE = pl.BlockSpec(memory_space=pltpu.VMEM)
 SCALAR = pl.BlockSpec(memory_space=pltpu.SMEM)
-
-
-def call(kernel, name, outs, args, scalars=(), scratch=()):
-    shapes = tuple(jax.ShapeDtypeStruct(s, F32) for s in outs)
-    result = pl.pallas_call(
+FAR = pl.BlockSpec(memory_space=pltpu.HBM)
+
+
+def in_hbm(x):
+    return pltpu.with_memory_space_constraint(x, pltpu.HBM)
+
+
+def in_vmem(x):
+    return pltpu.with_memory_space_constraint(x, pltpu.VMEM)
+
+
+def call(kernel, name, outs, args, scalars=(), scratch=(), far=(), near=()):
+    shapes = tuple(jax.ShapeDtypeStruct(s, F32) if isinstance(s, tuple) else s for s in outs)
+    specs = [SCALAR if i in scalars else FAR if i in far else WHOLE for i in range(len(args))]
+    return pl.pallas_call(
         kernel,
         name=name,
         out_shape=shapes,
-        in_specs=[SCALAR if i in scalars else WHOLE for i in range(len(args))],
+        in_specs=specs,
         out_specs=tuple(WHOLE for _ in shapes),
         scratch_shapes=list(scratch),
         compiler_params=pltpu.CompilerParams(vmem_limit_bytes=VMEM_LIMIT),
-    )(*args)
-    return result
+    )(*(in_hbm(x) if i in far else in_vmem(x) if i in near else x for i, x in enumerate(args)))
+
+
+def after(x, *earlier):
+    return lax.optimization_barrier((x, *earlier))[0]
 
 
 def per_device(
@@ -361,27 +423,46 @@
     u_own, v_own = u_range // cols_n, v_range // rows_n
     u_length, v_length = u_range * rows_n, v_range * cols_n
     u_rows, v_rows = u_own // LANES, v_own // LANES
-    full = u_range // LANES
-    row_lane, row_sub = tile_rows.reshape(1, slots), tile_rows.reshape(slots, 1)
-    col_lane, col_sub = tile_cols.reshape(1, slots), tile_cols.reshape(slots, 1)
-    own = lax.axis_index(COL).reshape(1)
-    products = [pltpu.VMEM((slots, size), F32), pltpu.VMEM((slots, size), F32)]
-
-    u_blocks = pl.pallas_call(
-        regroup_kernel,
-        name="regroup",
-        grid=(cols_n,),
-        in_specs=[pl.BlockSpec((u_here, u_own), lambda k: (0, k))],
-        out_specs=pl.BlockSpec((1, u_here, u_own), lambda k: (k, 0, 0)),
-        out_shape=jax.ShapeDtypeStruct((cols_n, u_here, u_own), F32),
-    )(u_start)
+    u_full, v_full = u_range // LANES, v_range // LANES
+    products = [pltpu.VMEM((2 * slots, size), F32), pltpu.VMEM((2 * slots, size), F32)]
+    sems = [pltpu.SemaphoreType.DMA((CHUNKS,))]
+    narrow = functools.partial(jax.ShapeDtypeStruct, dtype=BF16)
+
+    own_u, own_v = lax.axis_index(COL).reshape(1), lax.axis_index(ROW).reshape(1)
+    u_blocks, keep_u, keep_v, next_rows, row_lane, col_lane, row_sub, col_sub = call(
+        prepare_kernel,
+        "prepare",
+        [
+            (cols_n, u_here, u_own),
+            keep_u.T.shape,
+            keep_v.T.shape,
+            (v_rows, LANES),
+            (1, 2 * slots),
+            (1, 2 * slots),
+            (2 * slots, 1),
+            (2 * slots, 1),
+        ],
+        [
+            tile_count,
+            own_u,
+            own_v,
+            u_start,
+            tile_rows.reshape(1, slots),
+            tile_cols.reshape(1, slots),
+            keep_u.T,
+            keep_v.T,
+            v_next.reshape(v_rows, LANES),
+        ],
+        scalars=(0, 1, 2),
+        scratch=[pltpu.VMEM((2, 1, slots), jnp.int32), pltpu.SemaphoreType.DMA((cols_n + 5,))],
+        far=range(3, 9),
+    )
     u_got = swapped(u_blocks, COL).reshape(-1, u_own)
     u_kept, u_gram = call(kept_kernel, "left_kept", [(keep, u_own), (8, LANES)], [u_got, keep_u])
     u_wide = lax.all_gather(u_kept, COL, axis=0)
 
-    v_blocks = jnp.moveaxis(v_start.reshape(v_here, rows_n, v_own), 1, 0)
+    v_blocks = after(jnp.moveaxis(v_start.reshape(v_here, rows_n, v_own), 1, 0), u_kept)
     v_got = swapped(v_blocks, ROW).reshape(-1, v_own)
-    next_rows = v_next.reshape(v_rows, LANES)
     v_kept, message = call(
         kept_with_kernel,
         "right_kept",
@@ -389,6 +470,7 @@
         [v_got, keep_v, next_rows],
         scratch=[pltpu.VMEM((LANES, v_own), F32)],
     )
+    v_wide = lax.all_gather(v_kept, ROW, axis=0)
     got = swapped(message, ROW_COL)
     v_0, gram_v, message = call(
         functools.partial(first_kernel, v_length),
@@ -396,66 +478,82 @@
         [(v_rows, LANES), (PAD, LANES), (rows_n, v_rows, LANES)],
         [got, v_kept, next_rows],
     )
-
-    def forward(message, extra):
-        got = swapped(message, ROW)
-        (message,) = call(
-            functools.partial(forward_kernel, bool(extra)),
-            "forward",
-            [(cols_n, full + 8 * len(extra), LANES)],
-            [got, tile_blocks, col_sub, row_lane, tile_count, *extra],
-            scalars=(4,),
-            scratch=products,
+    v_0_wide = swapped(message, ROW)
+    tile_room = [pltpu.VMEM(tile_blocks.shape, BF16)]
+    (message,) = call(
+        first_forward_kernel,
+        "forward",
+        [narrow((cols_n, u_full + 32, LANES))],
+        [v_0_wide, tile_blocks, col_sub, row_lane, u_gram],
+        scratch=products + sems + tile_room,
+        far=(1,),
+    )
+    got = swapped(message, COL)
+
+    def wide_dots(got, wide, others, length, name, image, dots):
+        return call(
+            functools.partial(dots_kernel, length, True),
+            name,
+            [image, dots, pltpu.VMEM(wide.shape, F32)],
+            [got, wide, *others],
+            scratch=sems,
+            far=(1,),
         )
-        return swapped(message, COL)
-
-    def left(got, m, gram, others):
-        first = gram is None
-        image, message = call(
-            functools.partial(left_dots_kernel, u_length),
-            "left_dots",
-            [(full, LANES), (rows_n, 16, LANES) if first else (rows_n, LANES)],
-            [got, u_wide, *others],
+
+    def left(dots, image, wide, tiles, m, gram, others, message):
+        known = [] if gram is None else [gram]
+        return call(
+            functools.partial(vector_kernel, m, False, bool(known), None if known else "once"),
+            "left",
+            [(u_full, LANES), (u_rows, LANES), (PAD, LANES), (1, LANES), message],
+            [own_u, swapped(dots, ROW), image, wide, tiles, row_sub, col_lane, *known, *others],
+            scalars=(0,),
+            scratch=products if known else products + sems + tile_room,
+            near=(3, 4) if known else (3,),
+            far=() if known else (4,),
         )
-        got = swapped(message, ROW)
-        known = [] if first else [gram]
-        new, own_new, gram, scale, message = call(
-            functools.partial(left_kernel, m),
-            "left",
-            [(full, LANES), (u_rows, LANES), (PAD, LANES), (1, LANES), (rows_n, v_rows, LANES)],
-            [got, image, u_wide, tile_blocks, row_sub, col_lane, tile_count, own, *known, *others],
-            scalars=(6, 7),
-            scratch=products,
-        )
-        return new, own_new, gram, scale, swapped(message, ROW)
-
-    def right_dots(got, others):
-        image, message = call(
-            functools.partial(right_dots_kernel, v_length),
-            "right_dots",
-            [(v_rows, LANES), (devices, LANES)],
-            [got, v_kept, *others],
-        )
-        return image, swapped(message, ROW_COL)
-
-    got = forward(message, [u_gram])
-    u_0_wide, u_0, gram_u, alpha_0, got = left(got, keep, None, [])
-    image, got = right_dots(got, [v_0])
-    v_1, gram_v, beta_0, message = call(
-        functools.partial(right_kernel, keep + 1),
+
+    image, dots, u_near = wide_dots(got, u_wide, [], u_length, "left_dots", (u_full, LANES), (rows_n, 16, LANES))
+    u_0_wide, u_0, gram_u, alpha_0, message = left(
+        dots, image, u_near, tile_blocks, keep, None, [], narrow((rows_n, v_full, LANES))
+    )
+    image, dots, v_near = wide_dots(
+        swapped(message, ROW), v_wide, [v_0_wide], v_length, "right_dots", (v_full, LANES), (cols_n, LANES)
+    )
+    _, v_1, gram_v, beta_0, message, tiles = call(
+        functools.partial(vector_kernel, keep + 1, True, True, "keep"),
         "right",
-        [(v_rows, LANES), (PAD, LANES), (1, LANES), (rows_n, v_rows, LANES)],
-        [got, image, v_kept, gram_v, v_0],
-    )
-    got = forward(message, [])
-    _, u_1, gram_u, alpha_1, got = left(got, keep + 1, gram_u, [u_0_wide])
+        [(v_full, LANES), (v_rows, LANES), (PAD, LANES), (1, LANES), narrow((cols_n, u_full, LANES)), *tile_room],
+        [own_v, swapped(dots, COL), image, v_near, tile_blocks, col_sub, row_lane, gram_v, v_0_wide],
+        scalars=(0,),
+        scratch=products + sems,
+        near=(3,),
+        far=(4,),
+    )
+    got = swapped(message, COL)
+    image, dots = call(
+        functools.partial(dots_kernel, u_length, False),
+        "left_dots",
+        [(u_full, LANES), (rows_n, LANES)],
+        [got, u_near, u_0_wide],
+        near=(1,),
+    )
+    _, u_1, _, alpha_1, message = left(
+        dots, image, u_near, tiles, keep + 1, gram_u, [u_0_wide], (rows_n, v_rows, LANES)
+    )
+    got = swapped(message, ROW)
     (u_basis,) = call(left_out_kernel, "left_out", [(keep + 2, u_own)], [u_kept, u_0, u_1])
-    image, got = right_dots(got, [v_0, v_1])
+    image, dots = call(
+        functools.partial(right_dots_kernel, v_length),
+        "last_dots",
+        [(v_rows, LANES), (devices, LANES)],
+        [got, v_kept, v_0, v_1],
+    )
     v_basis, scales = call(
         functools.partial(last_kernel, keep + 2),
         "last_right",
         [(keep + 3, v_own), (2, 2)],
-        [got, image, v_kept, gram_v, v_0, v_1, alpha_0, alpha_1, beta_0],
+        [swapped(dots, ROW_COL), image, v_kept, gram_v, v_0, v_1, alpha_0, alpha_1, beta_0],
     )
     return u_basis, v_basis, scales
 

time: 224 us -> 212 us (0.946)
  blocking collectives: 95.9 us -> 152 us
  waiting for transfers between devices: 43.1 us -> 7.68 us
  starting transfers between devices: 29.9 us -> 3.9 us
  local copies, waits for them, and re-layouts: 12.8 us -> 0.01 us
  Pallas kernels: 25.9 us -> 33.1 us
    all_to_all x8 -> x11, blocking collectives: 95.9 us -> 152 us  [swapped(): return lax.all_to_all(blocks, axis, 0, 0, tiled=True)]
    all_to_all x5 -> x1, waiting for transfers between devices: 43.1 us -> 7.64 us  [swapped(): return lax.all_to_all(blocks, axis, 0, 0, tiled=True)]
    all_to_all x5 -> x1, starting transfers between devices: 29.9 us -> 3.82 us  [swapped(): return lax.all_to_all(blocks, axis, 0, 0, tiled=True)]
    unnamed x20 -> x2, local copies, waits for them, and re-layouts: 12.6 us -> 0.01 us
    pallas_call x15 -> x14, Pallas kernels: 25.9 us -> 33.1 us  [call(): pl.pallas_call(kernel, name=name, out_shape=shapes, in_specs=specs, out_s...]
  transfers between devices with their start and end apart: 6 -> 3, of which waited for: 5 -> 1; matrix products, arithmetic and copies ran while one was open for 1% -> 0% of each run, Pallas kernels for 3% -> 8%
where the time goes in v3:
time: 212 us
  blocking collectives  152 us (72%)
  Pallas kernels  33.1 us (16%)
  between operations  14.8 us (7%)
  waiting for transfers between devices  7.68 us (4%)
  starting transfers between devices  3.9 us (2%)
    all_to_all x11, blocking collectives, swapped(): return lax.all_to_all(blocks, axis, 0, 0, tiled=True)  152 us
    pallas_call x14, Pallas kernels, call(): pl.pallas_call(kernel, name=name, out_shape=shapes, in_specs=specs, out_s...  33.1 us
    all_to_all x1, waiting for transfers between devices, swapped(): return lax.all_to_all(blocks, axis, 0, 0, tiled=True)  7.64 us
  transfers between devices with their start and end apart: 3, of which 1 were waited for; matrix products, arithmetic and copies ran while one was open for 0% of the time, Pallas kernels for 8%

profile of v3, /device:TPU:1, one launch (start us, length us, event | category | flops | bytes accessed | tf_op | source)
XLA Modules:
  0.0 211.5 jit_solution(4018996885791118504)
XLA Ops:
  7.2 0.0 copy-start
  7.2 0.0 all-gather.5.cloned.1.call-start
  7.9 1.5 prepare.1
  9.5 22.9 %all_to_all.78 = f32[8,16,2048]{2,1,0:T(8,128)S(1)} all-to-all(f32[8,16,2048]{2,1,0:T(8,128)S(1)} %get-tuple-element.44), channel_id=1, replica_groups=mesh['row_0'=2,'row_1'=4,'row_2'=2,'col_0'=2,'col_1'=4] {'col_0','col_1'}, dimensions={0} | all-to-all | bytes 2097152 | tf_op jit(solution)/shard_map/all_to_all | solution.py:27
  32.3 1.6 left_kept.1
  33.9 0.0 all-gather.5.cloned.1.call-update
  33.9 0.0 all-gather.7.cloned.1.call-start
  34.0 0.0 copy-done
  34.0 19.8 %all_to_all.79 = f32[16,8,1024]{2,1,0:T(8,128)S(1)} all-to-all(f32[16,8,1024]{2,1,0:T(8,128)S(1)} %bitcast.35), channel_id=1, replica_groups=mesh['row_0'=2,'row_1'=4,'row_2'=2,'col_0'=2,'col_1'=4] {'row_0','row_1'..., dimensions={0} | all-to-all | bytes 1048576 | tf_op jit(solution)/shard_map/all_to_all | solution.py:27
  53.8 1.5 right_kept.1
  55.3 0.0 all-gather.7.cloned.1.call-update
  55.3 17.5 %all_to_all.80.got_ref = f32[128,8,128]{2,1,0:T(8,128)S(1)} all-to-all(f32[128,8,128]{2,1,0:T(8,128)S(1)} %get-tuple-element.50), channel_id=1, replica_groups=mesh['row_0'=2,'row_1'=4,'row_2'=2,'col_0'=2,'col_1'=4] {'row_0','row_1'..., dimensions={0} | all-to-all | bytes 1048576 | tf_op jit(solution)/shard_map/all_to_all | solution.py:27
  72.8 1.6 first_right.1
  74.4 10.9 %all_to_all.81.got_ref.refs_0_.refs_1_ = f32[16,8,128]{2,1,0:T(8,128)S(1)} all-to-all(f32[16,8,128]{2,1,0:T(8,128)S(1)} %get-tuple-element.52), channel_id=1, replica_groups=mesh['row_0'=2,'row_1'=4,'row_2'=2,'col_0'=2,'col_1'=4] {'row_0','row_1'..., dimensions={0} | all-to-all | bytes 131072 | tf_op jit(solution)/shard_map/all_to_all | solution.py:27
  85.4 4.8 %forward.1 = bf16[8,160,128]{2,1,0:T(8,128)(2,1)S(1)} custom-call(f32[16,8,128]{2,1,0:T(8,128)S(1)} %all_to_all.81.got_ref.refs_0_.refs_1_, bf16[64,256,256]{2,1,0:T(8,128)(2,1)} %tiles_ref.3, f32[128,1]{1,0:T(8,128)S(1)} %get-tuple-element.53.pick_ref, f32[1,128]{1,0:T(1,128)S(1)} %get-tuple-element.54.put_ref, f32[8,128]{1,0:T(8,128)S(1)} %get-tuple-element.55.gram_ref), custom_call_target="tpu_custom_call" | custom-call | tf_op jit(solution)/shard_map/forward/pallas_call | solution.py:399
  90.2 11.7 %all_to_all.82.got_ref = bf16[8,160,128]{2,1,0:T(8,128)(2,1)S(1)} all-to-all(bf16[8,160,128]{2,1,0:T(8,128)(2,1)S(1)} %forward.1), channel_id=1, replica_groups=mesh['row_0'=2,'row_1'=4,'row_2'=2,'col_0'=2,'col_1'=4] {'col_0','col_1'}, dimensions={0} | all-to-all | bytes 655360 | tf_op jit(solution)/shard_map/all_to_all | solution.py:27
  101.8 0.0 all-gather.5.cloned.1.call-done
  101.8 1.9 left_dots.2
  103.8 13.3 %all_to_all.83.got_ref = f32[16,16,128]{2,1,0:T(8,128)S(1)} all-to-all(f32[16,16,128]{2,1,0:T(8,128)S(1)} %get-tuple-element.56), channel_id=1, replica_groups=mesh['row_0'=2,'row_1'=4,'row_2'=2,'col_0'=2,'col_1'=4] {'row_0','row_1'..., dimensions={0} | all-to-all | bytes 262144 | tf_op jit(solution)/shard_map/all_to_all | solution.py:27
  117.1 4.9 %left.2 = (f32[128,128]{1,0:T(8,128)S(1)}, f32[16,128]{1,0:T(8,128)S(1)}, f32[48,128]{1,0:T(8,128)S(1)}, f32[1,128]{1,0:T(1,128)S(1)}, bf16[16,128,128]{2,1,0:T(8,128)(2,1)S(1)}) custom-call(s32[1]{0:T(128)} %bitcast.own_u_ref.own_ref, f32[16,16,128]{2,1,0:T(8,128)S(1)} %all_to_all.83.got_ref, f32[128,128]{1,0:T(8,128)S(1)} %get-tuple-element.57.image_ref, ...), custom_call_target="tpu_custom_call" | custom-call | tf_op jit(solution)/shard_map/left/pallas_call | solution.py:399
  122.0 12.7 %all_to_all.84.got_ref = bf16[16,128,128]{2,1,0:T(8,128)(2,1)S(1)} all-to-all(bf16[16,128,128]{2,1,0:T(8,128)(2,1)S(1)} %get-tuple-element.62), channel_id=1, replica_groups=mesh['row_0'=2,'row_1'=4,'row_2'=2,'col_0'=2,'col_1'=4] {'row_0','row_1'..., dimensions={0} | all-to-all | bytes 1048576 | tf_op jit(solution)/shard_map/all_to_all | solution.py:27
  134.7 0.0 all-gather.7.cloned.1.call-done
  134.7 2.0 right_dots.1
  136.6 12.9 %all_to_all.85 = f32[8,1,128]{2,1,0:T(1,128)S(1)} all-to-all(f32[8,1,128]{2,1,0:T(1,128)S(1)} %bitcast.32), channel_id=1, replica_groups=mesh['row_0'=2,'row_1'=4,'row_2'=2,'col_0'=2,'col_1'=4] {'col_0','col_1'}, dimensions={0} | all-to-all | bytes 8192 | tf_op jit(solution)/shard_map/all_to_all | solution.py:27
  149.5 5.0 %right.1 = (f32[128,128]{1,0:T(8,128)}, f32[8,128]{1,0:T(8,128)S(1)}, f32[48,128]{1,0:T(8,128)S(1)}, f32[1,128]{1,0:T(1,128)S(1)}, bf16[8,128,128]{2,1,0:T(8,128)(2,1)S(1)}, /*index=5*/bf16[64,256,256]{2,1,0:T(8,128)(2,1)S(1)}) custom-call(s32[1]{0:T(128)} %bitcast.1.own_v_ref.own_ref, f32[8,128]{1,0:T(8,128)S(1)} %bitcast.30, ...), custom_call_target="tpu_custom_call" | custom-call | tf_op jit(solution)/shard_map/right/pallas_call | solution.py:399
  154.5 10.0 %all_to_all.86.got_ref = bf16[8,128,128]{2,1,0:T(8,128)(2,1)S(1)} all-to-all(bf16[8,128,128]{2,1,0:T(8,128)(2,1)S(1)} %get-tuple-element.67), channel_id=1, replica_groups=mesh['row_0'=2,'row_1'=4,'row_2'=2,'col_0'=2,'col_1'=4] {'col_0','col_1'}, dimensions={0} | all-to-all | bytes 524288 | tf_op jit(solution)/shard_map/all_to_all | solution.py:27
  164.5 0.4 left_dots.3
  165.0 11.4 %all_to_all.87 = f32[16,1,128]{2,1,0:T(1,128)S(1)} all-to-all(f32[16,1,128]{2,1,0:T(1,128)S(1)} %bitcast.31), channel_id=1, replica_groups=mesh['row_0'=2,'row_1'=4,'row_2'=2,'col_0'=2,'col_1'=4] {'row_0','row_1'..., dimensions={0} | all-to-all | bytes 16384 | tf_op jit(solution)/shard_map/all_to_all | solution.py:27
  176.4 2.4 %left.3 = (f32[128,128]{1,0:T(8,128)}, f32[16,128]{1,0:T(8,128)S(1)}, f32[48,128]{1,0:T(8,128)}, f32[1,128]{1,0:T(1,128)S(1)}, f32[16,8,128]{2,1,0:T(8,128)S(1)}) custom-call(s32[1]{0:T(128)} %bitcast.own_u_ref.own_ref, f32[16,128]{1,0:T(8,128)S(1)} %bitcast.29, f32[128,128]{1,0:T(8,128)S(1)} %get-tuple-element.70.image_ref, ...), custom_call_target="tpu_custom_call" | custom-call | tf_op jit(solution)/shard_map/left/pallas_call | solution.py:399
  178.8 8.9 %all_to_all.88.got_ref = f32[16,8,128]{2,1,0:T(8,128)S(1)} all-to-all(f32[16,8,128]{2,1,0:T(8,128)S(1)} %get-tuple-element.74), channel_id=1, replica_groups=mesh['row_0'=2,'row_1'=4,'row_2'=2,'col_0'=2,'col_1'=4] {'row_0','row_1'..., dimensions={0} | all-to-all | bytes 131072 | tf_op jit(solution)/shard_map/all_to_all | solution.py:27
  187.8 1.8 last_dots.1
  189.5 3.8 %all-to-all-start.11 = ((f32[128,1,128]{2,1,0:T(1,128)}), f32[128,1,128]{2,1,0:T(1,128)S(1)}, u32[]{:S(2)}, u32[]{:S(2)}) async-start(f32[128,1,128]{2,1,0:T(1,128)} %bitcast.20), calls=%async_computation.11 | async-start | bytes 131072 | tf_op jit(solution)/shard_map/all_to_all | solution.py:27
  193.4 1.7 left_out.1
  195.1 7.6 %all-to-all-done.11 = f32[128,1,128]{2,1,0:T(1,128)S(1)} async-done(((f32[128,1,128]{2,1,0:T(1,128)}), f32[128,1,128]{2,1,0:T(1,128)S(1)}, u32[]{:S(2)}, u32[]{:S(2)}) %all-to-all-start.11) | async-done | bytes 65568 | tf_op jit(solution)/shard_map/all_to_all | solution.py:27
  202.8 1.9 last_right.1
Async XLA Ops:
  7.2 26.8 %copy-start = (f32[8,16384]{1,0:T(8,128)S(1)}, f32[8,16384]{1,0:T(8,128)}, u32[]{:S(2)}) copy-start(f32[8,16384]{1,0:T(8,128)} %param.10) | copy-start | bytes 1572868
  7.2 94.7 %all-gather.5.cloned.1.call-start = ((), (), s32[]{:S(2)}) async-start(), calls=%async_computation.12 | async-start | bytes 2949120 | tf_op jit(solution)/shard_map/all_gather | solution.py:462
  33.9 100.7 %all-gather.7.cloned.1.call-start = ((), (), s32[]{:S(2)}) async-start(), calls=%async_computation.13 | async-start | bytes 2785280 | tf_op jit(solution)/shard_map/all_gather | solution.py:473
  189.5 13.2 %all-to-all-start.11 = ((f32[128,1,128]{2,1,0:T(1,128)}), f32[128,1,128]{2,1,0:T(1,128)S(1)}, u32[]{:S(2)}, u32[]{:S(2)}) async-start(f32[128,1,128]{2,1,0:T(1,128)} %bitcast.20), calls=%async_computation.11 | async-start | bytes 131072 | tf_op jit(solution)/shard_map/all_to_all | solution.py:27
Sparse Core Ops, SparseCore 0:
  34.1 60.1 all-gather.4
  96.0 35.6 all-gather.6

commit v4 on v3

--- a/solution.py
+++ b/solution.py
@@ -18,6 +18,7 @@
 BF16 = jnp.bfloat16
 LANES = 128
 PAD = 48
+PLACES = 4
 EPS = 1e-06
 VMEM_LIMIT = 24 << 20
 CHUNKS = 8
@@ -97,7 +98,7 @@
 
 
 def prepare_kernel(
-    count_ref, own_u_ref, own_v_ref, start_ref, rows_ref, cols_ref, keep_u_ref, keep_v_ref, next_ref,
+    count_ref, own_ref, start_ref, rows_ref, cols_ref, keep_u_ref, keep_v_ref, next_ref,
     out_ref, keep_u_out, keep_v_out, next_out, row_lane_ref, col_lane_ref, row_sub_ref, col_sub_ref,
     index_ref, sems,
 ):
@@ -238,26 +239,38 @@
         message_ref[k, rows + 16 : rows + 32] = second
 
 
-def dots_kernel(length, fetch, got_ref, wide_ref, *refs):
-    copies = []
-    if fetch:
-        *others, image_ref, message_ref, near_ref, wide_sems = refs
-        copies = started(wide_ref, near_ref, wide_sems)
-        wide_ref = near_ref
+def forward_kernel(got_ref, tiles_ref, pick_ref, put_ref, message_ref, picked_ref, product_ref):
+    entries = got_ref[...].reshape(-1, LANES)
+    sums = multiplied(True, True, entries, tiles_ref, [], pick_ref, put_ref, picked_ref, product_ref)
+    message_ref[...] = jnp.broadcast_to(sums.astype(BF16)[None], message_ref.shape)
+
+
+def dots_kernel(length, first, own_ref, got_ref, *refs):
+    if first:
+        *pairs, image_ref, message_ref, near_ref, sems = refs
+        others = []
+        ranks = [own_ref[0] ^ (PLACES * h + k) for k in range(PLACES) for h in range(2)]
+        copies = [
+            pltpu.make_async_copy(pairs[n // 2].at[n % 2], near_ref.at[rank], sems.at[n])
+            for n, rank in enumerate(ranks)
+        ]
+        for copy in copies:
+            copy.start()
     else:
-        *others, image_ref, message_ref = refs
-    first = got_ref.shape[1] > LANES
+        near_ref, *others, image_ref, message_ref = refs
+        ranks, copies = range(near_ref.shape[0]), []
     image = jnp.sum(got_ref[:, :LANES].astype(F32), axis=0)
     image_ref[...] = image
-    parts, count, width = wide_ref.shape
+    _, count, width = near_ref.shape
     across = width // LANES
     acc = jnp.zeros((count, LANES), F32)
-    for k in range(parts):
-        if copies and k % (parts // CHUNKS) == 0:
-            copies[k // (parts // CHUNKS)].wait()
+    for n, rank in enumerate(ranks):
+        if copies:
+            copies[n].wait()
+        start = rank * across
+        part = image_ref[pl.ds(pl.multiple_of(start, across) if first else start, across)]
         for j in range(across):
-            r = k * across + j
-            acc = acc + wide_ref[k, :, j * LANES : (j + 1) * LANES] * image_ref[r : r + 1]
+            acc = acc + near_ref[rank, :, j * LANES : (j + 1) * LANES] * part[j : j + 1]
     dots = padded(jnp.sum(acc, axis=1, keepdims=True))
     for n, other in enumerate(others):
         dots = dots + at(total(other[...].reshape(image.shape) * image), count + n)
@@ -279,15 +292,15 @@
 
 
 def vector_kernel(
-    m, forward, known, fetch, own_ref, got_ref, image_ref, wide_ref, tiles_ref, pick_ref, put_ref, *refs
+    m, known, own_ref, got_ref, image_ref, wide_ref, tiles_ref, pick_ref, put_ref, *refs
 ):
     copies = []
-    if fetch:
-        *refs, near_ref, picked_ref, product_ref, tile_sems = refs if fetch == "keep" else refs[:-4] + refs[-1:] + refs[-4:-1]
+    if known:
+        *refs, picked_ref, product_ref = refs
+    else:
+        *refs, near_ref, picked_ref, product_ref, tile_sems = refs
         copies = started(tiles_ref, near_ref, tile_sems)
         tiles_ref = near_ref
-    else:
-        *refs, picked_ref, product_ref = refs
     *inputs, new_ref, own_out_ref, gram_ref, scale_ref, message_ref = refs
     parts, count, width = wide_ref.shape
     if known:
@@ -318,11 +331,8 @@
     new = new * inverse
     new_ref[...] = new
     own_out_ref[...] = new_ref[pl.ds(pl.multiple_of(own_ref[0] * across, across), across)]
-    sums = multiplied(forward, True, new, tiles_ref, copies, pick_ref, put_ref, picked_ref, product_ref)
-    if message_ref.shape[1] == sums.shape[0]:
-        message_ref[...] = jnp.broadcast_to(sums.astype(message_ref.dtype)[None], message_ref.shape)
-    else:
-        message_ref[...] = sums.reshape(message_ref.shape)
+    sums = multiplied(False, True, new, tiles_ref, copies, pick_ref, put_ref, picked_ref, product_ref)
+    message_ref[...] = sums.reshape(message_ref.shape)
 
 
 def right_dots_kernel(length, got_ref, basis_ref, *refs):
@@ -352,6 +362,16 @@
     return new * inverse, scale, grown
 
 
+def right_kernel(m, got_ref, image_ref, basis_ref, gram_in_ref, *refs):
+    refs = list(refs)
+    vector_ref, gram_ref, scale_ref, message_ref = refs[-4:]
+    new, scale, grown = new_right(m, got_ref, image_ref, basis_ref, gram_in_ref, refs[:-4])
+    vector_ref[...] = new
+    gram_ref[...] = grown
+    scale_ref[...] = jnp.broadcast_to(scale, scale_ref.shape)
+    message_ref[...] = jnp.broadcast_to(new[None], message_ref.shape)
+
+
 def put_rows(out_ref, row, vector):
     for j in range(vector.shape[0]):
         out_ref[row : row + 1, j * LANES : (j + 1) * LANES] = vector[j : j + 1]
@@ -382,7 +402,12 @@
 
 WHOLE = pl.BlockSpec(memory_space=pltpu.VMEM)
 SCALAR = pl.BlockSpec(memory_space=pltpu.SMEM)
+ANYWHERE = pl.BlockSpec(memory_space=pl.ANY)
 FAR = pl.BlockSpec(memory_space=pltpu.HBM)
+
+
+def turned(x, axis, count, k):
+    return lax.ppermute(x, axis, [(i, i ^ k) for i in range(count)])
 
 
 def in_hbm(x):
@@ -393,9 +418,12 @@
     return pltpu.with_memory_space_constraint(x, pltpu.VMEM)
 
 
-def call(kernel, name, outs, args, scalars=(), scratch=(), far=(), near=()):
+def call(kernel, name, outs, args, scalars=(), scratch=(), far=(), near=(), any_place=()):
     shapes = tuple(jax.ShapeDtypeStruct(s, F32) if isinstance(s, tuple) else s for s in outs)
-    specs = [SCALAR if i in scalars else FAR if i in far else WHOLE for i in range(len(args))]
+    specs = [
+        SCALAR if i in scalars else FAR if i in far else ANYWHERE if i in any_place else WHOLE
+        for i in range(len(args))
+    ]
     return pl.pallas_call(
         kernel,
         name=name,
@@ -428,7 +456,7 @@
     sems = [pltpu.SemaphoreType.DMA((CHUNKS,))]
     narrow = functools.partial(jax.ShapeDtypeStruct, dtype=BF16)
 
-    own_u, own_v = lax.axis_index(COL).reshape(1), lax.axis_index(ROW).reshape(1)
+    own_u = lax.axis_index(COL).reshape(1)
     u_blocks, keep_u, keep_v, next_rows, row_lane, col_lane, row_sub, col_sub = call(
         prepare_kernel,
         "prepare",
@@ -445,7 +473,6 @@
         [
             tile_count,
             own_u,
-            own_v,
             u_start,
             tile_rows.reshape(1, slots),
             tile_cols.reshape(1, slots),
@@ -453,24 +480,26 @@
             keep_v.T,
             v_next.reshape(v_rows, LANES),
         ],
-        scalars=(0, 1, 2),
+        scalars=(0, 1),
         scratch=[pltpu.VMEM((2, 1, slots), jnp.int32), pltpu.SemaphoreType.DMA((cols_n + 5,))],
-        far=range(3, 9),
+        far=range(2, 8),
     )
     u_got = swapped(u_blocks, COL).reshape(-1, u_own)
     u_kept, u_gram = call(kept_kernel, "left_kept", [(keep, u_own), (8, LANES)], [u_got, keep_u])
-    u_wide = lax.all_gather(u_kept, COL, axis=0)
+    u_sent = u_kept.astype(jnp.float16)
+    u_came = turned(u_sent, COL[0], 2, 1)
 
     v_blocks = after(jnp.moveaxis(v_start.reshape(v_here, rows_n, v_own), 1, 0), u_kept)
-    v_got = swapped(v_blocks, ROW).reshape(-1, v_own)
+    v_got, u_came = lax.optimization_barrier((swapped(v_blocks, ROW).reshape(-1, v_own), u_came))
+    u_pair = jnp.stack([u_sent, u_came])
+    u_pairs = [u_pair] + [turned(u_pair, COL[1], PLACES, k) for k in range(1, PLACES)]
     v_kept, message = call(
         kept_with_kernel,
         "right_kept",
         [(keep, v_own), (devices, 8, LANES)],
-        [v_got, keep_v, next_rows],
+        [after(v_got, u_pair), keep_v, next_rows],
         scratch=[pltpu.VMEM((LANES, v_own), F32)],
     )
-    v_wide = lax.all_gather(v_kept, ROW, axis=0)
     got = swapped(message, ROW_COL)
     v_0, gram_v, message = call(
         functools.partial(first_kernel, v_length),
@@ -478,69 +507,70 @@
         [(v_rows, LANES), (PAD, LANES), (rows_n, v_rows, LANES)],
         [got, v_kept, next_rows],
     )
-    v_0_wide = swapped(message, ROW)
     tile_room = [pltpu.VMEM(tile_blocks.shape, BF16)]
     (message,) = call(
         first_forward_kernel,
         "forward",
         [narrow((cols_n, u_full + 32, LANES))],
-        [v_0_wide, tile_blocks, col_sub, row_lane, u_gram],
+        [swapped(message, ROW), tile_blocks, col_sub, row_lane, u_gram],
         scratch=products + sems + tile_room,
         far=(1,),
     )
     got = swapped(message, COL)
-
-    def wide_dots(got, wide, others, length, name, image, dots):
+    image, dots, u_near = call(
+        functools.partial(dots_kernel, u_length, True),
+        "left_dots",
+        [(u_full, LANES), (rows_n, 16, LANES), pltpu.VMEM((cols_n, keep, u_own), F32)],
+        [own_u, got, *(pair.astype(F32) for pair in u_pairs)],
+        scalars=(0,),
+        scratch=sems,
+        any_place=range(2, 2 + PLACES),
+    )
+
+    def left(dots, image, tiles, m, gram, others):
+        known = [] if gram is None else [gram]
+        keep_tiles = [] if known else tile_room
         return call(
-            functools.partial(dots_kernel, length, True),
-            name,
-            [image, dots, pltpu.VMEM(wide.shape, F32)],
-            [got, wide, *others],
-            scratch=sems,
-            far=(1,),
-        )
-
-    def left(dots, image, wide, tiles, m, gram, others, message):
-        known = [] if gram is None else [gram]
-        return call(
-            functools.partial(vector_kernel, m, False, bool(known), None if known else "once"),
+            functools.partial(vector_kernel, m, bool(known)),
             "left",
-            [(u_full, LANES), (u_rows, LANES), (PAD, LANES), (1, LANES), message],
-            [own_u, swapped(dots, ROW), image, wide, tiles, row_sub, col_lane, *known, *others],
+            [(u_full, LANES), (u_rows, LANES), (PAD, LANES), (1, LANES), (rows_n, v_rows, LANES), *keep_tiles],
+            [own_u, swapped(dots, ROW), image, u_near, tiles, row_sub, col_lane, *known, *others],
             scalars=(0,),
-            scratch=products if known else products + sems + tile_room,
+            scratch=products if known else products + sems,
             near=(3, 4) if known else (3,),
             far=() if known else (4,),
         )
 
-    image, dots, u_near = wide_dots(got, u_wide, [], u_length, "left_dots", (u_full, LANES), (rows_n, 16, LANES))
-    u_0_wide, u_0, gram_u, alpha_0, message = left(
-        dots, image, u_near, tile_blocks, keep, None, [], narrow((rows_n, v_full, LANES))
-    )
-    image, dots, v_near = wide_dots(
-        swapped(message, ROW), v_wide, [v_0_wide], v_length, "right_dots", (v_full, LANES), (cols_n, LANES)
-    )
-    _, v_1, gram_v, beta_0, message, tiles = call(
-        functools.partial(vector_kernel, keep + 1, True, True, "keep"),
+    u_0_wide, u_0, gram_u, alpha_0, message, tiles = left(dots, image, tile_blocks, keep, None, [])
+    image, dots = call(
+        functools.partial(right_dots_kernel, v_length),
+        "right_dots",
+        [(v_rows, LANES), (devices, LANES)],
+        [swapped(message, ROW), v_kept, v_0],
+    )
+    v_1, gram_v, beta_0, message = call(
+        functools.partial(right_kernel, keep + 1),
         "right",
-        [(v_full, LANES), (v_rows, LANES), (PAD, LANES), (1, LANES), narrow((cols_n, u_full, LANES)), *tile_room],
-        [own_v, swapped(dots, COL), image, v_near, tile_blocks, col_sub, row_lane, gram_v, v_0_wide],
-        scalars=(0,),
-        scratch=products + sems,
-        near=(3,),
-        far=(4,),
-    )
-    got = swapped(message, COL)
+        [(v_rows, LANES), (PAD, LANES), (1, LANES), (rows_n, v_rows, LANES)],
+        [swapped(dots, ROW_COL), image, v_kept, gram_v, v_0],
+    )
+    (message,) = call(
+        forward_kernel,
+        "forward",
+        [narrow((cols_n, u_full, LANES))],
+        [swapped(message, ROW), tiles, col_sub, row_lane],
+        scratch=products,
+        near=(1,),
+    )
     image, dots = call(
         functools.partial(dots_kernel, u_length, False),
         "left_dots",
         [(u_full, LANES), (rows_n, LANES)],
-        [got, u_near, u_0_wide],
-        near=(1,),
-    )
-    _, u_1, _, alpha_1, message = left(
-        dots, image, u_near, tiles, keep + 1, gram_u, [u_0_wide], (rows_n, v_rows, LANES)
-    )
+        [own_u, swapped(message, COL), u_near, u_0_wide],
+        scalars=(0,),
+        near=(2,),
+    )
+    _, u_1, _, alpha_1, message = left(dots, image, tiles, keep + 1, gram_u, [u_0_wide])
     got = swapped(message, ROW)
     (u_basis,) = call(left_out_kernel, "left_out", [(keep + 2, u_own)], [u_kept, u_0, u_1])
     image, dots = call(

time: 212 us -> 198 us (0.934)
  blocking collectives: 152 us -> 115 us
  waiting for transfers between devices: 7.68 us -> 28.3 us
  starting transfers between devices: 3.9 us -> 24.5 us
  between operations: 14.8 us -> 1.43 us
  Pallas kernels: 33.1 us -> 26 us
    all_to_all x11 -> x9, blocking collectives: 152 us -> 115 us  [swapped(): return lax.all_to_all(blocks, axis, 0, 0, tiled=True)]
    all_to_all x1 -> x4, starting transfers between devices: 3.82 us -> 20.3 us  [swapped(): return lax.all_to_all(blocks, axis, 0, 0, tiled=True)]
    ppermute x0 -> x4, waiting for transfers between devices: none -> 13.4 us  [turned(): return lax.ppermute(x, axis, [(i, i ^ k) for i in range(count)])]
    all_to_all x1 -> x4, waiting for transfers between devices: 7.64 us -> 14.9 us  [swapped(): return lax.all_to_all(blocks, axis, 0, 0, tiled=True)]
    pallas_call x14 -> x15, Pallas kernels: 33.1 us -> 26 us  [call(): pl.pallas_call(kernel, name=name, out_shape=shapes, in_specs=specs, out_s...]
    ppermute x0 -> x4, starting transfers between devices: none -> 4.22 us  [turned(): return lax.ppermute(x, axis, [(i, i ^ k) for i in range(count)])]
  transfers between devices with their start and end apart: 3 -> 8, of which waited for: 1 -> 6; matrix products, arithmetic and copies ran while one was open for 0% -> 1% of each run, Pallas kernels for 8% -> 3%
where the time goes in v4:
time: 198 us; the launch traced here: 197 us
  blocking collectives  115 us (58%)
  waiting for transfers between devices  28.3 us (14%)
  Pallas kernels  26 us (13%)
  starting transfers between devices  24.5 us (12%)
    all_to_all x9, blocking collectives, swapped(): return lax.all_to_all(blocks, axis, 0, 0, tiled=True)  115 us
    pallas_call x15, Pallas kernels, call(): pl.pallas_call(kernel, name=name, out_shape=shapes, in_specs=specs, out_s...  26 us
    all_to_all x4, starting transfers between devices, swapped(): return lax.all_to_all(blocks, axis, 0, 0, tiled=True)  20.3 us
    all_to_all x4, waiting for transfers between devices, swapped(): return lax.all_to_all(blocks, axis, 0, 0, tiled=True)  14.9 us
    ppermute x4, waiting for transfers between devices, turned(): return lax.ppermute(x, axis, [(i, i ^ k) for i in range(count)])  13.4 us
    ppermute x4, starting transfers between devices, turned(): return lax.ppermute(x, axis, [(i, i ^ k) for i in range(count)])  4.22 us
  transfers between devices with their start and end apart: 8, of which 6 were waited for; matrix products, arithmetic and copies ran while one was open for 1% of the time, Pallas kernels for 3%

profile of v4, /device:TPU:1, one launch (start us, length us, event | category | flops | bytes accessed | tf_op | source)
XLA Modules:
  0.0 196.9 jit_solution(1294649712049914540)
XLA Ops:
  1.3 1.5 prepare.1
  2.8 0.0 copy-start
  2.8 22.9 %all_to_all.83 = f32[8,16,2048]{2,1,0:T(8,128)S(1)} all-to-all(f32[8,16,2048]{2,1,0:T(8,128)S(1)} %get-tuple-element.46), channel_id=1, replica_groups=mesh['row_0'=2,'row_1'=4,'row_2'=2,'col_0'=2,'col_1'=4] {'col_0','col_1'}, dimensions={0} | all-to-all | bytes 2097152 | tf_op jit(solution)/shard_map/all_to_all | solution.py:28
  25.7 1.6 left_kept.1
  27.3 8.0 %all-to-all-start.1 = ((f32[16,8,1024]{2,1,0:T(8,128)}), f32[16,8,1024]{2,1,0:T(8,128)S(1)}, u32[]{:S(2)}, u32[]{:S(2)}) async-start(f32[16,8,1024]{2,1,0:T(8,128)} %bitcast.33), calls=%async_computation.1 | async-start | bytes 1048576 | tf_op jit(solution)/shard_map/all_to_all | solution.py:28
  35.2 1.0 collective-permute-start
  36.2 10.3 %collective-permute-done = f16[40,2048]{1,0:T(8,128)(2,1)S(1)} collective-permute-done((f16[40,2048]{1,0:T(8,128)(2,1)S(1)}, f16[40,2048]{1,0:T(8,128)(2,1)S(1)}, u32[]{:S(2)}, u32[]{:S(2)}) %collective-permute-start) | collective-permute-done | bytes 163872 | tf_op jit(solution)/shard_map/ppermute | solution.py:410
  46.5 0.0 all-to-all-done.1
  46.6 0.1 fusion
  46.6 1.5 right_kept.1
  48.1 19.6 %all_to_all.84.got_ref = f32[128,8,128]{2,1,0:T(8,128)S(1)} all-to-all(f32[128,8,128]{2,1,0:T(8,128)S(1)} %get-tuple-element.55), channel_id=1, replica_groups=mesh['row_0'=2,'row_1'=4,'row_2'=2,'col_0'=2,'col_1'=4] {'row_0','row_1'..., dimensions={0} | all-to-all | bytes 1048576 | tf_op jit(solution)/shard_map/all_to_all | solution.py:28
  67.7 1.3 first_right.1
  69.1 4.9 %all-to-all-start.3 = ((f32[16,8,128]{2,1,0:T(8,128)}), f32[16,8,128]{2,1,0:T(8,128)S(1)}, u32[]{:S(2)}, u32[]{:S(2)}) async-start(f32[16,8,128]{2,1,0:T(8,128)} %get-tuple-element.57), calls=%async_computation.3 | async-start | bytes 131072 | tf_op jit(solution)/shard_map/all_to_all | solution.py:28
  74.0 1.3 collective-permute-start.2
  75.3 0.2 collective-permute-start.1
  75.5 1.7 collective-permute-start.3
  77.2 2.6 %all-to-all-done.3.got_ref = f32[16,8,128]{2,1,0:T(8,128)S(1)} async-done(((f32[16,8,128]{2,1,0:T(8,128)}), f32[16,8,128]{2,1,0:T(8,128)S(1)}, u32[]{:S(2)}, u32[]{:S(2)}) %all-to-all-start.3) | async-done | bytes 65568 | tf_op jit(solution)/shard_map/all_to_all | solution.py:28
  79.9 5.5 %forward.2 = bf16[8,160,128]{2,1,0:T(8,128)(2,1)} custom-call(f32[16,8,128]{2,1,0:T(8,128)S(1)} %all-to-all-done.3.got_ref, bf16[64,256,256]{2,1,0:T(8,128)(2,1)} %tiles_ref.1, f32[128,1]{1,0:T(8,128)S(1)} %get-tuple-element.58.pick_ref, f32[1,128]{1,0:T(1,128)S(1)} %get-tuple-element.59.put_ref, f32[8,128]{1,0:T(8,128)S(1)} %get-tuple-element.60.gram_ref), custom_call_target="tpu_custom_call" | custom-call | tf_op jit(solution)/shard_map/forward/pallas_call | solution.py:427
  85.4 0.0 copy-done
  85.4 3.6 %all-to-all-start.4 = ((bf16[8,160,128]{2,1,0:T(8,128)(2,1)}), bf16[8,160,128]{2,1,0:T(8,128)(2,1)S(1)}, u32[]{:S(2)}, u32[]{:S(2)}) async-start(bf16[8,160,128]{2,1,0:T(8,128)(2,1)} %forward.2), calls=%async_computation.4 | async-start | bytes 655360 | tf_op jit(solution)/shard_map/all_to_all | solution.py:28
  89.0 0.0 collective-permute-done.2
  89.1 1.1 collective-permute-done.1
  90.3 2.0 collective-permute-done.3
  92.2 1.0 convert_element_type.19.refs_3_
  93.3 3.6 %all-to-all-done.4.got_ref = bf16[8,160,128]{2,1,0:T(8,128)(2,1)S(1)} async-done(((bf16[8,160,128]{2,1,0:T(8,128)(2,1)}), bf16[8,160,128]{2,1,0:T(8,128)(2,1)S(1)}, u32[]{:S(2)}, u32[]{:S(2)}) %all-to-all-start.4) | async-done | bytes 327712 | tf_op jit(solution)/shard_map/all_to_all | solution.py:28
  96.9 0.0 copy-start.1
  96.9 1.3 left_dots.2
  98.2 11.1 %all_to_all.85.got_ref = f32[16,16,128]{2,1,0:T(8,128)S(1)} all-to-all(f32[16,16,128]{2,1,0:T(8,128)S(1)} %get-tuple-element.61), channel_id=1, replica_groups=mesh['row_0'=2,'row_1'=4,'row_2'=2,'col_0'=2,'col_1'=4] {'row_0','row_1'..., dimensions={0} | all-to-all | bytes 262144 | tf_op jit(solution)/shard_map/all_to_all | solution.py:28
  109.3 4.4 %left.2 = (f32[128,128]{1,0:T(8,128)S(1)}, f32[16,128]{1,0:T(8,128)S(1)}, f32[48,128]{1,0:T(8,128)S(1)}, f32[1,128]{1,0:T(1,128)S(1)}, f32[16,8,128]{2,1,0:T(8,128)S(1)}, /*index=5*/bf16[64,256,256]{2,1,0:T(8,128)(2,1)S(1)}) custom-call(s32[1]{0:T(128)} %bitcast.own_ref, f32[16,16,128]{2,1,0:T(8,128)S(1)} %all_to_all.85.got_ref, ...), custom_call_target="tpu_custom_call" | custom-call | tf_op jit(solution)/shard_map/left/pallas_call | solution.py:427
  113.7 9.0 %all_to_all.86.got_ref = f32[16,8,128]{2,1,0:T(8,128)S(1)} all-to-all(f32[16,8,128]{2,1,0:T(8,128)S(1)} %get-tuple-element.67), channel_id=1, replica_groups=mesh['row_0'=2,'row_1'=4,'row_2'=2,'col_0'=2,'col_1'=4] {'row_0','row_1'..., dimensions={0} | all-to-all | bytes 131072 | tf_op jit(solution)/shard_map/all_to_all | solution.py:28
  122.7 0.2 right_dots.1
  122.9 13.3 %all_to_all.87 = f32[128,1,128]{2,1,0:T(1,128)S(1)} all-to-all(f32[128,1,128]{2,1,0:T(1,128)S(1)} %bitcast.30), channel_id=1, replica_groups=mesh['row_0'=2,'row_1'=4,'row_2'=2,'col_0'=2,'col_1'=4] {'row_0','row_1'..., dimensions={0} | all-to-all | bytes 131072 | tf_op jit(solution)/shard_map/all_to_all | solution.py:28
  136.2 0.3 right.1
  136.5 9.4 %all_to_all.88.got_ref = f32[16,8,128]{2,1,0:T(8,128)S(1)} all-to-all(f32[16,8,128]{2,1,0:T(8,128)S(1)} %get-tuple-element.72), channel_id=1, replica_groups=mesh['row_0'=2,'row_1'=4,'row_2'=2,'col_0'=2,'col_1'=4] {'row_0','row_1'..., dimensions={0} | all-to-all | bytes 131072 | tf_op jit(solution)/shard_map/all_to_all | solution.py:28
  145.9 0.0 copy-done.1
  145.9 2.9 %forward.3 = bf16[8,128,128]{2,1,0:T(8,128)(2,1)S(1)} custom-call(f32[16,8,128]{2,1,0:T(8,128)S(1)} %all_to_all.88.got_ref, bf16[64,256,256]{2,1,0:T(8,128)(2,1)S(1)} %get-tuple-element.73.tiles_ref, f32[128,1]{1,0:T(8,128)S(1)} %copy-done.1, f32[1,128]{1,0:T(1,128)S(1)} %get-tuple-element.59.put_ref), custom_call_target="tpu_custom_call" | custom-call | tf_op jit(solution)/shard_map/forward/pallas_call | solution.py:427
  148.8 11.2 %all_to_all.89.got_ref = bf16[8,128,128]{2,1,0:T(8,128)(2,1)S(1)} all-to-all(bf16[8,128,128]{2,1,0:T(8,128)(2,1)S(1)} %forward.3), channel_id=1, replica_groups=mesh['row_0'=2,'row_1'=4,'row_2'=2,'col_0'=2,'col_1'=4] {'col_0','col_1'}, dimensions={0} | all-to-all | bytes 524288 | tf_op jit(solution)/shard_map/all_to_all | solution.py:28
  160.0 0.4 left_dots.3
  160.4 10.0 %all_to_all.90 = f32[16,1,128]{2,1,0:T(1,128)S(1)} all-to-all(f32[16,1,128]{2,1,0:T(1,128)S(1)} %bitcast.32), channel_id=1, replica_groups=mesh['row_0'=2,'row_1'=4,'row_2'=2,'col_0'=2,'col_1'=4] {'row_0','row_1'..., dimensions={0} | all-to-all | bytes 16384 | tf_op jit(solution)/shard_map/all_to_all | solution.py:28
  170.4 2.4 %left.3 = (f32[128,128]{1,0:T(8,128)}, f32[16,128]{1,0:T(8,128)S(1)}, f32[48,128]{1,0:T(8,128)}, f32[1,128]{1,0:T(1,128)S(1)}, f32[16,8,128]{2,1,0:T(8,128)S(1)}) custom-call(s32[1]{0:T(128)} %bitcast.own_ref, f32[16,128]{1,0:T(8,128)S(1)} %bitcast.31, f32[128,128]{1,0:T(8,128)S(1)} %get-tuple-element.76.image_ref, ...), custom_call_target="tpu_custom_call" | custom-call | tf_op jit(solution)/shard_map/left/pallas_call | solution.py:427
  172.9 8.9 %all_to_all.91.got_ref = f32[16,8,128]{2,1,0:T(8,128)S(1)} all-to-all(f32[16,8,128]{2,1,0:T(8,128)S(1)} %get-tuple-element.79), channel_id=1, replica_groups=mesh['row_0'=2,'row_1'=4,'row_2'=2,'col_0'=2,'col_1'=4] {'row_0','row_1'..., dimensions={0} | all-to-all | bytes 131072 | tf_op jit(solution)/shard_map/all_to_all | solution.py:28
  181.8 0.9 last_dots.1
  182.7 3.8 %all-to-all-start.12 = ((f32[128,1,128]{2,1,0:T(1,128)}), f32[128,1,128]{2,1,0:T(1,128)S(1)}, u32[]{:S(2)}, u32[]{:S(2)}) async-start(f32[128,1,128]{2,1,0:T(1,128)} %bitcast.19), calls=%async_computation.12 | async-start | bytes 131072 | tf_op jit(solution)/shard_map/all_to_all | solution.py:28
  186.5 0.8 left_out.1
  187.3 8.6 %all-to-all-done.12 = f32[128,1,128]{2,1,0:T(1,128)S(1)} async-done(((f32[128,1,128]{2,1,0:T(1,128)}), f32[128,1,128]{2,1,0:T(1,128)S(1)}, u32[]{:S(2)}, u32[]{:S(2)}) %all-to-all-start.12) | async-done | bytes 65568 | tf_op jit(solution)/shard_map/all_to_all | solution.py:28
  195.9 1.0 last_right.1
  (4 shorter events, 0.1 us)
Async XLA Ops:
  2.8 82.6 %copy-start = (f32[128,1]{1,0:T(8,128)}, f32[128,1]{1,0:T(8,128)S(1)}, u32[]{:S(2)}) copy-start(f32[128,1]{1,0:T(8,128)S(1)} %get-tuple-element.58.pick_ref) | copy-start | bytes 1540
  27.3 19.3 %all-to-all-start.1 = ((f32[16,8,1024]{2,1,0:T(8,128)}), f32[16,8,1024]{2,1,0:T(8,128)S(1)}, u32[]{:S(2)}, u32[]{:S(2)}) async-start(f32[16,8,1024]{2,1,0:T(8,128)} %bitcast.33), calls=%async_computation.1 | async-start | bytes 1048576 | tf_op jit(solution)/shard_map/all_to_all | solution.py:28
  35.2 11.3 %collective-permute-start = (f16[40,2048]{1,0:T(8,128)(2,1)S(1)}, f16[40,2048]{1,0:T(8,128)(2,1)S(1)}, u32[]{:S(2)}, u32[]{:S(2)}) collective-permute-start(f16[40,2048]{1,0:T(8,128)(2,1)S(1)} %convert_element_type.15), channel_id=1, source_target_pairs={{0,4},{4,0},{1,5},{5,1},{2,6},{6,2},{3,7},{7,3},{8,12},{12,8},{9,1... | collective-permute-start | bytes 491528 | tf_op jit(solution)/shard_map/ppermute | solution.py:410
  69.1 10.8 %all-to-all-start.3 = ((f32[16,8,128]{2,1,0:T(8,128)}), f32[16,8,128]{2,1,0:T(8,128)S(1)}, u32[]{:S(2)}, u32[]{:S(2)}) async-start(f32[16,8,128]{2,1,0:T(8,128)} %get-tuple-element.57), calls=%async_computation.3 | async-start | bytes 131072 | tf_op jit(solution)/shard_map/all_to_all | solution.py:28
  74.0 15.1 %collective-permute-start.2 = (f16[2,40,2048]{2,1,0:T(8,128)(2,1)S(1)}, f16[2,40,2048]{2,1,0:T(8,128)(2,1)S(1)}, u32[]{:S(2)}, u32[]{:S(2)}) collective-permute-start(f16[2,40,2048]{2,1,0:T(8,128)(2,1)S(1)} %get-tuple-element.90), channel_id=1, source_target_pairs={{0,2},{1,3},{2,0},{3,1},{4,6},{5,7},{6,4},{7,5},{8,10},{9,11},{10,... | collective-permute-start | bytes 983048 | tf_op jit(solution)/shard_map/ppermute | solution.py:410
  75.3 14.9 %collective-permute-start.1 = (f16[2,40,2048]{2,1,0:T(8,128)(2,1)S(1)}, f16[2,40,2048]{2,1,0:T(8,128)(2,1)S(1)}, u32[]{:S(2)}, u32[]{:S(2)}) collective-permute-start(f16[2,40,2048]{2,1,0:T(8,128)(2,1)S(1)} %get-tuple-element.90), channel_id=1, source_target_pairs={{0,1},{1,0},{2,3},{3,2},{4,5},{5,4},{6,7},{7,6},{8,9},{9,8},{10,11... | collective-permute-start | bytes 983048 | tf_op jit(solution)/shard_map/ppermute | solution.py:410
  75.5 16.7 %collective-permute-start.3 = (f16[2,40,2048]{2,1,0:T(8,128)(2,1)S(1)}, f16[2,40,2048]{2,1,0:T(8,128)(2,1)}, u32[]{:S(2)}, u32[]{:S(2)}) collective-permute-start(f16[2,40,2048]{2,1,0:T(8,128)(2,1)S(1)} %get-tuple-element.90), channel_id=1, source_target_pairs={{0,3},{1,2},{2,1},{3,0},{4,7},{5,6},{6,5},{7,4},{8,11},{9,10},{10,... | collective-permute-start | bytes 983048 | tf_op jit(solution)/shard_map/ppermute | solution.py:410
  85.4 11.5 %all-to-all-start.4 = ((bf16[8,160,128]{2,1,0:T(8,128)(2,1)}), bf16[8,160,128]{2,1,0:T(8,128)(2,1)S(1)}, u32[]{:S(2)}, u32[]{:S(2)}) async-start(bf16[8,160,128]{2,1,0:T(8,128)(2,1)} %forward.2), calls=%async_computation.4 | async-start | bytes 655360 | tf_op jit(solution)/shard_map/all_to_all | solution.py:28
  96.9 49.0 %copy-start.1 = (f32[128,1]{1,0:T(8,128)S(1)}, f32[128,1]{1,0:T(8,128)}, u32[]{:S(2)}) copy-start(f32[128,1]{1,0:T(8,128)} %copy-done) | copy-start | bytes 1540
  182.7 13.2 %all-to-all-start.12 = ((f32[128,1,128]{2,1,0:T(1,128)}), f32[128,1,128]{2,1,0:T(1,128)S(1)}, u32[]{:S(2)}, u32[]{:S(2)}) async-start(f32[128,1,128]{2,1,0:T(1,128)} %bitcast.19), calls=%async_computation.12 | async-start | bytes 131072 | tf_op jit(solution)/shard_map/all_to_all | solution.py:28

commit v5 on v4

--- a/solution.py
+++ b/solution.py
@@ -123,12 +123,15 @@
         lane_ref[...] = jnp.where(used, lane, -1.0)
 
 
-def kept_kernel(start_ref, keep_ref, out_ref, gram_ref):
-    basis = jnp.dot(keep_ref[...], start_ref[...], precision=HIGH, preferred_element_type=F32)
-    out_ref[...] = basis
-    rows = basis.shape[0]
-    wide = jnp.concatenate([basis, jnp.zeros((PAD - rows, basis.shape[1]), F32)], axis=0)
-    full = jnp.concatenate([wide, jnp.zeros((LANES - PAD, basis.shape[1]), F32)], axis=0)
+def kept_kernel(start_ref, keep_ref, out_ref):
+    out_ref[...] = jnp.dot(keep_ref[...], start_ref[...], precision=HIGH, preferred_element_type=F32)
+
+
+def gram_kernel(basis_ref, gram_ref):
+    basis = basis_ref[...]
+    rows, width = basis.shape
+    wide = jnp.concatenate([basis, jnp.zeros((PAD - rows, width), F32)], axis=0)
+    full = jnp.concatenate([wide, jnp.zeros((LANES - PAD, width), F32)], axis=0)
     gram = lax.dot_general(
         wide, full, (((1,), (1,)), ((), ())), precision=HIGH, preferred_element_type=F32
     )
@@ -484,23 +487,25 @@
         scratch=[pltpu.VMEM((2, 1, slots), jnp.int32), pltpu.SemaphoreType.DMA((cols_n + 5,))],
         far=range(2, 8),
     )
-    u_got = swapped(u_blocks, COL).reshape(-1, u_own)
-    u_kept, u_gram = call(kept_kernel, "left_kept", [(keep, u_own), (8, LANES)], [u_got, keep_u])
-    u_sent = u_kept.astype(jnp.float16)
+    v_blocks = jnp.moveaxis(v_start.reshape(v_here, rows_n, v_own), 1, 0)
+    v_got = swapped(v_blocks, ROW).reshape(-1, v_own)
+    u_got = swapped(after(u_blocks, v_got), COL).reshape(-1, u_own)
+    (u_kept,) = call(kept_kernel, "left_kept", [(keep, u_own)], [u_got, keep_u])
+    v_got, u_later = lax.optimization_barrier((v_got, u_kept))
+    u_sent = u_later.astype(jnp.float16)
+    (u_gram,) = call(gram_kernel, "left_gram", [(8, LANES)], [u_later])
     u_came = turned(u_sent, COL[0], 2, 1)
-
-    v_blocks = after(jnp.moveaxis(v_start.reshape(v_here, rows_n, v_own), 1, 0), u_kept)
-    v_got, u_came = lax.optimization_barrier((swapped(v_blocks, ROW).reshape(-1, v_own), u_came))
-    u_pair = jnp.stack([u_sent, u_came])
-    u_pairs = [u_pair] + [turned(u_pair, COL[1], PLACES, k) for k in range(1, PLACES)]
     v_kept, message = call(
         kept_with_kernel,
         "right_kept",
         [(keep, v_own), (devices, 8, LANES)],
-        [after(v_got, u_pair), keep_v, next_rows],
+        [v_got, keep_v, next_rows],
         scratch=[pltpu.VMEM((LANES, v_own), F32)],
     )
-    got = swapped(message, ROW_COL)
+    got, u_came = lax.optimization_barrier((swapped(message, ROW_COL), u_came))
+    u_pair = jnp.stack([u_sent, u_came])
+    u_pairs = [u_pair] + [turned(u_pair, COL[1], PLACES, k) for k in range(1, PLACES)]
+    got = after(got, u_pair)
     v_0, gram_v, message = call(
         functools.partial(first_kernel, v_length),
         "first_right",

time: 198 us -> 194 us (0.980)
  blocking collectives: 115 us -> 94.5 us
  starting transfers between devices: 24.5 us -> 36.1 us
  waiting for transfers between devices: 28.3 us -> 33.6 us
    all_to_all x9 -> x8, blocking collectives: 115 us -> 94.5 us  [swapped(): return lax.all_to_all(blocks, axis, 0, 0, tiled=True)]
    all_to_all x4 -> x5, starting transfers between devices: 20.3 us -> 29.5 us  [swapped(): return lax.all_to_all(blocks, axis, 0, 0, tiled=True)]
    all_to_all x4 -> x5, waiting for transfers between devices: 14.9 us -> 23.3 us  [swapped(): return lax.all_to_all(blocks, axis, 0, 0, tiled=True)]
    ppermute x4, waiting for transfers between devices: 13.4 us -> 10.3 us  [turned(): return lax.ppermute(x, axis, [(i, i ^ k) for i in range(count)])]
    ppermute x4, starting transfers between devices: 4.22 us -> 6.62 us  [turned(): return lax.ppermute(x, axis, [(i, i ^ k) for i in range(count)])]
    pallas_call x15 -> x16, Pallas kernels: 26 us -> 26.8 us  [call(): pl.pallas_call(kernel, name=name, out_shape=shapes, in_specs=specs, out_s...]
  transfers between devices with their start and end apart: 8 -> 9, of which waited for: 6 -> 8; matrix products, arithmetic and copies ran while one was open for 1% -> 1% of each run, Pallas kernels for 3% -> 5%
where the time goes in v5:
time: 194 us
  blocking collectives  94.5 us (49%)
  starting transfers between devices  36.1 us (19%)
  waiting for transfers between devices  33.6 us (17%)
  Pallas kernels  26.8 us (14%)
    all_to_all x8, blocking collectives, swapped(): return lax.all_to_all(blocks, axis, 0, 0, tiled=True)  94.5 us
    all_to_all x5, starting transfers between devices, swapped(): return lax.all_to_all(blocks, axis, 0, 0, tiled=True)  29.5 us
    pallas_call x16, Pallas kernels, call(): pl.pallas_call(kernel, name=name, out_shape=shapes, in_specs=specs, out_s...  26.8 us
    all_to_all x5, waiting for transfers between devices, swapped(): return lax.all_to_all(blocks, axis, 0, 0, tiled=True)  23.3 us
    ppermute x4, waiting for transfers between devices, turned(): return lax.ppermute(x, axis, [(i, i ^ k) for i in range(count)])  10.3 us
    ppermute x4, starting transfers between devices, turned(): return lax.ppermute(x, axis, [(i, i ^ k) for i in range(count)])  6.62 us
  transfers between devices with their start and end apart: 9, of which 8 were waited for; matrix products, arithmetic and copies ran while one was open for 1% of the time, Pallas kernels for 5%

profile of v5, /device:TPU:1, one launch (start us, length us, event | category | flops | bytes accessed | tf_op | source)
XLA Modules:
  0.0 193.6 jit_solution(1406095255093827512)
XLA Ops:
  0.6 7.8 %all-to-all-start = ((f32[16,8,1024]{2,1,0:T(8,128)}), f32[16,8,1024]{2,1,0:T(8,128)S(1)}, u32[]{:S(2)}, u32[]{:S(2)}) async-start(f32[16,8,1024]{2,1,0:T(8,128)} %bitcast.33), calls=%async_computation | async-start | bytes 1048576 | tf_op jit(solution)/shard_map/all_to_all | solution.py:28
  9.1 1.5 prepare.1
  10.6 0.0 copy-start
  10.6 7.6 %all-to-all-done = f32[16,8,1024]{2,1,0:T(8,128)S(1)} async-done(((f32[16,8,1024]{2,1,0:T(8,128)}), f32[16,8,1024]{2,1,0:T(8,128)S(1)}, u32[]{:S(2)}, u32[]{:S(2)}) %all-to-all-start) | async-done | bytes 524320 | tf_op jit(solution)/shard_map/all_to_all | solution.py:28
  18.2 20.9 %all_to_all.83 = f32[8,16,2048]{2,1,0:T(8,128)S(1)} all-to-all(f32[8,16,2048]{2,1,0:T(8,128)S(1)} %get-tuple-element.47), channel_id=1, replica_groups=mesh['row_0'=2,'row_1'=4,'row_2'=2,'col_0'=2,'col_1'=4] {'col_0','col_1'}, dimensions={0} | all-to-all | bytes 2097152 | tf_op jit(solution)/shard_map/all_to_all | solution.py:28
  39.1 0.6 left_kept.1.basis_ref
  39.7 2.3 %right_kept.1 = (f32[40,1024]{1,0:T(8,128)S(1)}, f32[128,8,128]{2,1,0:T(8,128)}) custom-call(f32[128,1024]{1,0:T(8,128)S(1)} %bitcast.27, f32[40,128]{1,0:T(8,128)S(1)} %get-tuple-element.50.keep_ref, f32[8,128]{1,0:T(8,128)S(1)} %get-tuple-element.51.next_ref), custom_call_target="tpu_custom_call" | custom-call | tf_op jit(solution)/shard_map/right_kept/pallas_call | solution.py:430
  42.0 7.1 %all-to-all-start.2 = ((f32[128,8,128]{2,1,0:T(8,128)}), f32[128,8,128]{2,1,0:T(8,128)S(1)}, u32[]{:S(2)}, u32[]{:S(2)}) async-start(f32[128,8,128]{2,1,0:T(8,128)} %get-tuple-element.52), calls=%async_computation.2 | async-start | bytes 1048576 | tf_op jit(solution)/shard_map/all_to_all | solution.py:28
  49.1 3.0 %collective-permute-start = (f16[40,2048]{1,0:T(8,128)(2,1)S(1)}, f16[40,2048]{1,0:T(8,128)(2,1)S(1)}, u32[]{:S(2)}, u32[]{:S(2)}) collective-permute-start(f16[40,2048]{1,0:T(8,128)(2,1)S(1)} %convert_element_type.15), channel_id=1, source_target_pairs={{0,4},{4,0},{1,5},{5,1},{2,6},{6,2},{3,7},{7,3},{8,12},{12,8},{9,1... | collective-permute-start | bytes 491528 | tf_op jit(solution)/shard_map/ppermute | solution.py:413
  52.1 9.1 %collective-permute-done = f16[40,2048]{1,0:T(8,128)(2,1)S(1)} collective-permute-done((f16[40,2048]{1,0:T(8,128)(2,1)S(1)}, f16[40,2048]{1,0:T(8,128)(2,1)S(1)}, u32[]{:S(2)}, u32[]{:S(2)}) %collective-permute-start) | collective-permute-done | bytes 163872 | tf_op jit(solution)/shard_map/ppermute | solution.py:413
  61.2 0.3 all-to-all-done.2.got_ref
  61.5 0.1 fusion
  61.6 1.3 first_right.1
  63.0 5.2 %all-to-all-start.3 = ((f32[16,8,128]{2,1,0:T(8,128)}), f32[16,8,128]{2,1,0:T(8,128)S(1)}, u32[]{:S(2)}, u32[]{:S(2)}) async-start(f32[16,8,128]{2,1,0:T(8,128)} %get-tuple-element.58), calls=%async_computation.3 | async-start | bytes 131072 | tf_op jit(solution)/shard_map/all_to_all | solution.py:28
  68.2 2.8 %collective-permute-start.2 = (f16[2,40,2048]{2,1,0:T(8,128)(2,1)S(1)}, f16[2,40,2048]{2,1,0:T(8,128)(2,1)S(1)}, u32[]{:S(2)}, u32[]{:S(2)}) collective-permute-start(f16[2,40,2048]{2,1,0:T(8,128)(2,1)S(1)} %get-tuple-element.90), channel_id=1, source_target_pairs={{0,2},{1,3},{2,0},{3,1},{4,6},{5,7},{6,4},{7,5},{8,10},{9,11},{10,... | collective-permute-start | bytes 983048 | tf_op jit(solution)/shard_map/ppermute | solution.py:413
  71.0 0.4 collective-permute-start.1
  71.4 0.5 collective-permute-start.3
  71.9 0.9 left_gram.1.gram_ref
  72.8 1.3 all-to-all-done.3.got_ref
  74.0 5.5 %forward.2 = bf16[8,160,128]{2,1,0:T(8,128)(2,1)} custom-call(f32[16,8,128]{2,1,0:T(8,128)S(1)} %all-to-all-done.3.got_ref, bf16[64,256,256]{2,1,0:T(8,128)(2,1)} %tiles_ref.1, f32[128,1]{1,0:T(8,128)S(1)} %get-tuple-element.59.pick_ref, f32[1,128]{1,0:T(1,128)S(1)} %get-tuple-element.60.put_ref, f32[8,128]{1,0:T(8,128)S(1)} %left_gram.1.gram_ref), custom_call_target="tpu_custom_call" | custom-call | tf_op jit(solution)/shard_map/forward/pallas_call | solution.py:430
  79.6 0.0 copy-done
  79.6 5.6 %all-to-all-start.4 = ((bf16[8,160,128]{2,1,0:T(8,128)(2,1)}), bf16[8,160,128]{2,1,0:T(8,128)(2,1)S(1)}, u32[]{:S(2)}, u32[]{:S(2)}) async-start(bf16[8,160,128]{2,1,0:T(8,128)(2,1)} %forward.2), calls=%async_computation.4 | async-start | bytes 655360 | tf_op jit(solution)/shard_map/all_to_all | solution.py:28
  85.2 0.0 collective-permute-done.2
  85.2 1.0 collective-permute-done.1
  86.3 0.2 collective-permute-done.3
  86.5 1.0 convert_element_type.19.refs_3_
  87.5 5.5 %all-to-all-done.4.got_ref = bf16[8,160,128]{2,1,0:T(8,128)(2,1)S(1)} async-done(((bf16[8,160,128]{2,1,0:T(8,128)(2,1)}), bf16[8,160,128]{2,1,0:T(8,128)(2,1)S(1)}, u32[]{:S(2)}, u32[]{:S(2)}) %all-to-all-start.4) | async-done | bytes 327712 | tf_op jit(solution)/shard_map/all_to_all | solution.py:28
  93.0 0.0 copy-start.1
  93.0 1.3 left_dots.2
  94.4 11.7 %all_to_all.84.got_ref = f32[16,16,128]{2,1,0:T(8,128)S(1)} all-to-all(f32[16,16,128]{2,1,0:T(8,128)S(1)} %get-tuple-element.61), channel_id=1, replica_groups=mesh['row_0'=2,'row_1'=4,'row_2'=2,'col_0'=2,'col_1'=4] {'row_0','row_1'..., dimensions={0} | all-to-all | bytes 262144 | tf_op jit(solution)/shard_map/all_to_all | solution.py:28
  106.0 4.4 %left.2 = (f32[128,128]{1,0:T(8,128)S(1)}, f32[16,128]{1,0:T(8,128)S(1)}, f32[48,128]{1,0:T(8,128)S(1)}, f32[1,128]{1,0:T(1,128)S(1)}, f32[16,8,128]{2,1,0:T(8,128)S(1)}, /*index=5*/bf16[64,256,256]{2,1,0:T(8,128)(2,1)S(1)}) custom-call(s32[1]{0:T(128)} %bitcast.own_ref, f32[16,16,128]{2,1,0:T(8,128)S(1)} %all_to_all.84.got_ref, ...), custom_call_target="tpu_custom_call" | custom-call | tf_op jit(solution)/shard_map/left/pallas_call | solution.py:430
  110.4 8.9 %all_to_all.85.got_ref = f32[16,8,128]{2,1,0:T(8,128)S(1)} all-to-all(f32[16,8,128]{2,1,0:T(8,128)S(1)} %get-tuple-element.67), channel_id=1, replica_groups=mesh['row_0'=2,'row_1'=4,'row_2'=2,'col_0'=2,'col_1'=4] {'row_0','row_1'..., dimensions={0} | all-to-all | bytes 131072 | tf_op jit(solution)/shard_map/all_to_all | solution.py:28
  119.4 0.2 right_dots.1
  119.6 13.3 %all_to_all.86 = f32[128,1,128]{2,1,0:T(1,128)S(1)} all-to-all(f32[128,1,128]{2,1,0:T(1,128)S(1)} %bitcast.30), channel_id=1, replica_groups=mesh['row_0'=2,'row_1'=4,'row_2'=2,'col_0'=2,'col_1'=4] {'row_0','row_1'..., dimensions={0} | all-to-all | bytes 131072 | tf_op jit(solution)/shard_map/all_to_all | solution.py:28
  132.9 0.3 right.1
  133.3 9.4 %all_to_all.87.got_ref = f32[16,8,128]{2,1,0:T(8,128)S(1)} all-to-all(f32[16,8,128]{2,1,0:T(8,128)S(1)} %get-tuple-element.72), channel_id=1, replica_groups=mesh['row_0'=2,'row_1'=4,'row_2'=2,'col_0'=2,'col_1'=4] {'row_0','row_1'..., dimensions={0} | all-to-all | bytes 131072 | tf_op jit(solution)/shard_map/all_to_all | solution.py:28
  142.6 0.0 copy-done.1
  142.6 2.9 %forward.3 = bf16[8,128,128]{2,1,0:T(8,128)(2,1)S(1)} custom-call(f32[16,8,128]{2,1,0:T(8,128)S(1)} %all_to_all.87.got_ref, bf16[64,256,256]{2,1,0:T(8,128)(2,1)S(1)} %get-tuple-element.73.tiles_ref, f32[128,1]{1,0:T(8,128)S(1)} %copy-done.1, f32[1,128]{1,0:T(1,128)S(1)} %get-tuple-element.60.put_ref), custom_call_target="tpu_custom_call" | custom-call | tf_op jit(solution)/shard_map/forward/pallas_call | solution.py:430
  145.5 11.2 %all_to_all.88.got_ref = bf16[8,128,128]{2,1,0:T(8,128)(2,1)S(1)} all-to-all(bf16[8,128,128]{2,1,0:T(8,128)(2,1)S(1)} %forward.3), channel_id=1, replica_groups=mesh['row_0'=2,'row_1'=4,'row_2'=2,'col_0'=2,'col_1'=4] {'col_0','col_1'}, dimensions={0} | all-to-all | bytes 524288 | tf_op jit(solution)/shard_map/all_to_all | solution.py:28
  156.7 0.4 left_dots.3
  157.1 10.0 %all_to_all.89 = f32[16,1,128]{2,1,0:T(1,128)S(1)} all-to-all(f32[16,1,128]{2,1,0:T(1,128)S(1)} %bitcast.32), channel_id=1, replica_groups=mesh['row_0'=2,'row_1'=4,'row_2'=2,'col_0'=2,'col_1'=4] {'row_0','row_1'..., dimensions={0} | all-to-all | bytes 16384 | tf_op jit(solution)/shard_map/all_to_all | solution.py:28
  167.2 2.4 %left.3 = (f32[128,128]{1,0:T(8,128)}, f32[16,128]{1,0:T(8,128)S(1)}, f32[48,128]{1,0:T(8,128)}, f32[1,128]{1,0:T(1,128)S(1)}, f32[16,8,128]{2,1,0:T(8,128)S(1)}) custom-call(s32[1]{0:T(128)} %bitcast.own_ref, f32[16,128]{1,0:T(8,128)S(1)} %bitcast.31, f32[128,128]{1,0:T(8,128)S(1)} %get-tuple-element.76.image_ref, ...), custom_call_target="tpu_custom_call" | custom-call | tf_op jit(solution)/shard_map/left/pallas_call | solution.py:430
  169.6 8.9 %all_to_all.90.got_ref = f32[16,8,128]{2,1,0:T(8,128)S(1)} all-to-all(f32[16,8,128]{2,1,0:T(8,128)S(1)} %get-tuple-element.79), channel_id=1, replica_groups=mesh['row_0'=2,'row_1'=4,'row_2'=2,'col_0'=2,'col_1'=4] {'row_0','row_1'..., dimensions={0} | all-to-all | bytes 131072 | tf_op jit(solution)/shard_map/all_to_all | solution.py:28
  178.6 0.9 last_dots.1
  179.4 3.8 %all-to-all-start.12 = ((f32[128,1,128]{2,1,0:T(1,128)}), f32[128,1,128]{2,1,0:T(1,128)S(1)}, u32[]{:S(2)}, u32[]{:S(2)}) async-start(f32[128,1,128]{2,1,0:T(1,128)} %bitcast.19), calls=%async_computation.12 | async-start | bytes 131072 | tf_op jit(solution)/shard_map/all_to_all | solution.py:28
  183.2 0.8 left_out.1
  184.0 8.6 %all-to-all-done.12 = f32[128,1,128]{2,1,0:T(1,128)S(1)} async-done(((f32[128,1,128]{2,1,0:T(1,128)}), f32[128,1,128]{2,1,0:T(1,128)S(1)}, u32[]{:S(2)}, u32[]{:S(2)}) %all-to-all-start.12) | async-done | bytes 65568 | tf_op jit(solution)/shard_map/all_to_all | solution.py:28
  192.6 1.0 last_right.1
  (4 shorter events, 0.1 us)
Async XLA Ops:
  0.6 17.6 %all-to-all-start = ((f32[16,8,1024]{2,1,0:T(8,128)}), f32[16,8,1024]{2,1,0:T(8,128)S(1)}, u32[]{:S(2)}, u32[]{:S(2)}) async-start(f32[16,8,1024]{2,1,0:T(8,128)} %bitcast.33), calls=%async_computation | async-start | bytes 1048576 | tf_op jit(solution)/shard_map/all_to_all | solution.py:28
  10.6 69.0 %copy-start = (f32[128,1]{1,0:T(8,128)}, f32[128,1]{1,0:T(8,128)S(1)}, u32[]{:S(2)}) copy-start(f32[128,1]{1,0:T(8,128)S(1)} %get-tuple-element.59.pick_ref) | copy-start | bytes 1540
  42.0 19.5 %all-to-all-start.2 = ((f32[128,8,128]{2,1,0:T(8,128)}), f32[128,8,128]{2,1,0:T(8,128)S(1)}, u32[]{:S(2)}, u32[]{:S(2)}) async-start(f32[128,8,128]{2,1,0:T(8,128)} %get-tuple-element.52), calls=%async_computation.2 | async-start | bytes 1048576 | tf_op jit(solution)/shard_map/all_to_all | solution.py:28
  49.1 12.1 %collective-permute-start = (f16[40,2048]{1,0:T(8,128)(2,1)S(1)}, f16[40,2048]{1,0:T(8,128)(2,1)S(1)}, u32[]{:S(2)}, u32[]{:S(2)}) collective-permute-start(f16[40,2048]{1,0:T(8,128)(2,1)S(1)} %convert_element_type.15), channel_id=1, source_target_pairs={{0,4},{4,0},{1,5},{5,1},{2,6},{6,2},{3,7},{7,3},{8,12},{12,8},{9,1... | collective-permute-start | bytes 491528 | tf_op jit(solution)/shard_map/ppermute | solution.py:413
  63.0 11.1 %all-to-all-start.3 = ((f32[16,8,128]{2,1,0:T(8,128)}), f32[16,8,128]{2,1,0:T(8,128)S(1)}, u32[]{:S(2)}, u32[]{:S(2)}) async-start(f32[16,8,128]{2,1,0:T(8,128)} %get-tuple-element.58), calls=%async_computation.3 | async-start | bytes 131072 | tf_op jit(solution)/shard_map/all_to_all | solution.py:28
  68.2 16.9 %collective-permute-start.2 = (f16[2,40,2048]{2,1,0:T(8,128)(2,1)S(1)}, f16[2,40,2048]{2,1,0:T(8,128)(2,1)S(1)}, u32[]{:S(2)}, u32[]{:S(2)}) collective-permute-start(f16[2,40,2048]{2,1,0:T(8,128)(2,1)S(1)} %get-tuple-element.90), channel_id=1, source_target_pairs={{0,2},{1,3},{2,0},{3,1},{4,6},{5,7},{6,4},{7,5},{8,10},{9,11},{10,... | collective-permute-start | bytes 983048 | tf_op jit(solution)/shard_map/ppermute | solution.py:413
  71.0 15.2 %collective-permute-start.1 = (f16[2,40,2048]{2,1,0:T(8,128)(2,1)S(1)}, f16[2,40,2048]{2,1,0:T(8,128)(2,1)S(1)}, u32[]{:S(2)}, u32[]{:S(2)}) collective-permute-start(f16[2,40,2048]{2,1,0:T(8,128)(2,1)S(1)} %get-tuple-element.90), channel_id=1, source_target_pairs={{0,1},{1,0},{2,3},{3,2},{4,5},{5,4},{6,7},{7,6},{8,9},{9,8},{10,11... | collective-permute-start | bytes 983048 | tf_op jit(solution)/shard_map/ppermute | solution.py:413
  71.4 15.1 %collective-permute-start.3 = (f16[2,40,2048]{2,1,0:T(8,128)(2,1)S(1)}, f16[2,40,2048]{2,1,0:T(8,128)(2,1)}, u32[]{:S(2)}, u32[]{:S(2)}) collective-permute-start(f16[2,40,2048]{2,1,0:T(8,128)(2,1)S(1)} %get-tuple-element.90), channel_id=1, source_target_pairs={{0,3},{1,2},{2,1},{3,0},{4,7},{5,6},{6,5},{7,4},{8,11},{9,10},{10,... | collective-permute-start | bytes 983048 | tf_op jit(solution)/shard_map/ppermute | solution.py:413
  79.6 13.4 %all-to-all-start.4 = ((bf16[8,160,128]{2,1,0:T(8,128)(2,1)}), bf16[8,160,128]{2,1,0:T(8,128)(2,1)S(1)}, u32[]{:S(2)}, u32[]{:S(2)}) async-start(bf16[8,160,128]{2,1,0:T(8,128)(2,1)} %forward.2), calls=%async_computation.4 | async-start | bytes 655360 | tf_op jit(solution)/shard_map/all_to_all | solution.py:28
  93.0 49.6 %copy-start.1 = (f32[128,1]{1,0:T(8,128)S(1)}, f32[128,1]{1,0:T(8,128)}, u32[]{:S(2)}) copy-start(f32[128,1]{1,0:T(8,128)} %copy-done) | copy-start | bytes 1540
  179.4 13.2 %all-to-all-start.12 = ((f32[128,1,128]{2,1,0:T(1,128)}), f32[128,1,128]{2,1,0:T(1,128)S(1)}, u32[]{:S(2)}, u32[]{:S(2)}) async-start(f32[128,1,128]{2,1,0:T(1,128)} %bitcast.19), calls=%async_computation.12 | async-start | bytes 131072 | tf_op jit(solution)/shard_map/all_to_all | solution.py:28

commit v6 on v5

--- a/solution.py
+++ b/solution.py
@@ -491,10 +491,6 @@
     v_got = swapped(v_blocks, ROW).reshape(-1, v_own)
     u_got = swapped(after(u_blocks, v_got), COL).reshape(-1, u_own)
     (u_kept,) = call(kept_kernel, "left_kept", [(keep, u_own)], [u_got, keep_u])
-    v_got, u_later = lax.optimization_barrier((v_got, u_kept))
-    u_sent = u_later.astype(jnp.float16)
-    (u_gram,) = call(gram_kernel, "left_gram", [(8, LANES)], [u_later])
-    u_came = turned(u_sent, COL[0], 2, 1)
     v_kept, message = call(
         kept_with_kernel,
         "right_kept",
@@ -502,6 +498,10 @@
         [v_got, keep_v, next_rows],
         scratch=[pltpu.VMEM((LANES, v_own), F32)],
     )
+    message, u_later = lax.optimization_barrier((message, u_kept))
+    u_sent = u_later.astype(jnp.float16)
+    (u_gram,) = call(gram_kernel, "left_gram", [(8, LANES)], [u_later])
+    u_came = turned(u_sent, COL[0], 2, 1)
     got, u_came = lax.optimization_barrier((swapped(message, ROW_COL), u_came))
     u_pair = jnp.stack([u_sent, u_came])
     u_pairs = [u_pair] + [turned(u_pair, COL[1], PLACES, k) for k in range(1, PLACES)]

time: 194 us -> 192 us (0.990)
  blocking collectives: 94.5 us -> 73.5 us
  waiting for transfers between devices: 33.6 us -> 43.5 us
  starting transfers between devices: 36.1 us -> 43.6 us
    all_to_all x8 -> x7, blocking collectives: 94.5 us -> 73.5 us  [swapped(): return lax.all_to_all(blocks, axis, 0, 0, tiled=True)]
    all_to_all x5 -> x6, waiting for transfers between devices: 23.3 us -> 33.2 us  [swapped(): return lax.all_to_all(blocks, axis, 0, 0, tiled=True)]
    all_to_all x5 -> x6, starting transfers between devices: 29.5 us -> 36.9 us  [swapped(): return lax.all_to_all(blocks, axis, 0, 0, tiled=True)]
  transfers between devices with their start and end apart: 9 -> 10, of which waited for: 8 -> 9; matrix products, arithmetic and copies ran while one was open for 1% -> 1% of each run, Pallas kernels for 5% -> 6%
where the time goes in v6:
time: 192 us
  blocking collectives  73.5 us (38%)
  starting transfers between devices  43.6 us (23%)
  waiting for transfers between devices  43.5 us (23%)
  Pallas kernels  27.7 us (14%)
    all_to_all x7, blocking collectives, swapped(): return lax.all_to_all(blocks, axis, 0, 0, tiled=True)  73.5 us
    all_to_all x6, starting transfers between devices, swapped(): return lax.all_to_all(blocks, axis, 0, 0, tiled=True)  36.9 us
    all_to_all x6, waiting for transfers between devices, swapped(): return lax.all_to_all(blocks, axis, 0, 0, tiled=True)  33.2 us
    pallas_call x16, Pallas kernels, call(): pl.pallas_call(kernel, name=name, out_shape=shapes, in_specs=specs, out_s...  27.7 us
    ppermute x4, waiting for transfers between devices, turned(): return lax.ppermute(x, axis, [(i, i ^ k) for i in range(count)])  10.3 us
    ppermute x4, starting transfers between devices, turned(): return lax.ppermute(x, axis, [(i, i ^ k) for i in range(count)])  6.62 us
  transfers between devices with their start and end apart: 10, of which 9 were waited for; matrix products, arithmetic and copies ran while one was open for 1% of the time, Pallas kernels for 6%

profile of v6, /device:TPU:1, one launch (start us, length us, event | category | flops | bytes accessed | tf_op | source)
XLA Modules:
  0.0 191.6 jit_solution(3079573584293649104)
XLA Ops:
  0.6 7.8 %all-to-all-start = ((f32[16,8,1024]{2,1,0:T(8,128)}), f32[16,8,1024]{2,1,0:T(8,128)S(1)}, u32[]{:S(2)}, u32[]{:S(2)}) async-start(f32[16,8,1024]{2,1,0:T(8,128)} %bitcast.33), calls=%async_computation | async-start | bytes 1048576 | tf_op jit(solution)/shard_map/all_to_all | solution.py:28
  9.1 2.4 %prepare.1 = (f32[8,16,2048]{2,1,0:T(8,128)}, f32[40,128]{1,0:T(8,128)S(1)}, f32[40,128]{1,0:T(8,128)S(1)}, f32[8,128]{1,0:T(8,128)S(1)}, f32[1,128]{1,0:T(1,128...) custom-call(s32[1]{0:T(128)S(6)} %copy.15.count_ref, s32[1]{0:T(128)} %bitcast.own_ref, ...), custom_call_target="tpu_custom_call" | custom-call | tf_op jit(solution)/shard_map/prepare/pallas_call | solution.py:430
  11.5 0.0 copy-start
  11.5 0.6 copy-done
  12.1 6.1 %all-to-all-done = f32[16,8,1024]{2,1,0:T(8,128)S(1)} async-done(((f32[16,8,1024]{2,1,0:T(8,128)}), f32[16,8,1024]{2,1,0:T(8,128)S(1)}, u32[]{:S(2)}, u32[]{:S(2)}) %all-to-all-start) | async-done | bytes 524320 | tf_op jit(solution)/shard_map/all_to_all | solution.py:28
  18.2 6.4 %all-to-all-start.1 = ((f32[8,16,2048]{2,1,0:T(8,128)}), f32[8,16,2048]{2,1,0:T(8,128)S(1)}, u32[]{:S(2)}, u32[]{:S(2)}) async-start(f32[8,16,2048]{2,1,0:T(8,128)} %get-tuple-element.47), calls=%async_computation.1 | async-start | bytes 2097152 | tf_op jit(solution)/shard_map/all_to_all | solution.py:28
  24.6 2.3 %right_kept.1 = (f32[40,1024]{1,0:T(8,128)S(1)}, f32[128,8,128]{2,1,0:T(8,128)}) custom-call(f32[128,1024]{1,0:T(8,128)S(1)} %bitcast.27, f32[40,128]{1,0:T(8,128)S(1)} %get-tuple-element.49.keep_ref, f32[8,128]{1,0:T(8,128)S(1)} %get-tuple-element.50.next_ref), custom_call_target="tpu_custom_call" | custom-call | tf_op jit(solution)/shard_map/right_kept/pallas_call | solution.py:430
  26.8 11.4 %all-to-all-done.1 = f32[8,16,2048]{2,1,0:T(8,128)S(1)} async-done(((f32[8,16,2048]{2,1,0:T(8,128)}), f32[8,16,2048]{2,1,0:T(8,128)S(1)}, u32[]{:S(2)}, u32[]{:S(2)}) %all-to-all-start.1) | async-done | bytes 1048608 | tf_op jit(solution)/shard_map/all_to_all | solution.py:28
  38.2 0.6 left_kept.1.basis_ref
  38.8 8.2 %all-to-all-start.2 = ((f32[128,8,128]{2,1,0:T(8,128)}), f32[128,8,128]{2,1,0:T(8,128)S(1)}, u32[]{:S(2)}, u32[]{:S(2)}) async-start(f32[128,8,128]{2,1,0:T(8,128)} %get-tuple-element.52), calls=%async_computation.2 | async-start | bytes 1048576 | tf_op jit(solution)/shard_map/all_to_all | solution.py:28
  47.0 3.0 %collective-permute-start = (f16[40,2048]{1,0:T(8,128)(2,1)S(1)}, f16[40,2048]{1,0:T(8,128)(2,1)S(1)}, u32[]{:S(2)}, u32[]{:S(2)}) collective-permute-start(f16[40,2048]{1,0:T(8,128)(2,1)S(1)} %convert_element_type.15), channel_id=1, source_target_pairs={{0,4},{4,0},{1,5},{5,1},{2,6},{6,2},{3,7},{7,3},{8,12},{12,8},{9,1... | collective-permute-start | bytes 491528 | tf_op jit(solution)/shard_map/ppermute | solution.py:413
  50.0 9.1 %collective-permute-done = f16[40,2048]{1,0:T(8,128)(2,1)S(1)} collective-permute-done((f16[40,2048]{1,0:T(8,128)(2,1)S(1)}, f16[40,2048]{1,0:T(8,128)(2,1)S(1)}, u32[]{:S(2)}, u32[]{:S(2)}) %collective-permute-start) | collective-permute-done | bytes 163872 | tf_op jit(solution)/shard_map/ppermute | solution.py:413
  59.1 0.3 all-to-all-done.2.got_ref
  59.5 0.1 fusion
  59.6 1.3 first_right.1
  60.9 5.2 %all-to-all-start.3 = ((f32[16,8,128]{2,1,0:T(8,128)}), f32[16,8,128]{2,1,0:T(8,128)S(1)}, u32[]{:S(2)}, u32[]{:S(2)}) async-start(f32[16,8,128]{2,1,0:T(8,128)} %get-tuple-element.58), calls=%async_computation.3 | async-start | bytes 131072 | tf_op jit(solution)/shard_map/all_to_all | solution.py:28
  66.1 2.8 %collective-permute-start.2 = (f16[2,40,2048]{2,1,0:T(8,128)(2,1)S(1)}, f16[2,40,2048]{2,1,0:T(8,128)(2,1)S(1)}, u32[]{:S(2)}, u32[]{:S(2)}) collective-permute-start(f16[2,40,2048]{2,1,0:T(8,128)(2,1)S(1)} %get-tuple-element.90), channel_id=1, source_target_pairs={{0,2},{1,3},{2,0},{3,1},{4,6},{5,7},{6,4},{7,5},{8,10},{9,11},{10,... | collective-permute-start | bytes 983048 | tf_op jit(solution)/shard_map/ppermute | solution.py:413
  69.0 0.4 collective-permute-start.1
  69.3 0.5 collective-permute-start.3
  69.8 0.9 left_gram.1.gram_ref
  70.7 1.3 all-to-all-done.3.got_ref
  72.0 5.5 %forward.2 = bf16[8,160,128]{2,1,0:T(8,128)(2,1)} custom-call(f32[16,8,128]{2,1,0:T(8,128)S(1)} %all-to-all-done.3.got_ref, bf16[64,256,256]{2,1,0:T(8,128)(2,1)} %tiles_ref.1, f32[128,1]{1,0:T(8,128)S(1)} %get-tuple-element.59.pick_ref, f32[1,128]{1,0:T(1,128)S(1)} %get-tuple-element.60.put_ref, f32[8,128]{1,0:T(8,128)S(1)} %left_gram.1.gram_ref), custom_call_target="tpu_custom_call" | custom-call | tf_op jit(solution)/shard_map/forward/pallas_call | solution.py:430
  77.5 5.6 %all-to-all-start.4 = ((bf16[8,160,128]{2,1,0:T(8,128)(2,1)}), bf16[8,160,128]{2,1,0:T(8,128)(2,1)S(1)}, u32[]{:S(2)}, u32[]{:S(2)}) async-start(bf16[8,160,128]{2,1,0:T(8,128)(2,1)} %forward.2), calls=%async_computation.4 | async-start | bytes 655360 | tf_op jit(solution)/shard_map/all_to_all | solution.py:28
  83.1 0.0 collective-permute-done.2
  83.1 1.0 collective-permute-done.1
  84.2 0.2 collective-permute-done.3
  84.4 1.0 convert_element_type.19.refs_3_
  85.4 5.5 %all-to-all-done.4.got_ref = bf16[8,160,128]{2,1,0:T(8,128)(2,1)S(1)} async-done(((bf16[8,160,128]{2,1,0:T(8,128)(2,1)}), bf16[8,160,128]{2,1,0:T(8,128)(2,1)S(1)}, u32[]{:S(2)}, u32[]{:S(2)}) %all-to-all-start.4) | async-done | bytes 327712 | tf_op jit(solution)/shard_map/all_to_all | solution.py:28
  90.9 1.3 left_dots.2
  92.3 11.7 %all_to_all.83.got_ref = f32[16,16,128]{2,1,0:T(8,128)S(1)} all-to-all(f32[16,16,128]{2,1,0:T(8,128)S(1)} %get-tuple-element.61), channel_id=1, replica_groups=mesh['row_0'=2,'row_1'=4,'row_2'=2,'col_0'=2,'col_1'=4] {'row_0','row_1'..., dimensions={0} | all-to-all | bytes 262144 | tf_op jit(solution)/shard_map/all_to_all | solution.py:28
  104.0 4.4 %left.2 = (f32[128,128]{1,0:T(8,128)S(1)}, f32[16,128]{1,0:T(8,128)S(1)}, f32[48,128]{1,0:T(8,128)S(1)}, f32[1,128]{1,0:T(1,128)S(1)}, f32[16,8,128]{2,1,0:T(8,128)S(1)}, /*index=5*/bf16[64,256,256]{2,1,0:T(8,128)(2,1)S(1)}) custom-call(s32[1]{0:T(128)} %bitcast.own_ref, f32[16,16,128]{2,1,0:T(8,128)S(1)} %all_to_all.83.got_ref, ...), custom_call_target="tpu_custom_call" | custom-call | tf_op jit(solution)/shard_map/left/pallas_call | solution.py:430
  108.4 8.9 %all_to_all.84.got_ref = f32[16,8,128]{2,1,0:T(8,128)S(1)} all-to-all(f32[16,8,128]{2,1,0:T(8,128)S(1)} %get-tuple-element.67), channel_id=1, replica_groups=mesh['row_0'=2,'row_1'=4,'row_2'=2,'col_0'=2,'col_1'=4] {'row_0','row_1'..., dimensions={0} | all-to-all | bytes 131072 | tf_op jit(solution)/shard_map/all_to_all | solution.py:28
  117.3 0.2 right_dots.1
  117.5 13.3 %all_to_all.85 = f32[128,1,128]{2,1,0:T(1,128)S(1)} all-to-all(f32[128,1,128]{2,1,0:T(1,128)S(1)} %bitcast.30), channel_id=1, replica_groups=mesh['row_0'=2,'row_1'=4,'row_2'=2,'col_0'=2,'col_1'=4] {'row_0','row_1'..., dimensions={0} | all-to-all | bytes 131072 | tf_op jit(solution)/shard_map/all_to_all | solution.py:28
  130.9 0.3 right.1
  131.2 9.4 %all_to_all.86.got_ref = f32[16,8,128]{2,1,0:T(8,128)S(1)} all-to-all(f32[16,8,128]{2,1,0:T(8,128)S(1)} %get-tuple-element.72), channel_id=1, replica_groups=mesh['row_0'=2,'row_1'=4,'row_2'=2,'col_0'=2,'col_1'=4] {'row_0','row_1'..., dimensions={0} | all-to-all | bytes 131072 | tf_op jit(solution)/shard_map/all_to_all | solution.py:28
  140.6 0.0 copy-done.3
  140.6 2.9 %forward.3 = bf16[8,128,128]{2,1,0:T(8,128)(2,1)S(1)} custom-call(f32[16,8,128]{2,1,0:T(8,128)S(1)} %all_to_all.86.got_ref, bf16[64,256,256]{2,1,0:T(8,128)(2,1)S(1)} %get-tuple-element.73.tiles_ref, f32[128,1]{1,0:T(8,128)S(1)} %copy-done.3, f32[1,128]{1,0:T(1,128)S(1)} %get-tuple-element.60.put_ref), custom_call_target="tpu_custom_call" | custom-call | tf_op jit(solution)/shard_map/forward/pallas_call | solution.py:430
  143.5 11.2 %all_to_all.87.got_ref = bf16[8,128,128]{2,1,0:T(8,128)(2,1)S(1)} all-to-all(bf16[8,128,128]{2,1,0:T(8,128)(2,1)S(1)} %forward.3), channel_id=1, replica_groups=mesh['row_0'=2,'row_1'=4,'row_2'=2,'col_0'=2,'col_1'=4] {'col_0','col_1'}, dimensions={0} | all-to-all | bytes 524288 | tf_op jit(solution)/shard_map/all_to_all | solution.py:28
  154.6 0.4 left_dots.3
  155.1 10.0 %all_to_all.88 = f32[16,1,128]{2,1,0:T(1,128)S(1)} all-to-all(f32[16,1,128]{2,1,0:T(1,128)S(1)} %bitcast.32), channel_id=1, replica_groups=mesh['row_0'=2,'row_1'=4,'row_2'=2,'col_0'=2,'col_1'=4] {'row_0','row_1'..., dimensions={0} | all-to-all | bytes 16384 | tf_op jit(solution)/shard_map/all_to_all | solution.py:28
  165.1 2.4 %left.3 = (f32[128,128]{1,0:T(8,128)}, f32[16,128]{1,0:T(8,128)S(1)}, f32[48,128]{1,0:T(8,128)}, f32[1,128]{1,0:T(1,128)S(1)}, f32[16,8,128]{2,1,0:T(8,128)S(1)}) custom-call(s32[1]{0:T(128)} %bitcast.own_ref, f32[16,128]{1,0:T(8,128)S(1)} %bitcast.31, f32[128,128]{1,0:T(8,128)S(1)} %get-tuple-element.76.image_ref, ...), custom_call_target="tpu_custom_call" | custom-call | tf_op jit(solution)/shard_map/left/pallas_call | solution.py:430
  167.5 8.9 %all_to_all.89.got_ref = f32[16,8,128]{2,1,0:T(8,128)S(1)} all-to-all(f32[16,8,128]{2,1,0:T(8,128)S(1)} %get-tuple-element.79), channel_id=1, replica_groups=mesh['row_0'=2,'row_1'=4,'row_2'=2,'col_0'=2,'col_1'=4] {'row_0','row_1'..., dimensions={0} | all-to-all | bytes 131072 | tf_op jit(solution)/shard_map/all_to_all | solution.py:28
  176.5 0.9 last_dots.1
  177.3 3.8 %all-to-all-start.12 = ((f32[128,1,128]{2,1,0:T(1,128)}), f32[128,1,128]{2,1,0:T(1,128)S(1)}, u32[]{:S(2)}, u32[]{:S(2)}) async-start(f32[128,1,128]{2,1,0:T(1,128)} %bitcast.19), calls=%async_computation.12 | async-start | bytes 131072 | tf_op jit(solution)/shard_map/all_to_all | solution.py:28
  181.2 0.8 left_out.1
  182.0 8.6 %all-to-all-done.12 = f32[128,1,128]{2,1,0:T(1,128)S(1)} async-done(((f32[128,1,128]{2,1,0:T(1,128)}), f32[128,1,128]{2,1,0:T(1,128)S(1)}, u32[]{:S(2)}, u32[]{:S(2)}) %all-to-all-start.12) | async-done | bytes 65568 | tf_op jit(solution)/shard_map/all_to_all | solution.py:28
  190.6 1.0 last_right.1
  (9 shorter events, 0.1 us)
Async XLA Ops:
  0.6 17.6 %all-to-all-start = ((f32[16,8,1024]{2,1,0:T(8,128)}), f32[16,8,1024]{2,1,0:T(8,128)S(1)}, u32[]{:S(2)}, u32[]{:S(2)}) async-start(f32[16,8,1024]{2,1,0:T(8,128)} %bitcast.33), calls=%async_computation | async-start | bytes 1048576 | tf_op jit(solution)/shard_map/all_to_all | solution.py:28
  11.5 0.6 copy-start
  12.1 65.4 %copy-start.2 = (f32[128,1]{1,0:T(8,128)}, f32[128,1]{1,0:T(8,128)S(1)}, u32[]{:S(2)}) copy-start(f32[128,1]{1,0:T(8,128)S(1)} %get-tuple-element.59.pick_ref) | copy-start | bytes 1540
  18.2 20.0 %all-to-all-start.1 = ((f32[8,16,2048]{2,1,0:T(8,128)}), f32[8,16,2048]{2,1,0:T(8,128)S(1)}, u32[]{:S(2)}, u32[]{:S(2)}) async-start(f32[8,16,2048]{2,1,0:T(8,128)} %get-tuple-element.47), calls=%async_computation.1 | async-start | bytes 2097152 | tf_op jit(solution)/shard_map/all_to_all | solution.py:28
  38.8 20.6 %all-to-all-start.2 = ((f32[128,8,128]{2,1,0:T(8,128)}), f32[128,8,128]{2,1,0:T(8,128)S(1)}, u32[]{:S(2)}, u32[]{:S(2)}) async-start(f32[128,8,128]{2,1,0:T(8,128)} %get-tuple-element.52), calls=%async_computation.2 | async-start | bytes 1048576 | tf_op jit(solution)/shard_map/all_to_all | solution.py:28
  47.0 12.1 %collective-permute-start = (f16[40,2048]{1,0:T(8,128)(2,1)S(1)}, f16[40,2048]{1,0:T(8,128)(2,1)S(1)}, u32[]{:S(2)}, u32[]{:S(2)}) collective-permute-start(f16[40,2048]{1,0:T(8,128)(2,1)S(1)} %convert_element_type.15), channel_id=1, source_target_pairs={{0,4},{4,0},{1,5},{5,1},{2,6},{6,2},{3,7},{7,3},{8,12},{12,8},{9,1... | collective-permute-start | bytes 491528 | tf_op jit(solution)/shard_map/ppermute | solution.py:413
  59.6 44.4 %copy-start.1 = (f32[128,1]{1,0:T(8,128)S(1)}, f32[128,1]{1,0:T(8,128)}, u32[]{:S(2)}) copy-start(f32[128,1]{1,0:T(8,128)} %copy-done) | copy-start | bytes 1540
  60.9 11.1 %all-to-all-start.3 = ((f32[16,8,128]{2,1,0:T(8,128)}), f32[16,8,128]{2,1,0:T(8,128)S(1)}, u32[]{:S(2)}, u32[]{:S(2)}) async-start(f32[16,8,128]{2,1,0:T(8,128)} %get-tuple-element.58), calls=%async_computation.3 | async-start | bytes 131072 | tf_op jit(solution)/shard_map/all_to_all | solution.py:28
  66.1 16.9 %collective-permute-start.2 = (f16[2,40,2048]{2,1,0:T(8,128)(2,1)S(1)}, f16[2,40,2048]{2,1,0:T(8,128)(2,1)S(1)}, u32[]{:S(2)}, u32[]{:S(2)}) collective-permute-start(f16[2,40,2048]{2,1,0:T(8,128)(2,1)S(1)} %get-tuple-element.90), channel_id=1, source_target_pairs={{0,2},{1,3},{2,0},{3,1},{4,6},{5,7},{6,4},{7,5},{8,10},{9,11},{10,... | collective-permute-start | bytes 983048 | tf_op jit(solution)/shard_map/ppermute | solution.py:413
  69.0 15.2 %collective-permute-start.1 = (f16[2,40,2048]{2,1,0:T(8,128)(2,1)S(1)}, f16[2,40,2048]{2,1,0:T(8,128)(2,1)S(1)}, u32[]{:S(2)}, u32[]{:S(2)}) collective-permute-start(f16[2,40,2048]{2,1,0:T(8,128)(2,1)S(1)} %get-tuple-element.90), channel_id=1, source_target_pairs={{0,1},{1,0},{2,3},{3,2},{4,5},{5,4},{6,7},{7,6},{8,9},{9,8},{10,11... | collective-permute-start | bytes 983048 | tf_op jit(solution)/shard_map/ppermute | solution.py:413
  69.3 15.1 %collective-permute-start.3 = (f16[2,40,2048]{2,1,0:T(8,128)(2,1)S(1)}, f16[2,40,2048]{2,1,0:T(8,128)(2,1)}, u32[]{:S(2)}, u32[]{:S(2)}) collective-permute-start(f16[2,40,2048]{2,1,0:T(8,128)(2,1)S(1)} %get-tuple-element.90), channel_id=1, source_target_pairs={{0,3},{1,2},{2,1},{3,0},{4,7},{5,6},{6,5},{7,4},{8,11},{9,10},{10,... | collective-permute-start | bytes 983048 | tf_op jit(solution)/shard_map/ppermute | solution.py:413
  77.5 13.4 %all-to-all-start.4 = ((bf16[8,160,128]{2,1,0:T(8,128)(2,1)}), bf16[8,160,128]{2,1,0:T(8,128)(2,1)S(1)}, u32[]{:S(2)}, u32[]{:S(2)}) async-start(bf16[8,160,128]{2,1,0:T(8,128)(2,1)} %forward.2), calls=%async_computation.4 | async-start | bytes 655360 | tf_op jit(solution)/shard_map/all_to_all | solution.py:28
  90.9 49.6 %copy-start.3 = (f32[128,1]{1,0:T(8,128)S(1)}, f32[128,1]{1,0:T(8,128)}, u32[]{:S(2)}) copy-start(f32[128,1]{1,0:T(8,128)} %copy-done.2) | copy-start | bytes 1540
  177.3 13.2 %all-to-all-start.12 = ((f32[128,1,128]{2,1,0:T(1,128)}), f32[128,1,128]{2,1,0:T(1,128)S(1)}, u32[]{:S(2)}, u32[]{:S(2)}) async-start(f32[128,1,128]{2,1,0:T(1,128)} %bitcast.19), calls=%async_computation.12 | async-start | bytes 131072 | tf_op jit(solution)/shard_map/all_to_all | solution.py:28
